TPU v7x, 32 devices: a whole 2x2x4 slice. The times are simulated.
32 devices in a mesh: dp: 4 (over y, core), fsdp: 8 (over z, x).
Axes of the slice: x: 2, y: 2, z: 4, core: 2. Of those that a mesh axis runs over, the one named last changes fastest.
Arguments:
- rows_in: bfloat16 [96, 320, 1024], P(('dp', 'fsdp')), may hold values from -6 to 6
- slot_row: int32 [192], P(('dp', 'fsdp')), may hold values from 0 to 11, as said below
- live_count: int32 [32], P(('dp', 'fsdp')), may hold values from 1 to 3, as said below
- slot_activation_gradient: bfloat16 [192, 320, 1024], P(('dp', 'fsdp')), may hold values from -6 to 6
- query_weight: bfloat16 [1024, 1024], P(('dp', 'fsdp')), may hold values from -0.1875 to 0.1875
- key_weight: bfloat16 [1024, 1024], P(('dp', 'fsdp')), may hold values from -0.1875 to 0.1875
- value_weight: bfloat16 [1024, 1024], P(('dp', 'fsdp')), may hold values from -0.1875 to 0.1875
- output_weight: bfloat16 [1024, 1024], P(('dp', 'fsdp')), may hold values from -1.5 to 1.5
- query_bias: bfloat16 [1024], P(('dp', 'fsdp')), may hold values from -3 to 3
- value_bias: bfloat16 [1024], P(('dp', 'fsdp')), may hold values from -3 to 3
- output_bias: bfloat16 [1024], P(('dp', 'fsdp')), may hold values from -3 to 3
- attn_gain: bfloat16 [1024], P(('dp', 'fsdp')), may hold values from 0.5 to 1.5
- attn_shift: bfloat16 [1024], P(('dp', 'fsdp')), may hold values from -3 to 3
- expand_weight: bfloat16 [1024, 4096], P(('dp', 'fsdp')), may hold values from -0.1875 to 0.1875
- up_bias: bfloat16 [4096], P(('dp', 'fsdp')), may hold values from -3 to 3
- down_weight: bfloat16 [4096, 1024], P(('dp', 'fsdp')), may hold values from -0.1875 to 0.1875
- down_bias: bfloat16 [1024], P(('dp', 'fsdp')), may hold values from -3 to 3
- ffn_gain: bfloat16 [1024], P(('dp', 'fsdp')), may hold values from 0.5 to 1.5
- ffn_shift: bfloat16 [1024], P(('dp', 'fsdp')), may hold values from -3 to 3
Outputs:
- slot_acts: bfloat16 [192, 320, 1024], P(('dp', 'fsdp'))
- input_grad: float32 [96, 320, 1024], P(('dp', 'fsdp'))
- query_weight_grad: float32 [1024, 1024], P(('dp', 'fsdp'))
- key_weight_grad: float32 [1024, 1024], P(('dp', 'fsdp'))
- value_weight_grad: float32 [1024, 1024], P(('dp', 'fsdp'))
- output_weight_grad: float32 [1024, 1024], P(('dp', 'fsdp'))
- query_bias_grad: float32 [1024], P(('dp', 'fsdp'))
- value_bias_grad: float32 [1024], P(('dp', 'fsdp'))
- output_bias_grad: float32 [1024], P(('dp', 'fsdp'))
- attn_gain_grad: float32 [1024], P(('dp', 'fsdp'))
- attn_shift_grad: float32 [1024], P(('dp', 'fsdp'))
- up_weight_grad: float32 [1024, 4096], P(('dp', 'fsdp'))
- up_bias_grad: float32 [4096], P(('dp', 'fsdp'))
- down_weight_grad: float32 [4096, 1024], P(('dp', 'fsdp'))
- down_bias_grad: float32 [1024], P(('dp', 'fsdp'))
- ffn_gain_grad: float32 [1024], P(('dp', 'fsdp'))
- ffn_shift_grad: float32 [1024], P(('dp', 'fsdp'))
Inputs may be any that keep to these rules, and one draw needn't show every extreme that they name: v = slot_row[s] names row v % 3 of the device with dp index v // 3 and the slot's own fsdp index. Only live rows are named, and every live row is named by at least one slot. Row i of a device is live when i < live_count of that device. In every group of devices that share an fsdp index some device has 3.
All inputs are finite; a program needn't handle non-finite values.
Results may differ from a plain program's by a relative error of at most 0.02.
Values may be sent and summed in bfloat16 or wider, within the bound.
A program may use at most 256 MiB of HBM per device.

v0:
```python
from functools import partial

import jax
import jax.numpy as jnp
from jax import lax
from jax.sharding import PartitionSpec as P

HEADS = 16


EPSILON = 1e-05


def norm_forward(hidden, gain, shift):
    center = hidden - jnp.mean(hidden, axis=-1, keepdims=True)
    inverse = lax.rsqrt(jnp.mean(center * center, axis=-1, keepdims=True) + EPSILON)
    normed = center * inverse
    return (normed * gain + shift, normed, inverse)


def norm_backward(incoming, gain, normed, inverse):
    scaled = incoming * gain
    inner = (
        scaled
        - jnp.mean(scaled, axis=-1, keepdims=True)
        - normed * jnp.mean(scaled * normed, axis=-1, keepdims=True)
    )
    return (
        inner * inverse,
        jnp.sum(incoming * normed, axis=(0, 1)),
        jnp.sum(incoming, axis=(0, 1)),
    )


def apply_weight(acts, weight):
    return jnp.einsum("rsd,de->rse", acts, weight, preferred_element_type=jnp.float32)


def apply_back(grads, weight):
    return jnp.einsum("rse,de->rsd", grads, weight, preferred_element_type=jnp.float32)


def weight_term(acts, grads):
    return jnp.einsum("rsd,rse->de", acts, grads, preferred_element_type=jnp.float32)


def bias_term(grads):
    return jnp.sum(grads, axis=(0, 1), dtype=jnp.float32)


def on_device(
    rows_in,
    slot_row,
    live_count,
    slot_activation_gradient,
    query_weight,
    key_weight,
    value_weight,
    output_weight,
    query_bias,
    value_bias,
    output_bias,
    attn_gain,
    attn_shift,
    expand_weight,
    up_bias,
    down_weight,
    down_bias,
    ffn_gain,
    ffn_shift,
):
    row_count, token_count, feature_count = rows_in.shape
    head_size = feature_count // HEADS
    score_scale = head_size ** (-0.5)
    split_shape = (row_count, token_count, HEADS, head_size)
    wanted = lax.broadcasted_iota(
        jnp.int32, (row_count * lax.axis_size("dp"), slot_row.shape[0]), 0
    )
    one_hot_matrix = (wanted == slot_row[None, :]).astype(jnp.bfloat16)
    upstream = lax.psum_scatter(
        jnp.einsum(
            "az,zfy->afy",
            one_hot_matrix,
            slot_activation_gradient,
            preferred_element_type=jnp.float32,
        ).astype(jnp.bfloat16),
        "dp",
        scatter_dimension=0,
        tiled=True,
    ).astype(jnp.float32)
    (
        query_full,
        key_full,
        value_full,
        output_full,
        qbias_full,
        vbias_full,
        obias_full,
        gain1_full,
        shift1_full,
    ) = (
        lax.all_gather(query_weight, ("dp", "fsdp"), axis=0, tiled=True),
        lax.all_gather(key_weight, ("dp", "fsdp"), axis=0, tiled=True),
        lax.all_gather(value_weight, ("dp", "fsdp"), axis=0, tiled=True),
        lax.all_gather(output_weight, ("dp", "fsdp"), axis=0, tiled=True),
        lax.all_gather(query_bias, ("dp", "fsdp"), axis=0, tiled=True),
        lax.all_gather(value_bias, ("dp", "fsdp"), axis=0, tiled=True),
        lax.all_gather(output_bias, ("dp", "fsdp"), axis=0, tiled=True),
        lax.all_gather(attn_gain, ("dp", "fsdp"), axis=0, tiled=True),
        lax.all_gather(attn_shift, ("dp", "fsdp"), axis=0, tiled=True),
    )
    up_full, upbias_full, down_full, downbias_full, gain2_full, shift2_full = (
        lax.all_gather(expand_weight, ("dp", "fsdp"), axis=0, tiled=True),
        lax.all_gather(up_bias, ("dp", "fsdp"), axis=0, tiled=True),
        lax.all_gather(down_weight, ("dp", "fsdp"), axis=0, tiled=True),
        lax.all_gather(down_bias, ("dp", "fsdp"), axis=0, tiled=True),
        lax.all_gather(ffn_gain, ("dp", "fsdp"), axis=0, tiled=True),
        lax.all_gather(ffn_shift, ("dp", "fsdp"), axis=0, tiled=True),
    )
    inputs = rows_in.astype(jnp.float32)
    query = (apply_weight(rows_in, query_full) + qbias_full.astype(jnp.float32)).astype(
        jnp.bfloat16
    )
    keys = apply_weight(rows_in, key_full).astype(jnp.bfloat16)
    values = (apply_weight(rows_in, value_full) + vbias_full.astype(jnp.float32)).astype(
        jnp.bfloat16
    )
    query_heads = query.reshape(split_shape)
    key_heads = keys.reshape(split_shape)
    value_heads = values.reshape(split_shape)
    scores = (
        jnp.einsum("rqhd,rkhd->rhqk", query_heads, key_heads, preferred_element_type=jnp.float32)
        * score_scale
    )
    row_top = jnp.max(scores, axis=-1, keepdims=True)
    expo = jnp.exp(scores - row_top)
    row_sum = jnp.sum(expo, axis=-1, keepdims=True)
    logsum = row_top + jnp.log(row_sum)
    probs_low = (expo / row_sum).astype(jnp.bfloat16)
    mixed = jnp.einsum(
        "rhqk,rkhd->rqhd", probs_low, value_heads, preferred_element_type=jnp.float32
    )
    mixed = mixed.reshape(row_count, token_count, feature_count).astype(jnp.bfloat16)
    gain1 = gain1_full.astype(jnp.float32)
    resid1 = inputs + apply_weight(mixed, output_full) + obias_full.astype(jnp.float32)
    normed1_out, normed1, inverse1 = norm_forward(resid1, gain1, shift1_full.astype(jnp.float32))
    normed1_low = normed1_out.astype(jnp.bfloat16)
    pre_act = apply_weight(normed1_low, up_full) + upbias_full.astype(jnp.float32)
    act_low = jax.nn.gelu(pre_act, approximate=False).astype(jnp.bfloat16)
    gain2 = gain2_full.astype(jnp.float32)
    resid2 = normed1_out + apply_weight(act_low, down_full) + downbias_full.astype(jnp.float32)
    final, second_normed, inverse2 = norm_forward(resid2, gain2, shift2_full.astype(jnp.float32))
    final_low = final.astype(jnp.bfloat16)
    shard_rows = lax.all_gather(final_low, "dp", axis=0, tiled=True)
    span_rows = shard_rows.shape[0]
    inside = (slot_row >= 0) & (slot_row < span_rows)
    picked = jnp.take(shard_rows, jnp.clip(slot_row, 0, span_rows - 1), axis=0)
    slot_acts = jnp.where(
        inside[:, None, None], picked, jnp.zeros(slot_activation_gradient.shape, jnp.bfloat16)
    )
    (
        query_full,
        key_full,
        value_full,
        output_full,
        qbias_full,
        vbias_full,
        obias_full,
        gain1_full,
        shift1_full,
        up_full,
        upbias_full,
        down_full,
        downbias_full,
        gain2_full,
        shift2_full,
    ) = (
        lax.all_gather(query_weight, ("dp", "fsdp"), axis=0, tiled=True),
        lax.all_gather(key_weight, ("dp", "fsdp"), axis=0, tiled=True),
        lax.all_gather(value_weight, ("dp", "fsdp"), axis=0, tiled=True),
        lax.all_gather(output_weight, ("dp", "fsdp"), axis=0, tiled=True),
        lax.all_gather(query_bias, ("dp", "fsdp"), axis=0, tiled=True),
        lax.all_gather(value_bias, ("dp", "fsdp"), axis=0, tiled=True),
        lax.all_gather(output_bias, ("dp", "fsdp"), axis=0, tiled=True),
        lax.all_gather(attn_gain, ("dp", "fsdp"), axis=0, tiled=True),
        lax.all_gather(attn_shift, ("dp", "fsdp"), axis=0, tiled=True),
        lax.all_gather(expand_weight, ("dp", "fsdp"), axis=0, tiled=True),
        lax.all_gather(up_bias, ("dp", "fsdp"), axis=0, tiled=True),
        lax.all_gather(down_weight, ("dp", "fsdp"), axis=0, tiled=True),
        lax.all_gather(down_bias, ("dp", "fsdp"), axis=0, tiled=True),
        lax.all_gather(ffn_gain, ("dp", "fsdp"), axis=0, tiled=True),
        lax.all_gather(ffn_shift, ("dp", "fsdp"), axis=0, tiled=True),
    )
    gain1 = gain1_full.astype(jnp.float32)
    gain2 = gain2_full.astype(jnp.float32)
    grad2, gain2_grad, shift2_grad = norm_backward(upstream, gain2, second_normed, inverse2)
    ffn_low = grad2.astype(jnp.bfloat16)
    down_grad = weight_term(act_low, ffn_low)
    down_bias_grad = bias_term(ffn_low)
    act_grad = apply_back(ffn_low, down_full)
    gelu_value, gelu_back = jax.vjp(partial(jax.nn.gelu, approximate=False), pre_act)
    pre_grad = gelu_back(act_grad)[0].astype(jnp.bfloat16)
    up_grad = weight_term(normed1_low, pre_grad)
    up_bias_grad = bias_term(pre_grad)
    normed1_grad = grad2 + apply_back(pre_grad, up_full)
    grad1, gain1_grad, shift1_grad = norm_backward(normed1_grad, gain1, normed1, inverse1)
    attn_low = grad1.astype(jnp.bfloat16)
    output_grad = weight_term(mixed, attn_low)
    output_bias_grad = bias_term(attn_low)
    mixed_grad = apply_back(attn_low, output_full).astype(jnp.bfloat16).reshape(split_shape)
    scores_again = (
        jnp.einsum("rqhd,rkhd->rhqk", query_heads, key_heads, preferred_element_type=jnp.float32)
        * score_scale
    )
    probs = jnp.exp(scores_again - logsum)
    probs_again = probs.astype(jnp.bfloat16)
    value_grad = jnp.einsum(
        "rhqk,rqhd->rkhd", probs_again, mixed_grad, preferred_element_type=jnp.float32
    )
    value_grad = value_grad.astype(jnp.bfloat16).reshape(row_count, token_count, feature_count)
    prob_grad = jnp.einsum(
        "rqhd,rkhd->rhqk", mixed_grad, value_heads, preferred_element_type=jnp.float32
    )
    score_grad = (probs * (prob_grad - jnp.sum(probs * prob_grad, axis=-1, keepdims=True))).astype(
        jnp.bfloat16
    )
    query_grad = (
        jnp.einsum("rhqk,rkhd->rqhd", score_grad, key_heads, preferred_element_type=jnp.float32)
        * score_scale
    )
    query_grad = query_grad.astype(jnp.bfloat16).reshape(row_count, token_count, feature_count)
    key_grad = (
        jnp.einsum("rhqk,rqhd->rkhd", score_grad, query_heads, preferred_element_type=jnp.float32)
        * score_scale
    )
    key_grad = key_grad.astype(jnp.bfloat16).reshape(row_count, token_count, feature_count)
    query_wgrad = weight_term(rows_in, query_grad)
    key_wgrad = weight_term(rows_in, key_grad)
    value_wgrad = weight_term(rows_in, value_grad)
    query_bias_grad = bias_term(query_grad)
    value_bias_grad = bias_term(value_grad)
    input_full = (
        grad1
        + apply_back(query_grad, query_full)
        + apply_back(key_grad, key_full)
        + apply_back(value_grad, value_full)
    )
    live_rows = lax.broadcasted_iota(jnp.int32, (row_count,), 0) < live_count[0]
    input_grad = jnp.where(live_rows[:, None, None], input_full, 0.0)
    summed = (
        lax.psum_scatter(query_wgrad, ("dp", "fsdp"), scatter_dimension=0, tiled=True),
        lax.psum_scatter(key_wgrad, ("dp", "fsdp"), scatter_dimension=0, tiled=True),
        lax.psum_scatter(value_wgrad, ("dp", "fsdp"), scatter_dimension=0, tiled=True),
        lax.psum_scatter(output_grad, ("dp", "fsdp"), scatter_dimension=0, tiled=True),
        lax.psum_scatter(query_bias_grad, ("dp", "fsdp"), scatter_dimension=0, tiled=True),
        lax.psum_scatter(value_bias_grad, ("dp", "fsdp"), scatter_dimension=0, tiled=True),
        lax.psum_scatter(output_bias_grad, ("dp", "fsdp"), scatter_dimension=0, tiled=True),
        lax.psum_scatter(gain1_grad, ("dp", "fsdp"), scatter_dimension=0, tiled=True),
        lax.psum_scatter(shift1_grad, ("dp", "fsdp"), scatter_dimension=0, tiled=True),
        lax.psum_scatter(up_grad, ("dp", "fsdp"), scatter_dimension=0, tiled=True),
        lax.psum_scatter(up_bias_grad, ("dp", "fsdp"), scatter_dimension=0, tiled=True),
        lax.psum_scatter(down_grad, ("dp", "fsdp"), scatter_dimension=0, tiled=True),
        lax.psum_scatter(down_bias_grad, ("dp", "fsdp"), scatter_dimension=0, tiled=True),
        lax.psum_scatter(gain2_grad, ("dp", "fsdp"), scatter_dimension=0, tiled=True),
        lax.psum_scatter(shift2_grad, ("dp", "fsdp"), scatter_dimension=0, tiled=True),
    )
    return (
        slot_acts,
        input_grad,
        summed[0],
        summed[1],
        summed[2],
        summed[3],
        summed[4],
        summed[5],
        summed[6],
        summed[7],
        summed[8],
        summed[9],
        summed[10],
        summed[11],
        summed[12],
        summed[13],
        summed[14],
    )


def solution(mesh):
    placed = (
        P(("dp", "fsdp"), None, None),
        P(("dp", "fsdp")),
        P(("dp", "fsdp")),
        P(("dp", "fsdp"), None, None),
        P(("dp", "fsdp"), None),
        P(("dp", "fsdp"), None),
        P(("dp", "fsdp"), None),
        P(("dp", "fsdp"), None),
        P(("dp", "fsdp")),
        P(("dp", "fsdp")),
        P(("dp", "fsdp")),
        P(("dp", "fsdp")),
        P(("dp", "fsdp")),
        P(("dp", "fsdp"), None),
        P(("dp", "fsdp")),
        P(("dp", "fsdp"), None),
        P(("dp", "fsdp")),
        P(("dp", "fsdp")),
        P(("dp", "fsdp")),
    )
    return jax.shard_map(
        on_device,
        mesh=mesh,
        in_specs=placed,
        out_specs=(
            P(("dp", "fsdp"), None, None),
            P(("dp", "fsdp"), None, None),
            P(("dp", "fsdp"), None),
            P(("dp", "fsdp"), None),
            P(("dp", "fsdp"), None),
            P(("dp", "fsdp"), None),
            P(("dp", "fsdp")),
            P(("dp", "fsdp")),
            P(("dp", "fsdp")),
            P(("dp", "fsdp")),
            P(("dp", "fsdp")),
            P(("dp", "fsdp"), None),
            P(("dp", "fsdp")),
            P(("dp", "fsdp"), None),
            P(("dp", "fsdp")),
            P(("dp", "fsdp")),
            P(("dp", "fsdp")),
        ),
        check_vma=False,
    )
```

profile of v0, /device:TPU:0, one launch (start us, length us, event | category | flops | bytes accessed | tf_op | source)
XLA Modules:
  0.0 1803.1 jit_solution(4948897000619133253)
XLA Ops:
  20.3 11.5 copy.124
  34.3 42.8 %all-reduce.18 = (bf16[1024]{0:T(1024)(128)(2,1)S(1)}, bf16[1024]{0:T(1024)(128)(2,1)S(1)}, bf16[1024]{0:T(1024)(128)(2,1)S(1)}, bf16[1024]{0:T(1024)(128)(2,1)S...) all-reduce(bf16[1024]{0:T(1024)(128)(2,1)S(1)} %dynamic-update-slic, ...), channel_id=1, replica_groups=mesh['dp'=4,'fsdp'=8] {'dp','fsdp'}, use_global_device_ids=true, to_apply=%add.2 | all-reduce | flops 8192 | bytes 32768
  77.2 65.5 %all-gather = bf16[32,1,128]{2,1,0:T(2,128)(2,1)S(1)} all-gather(bf16[1,1,128]{2,1,0:T(2,128)(2,1)S(1)} %bitcast.153), channel_id=1, replica_groups=mesh['dp'=4,'fsdp'=8] {'dp','fsdp'}, dimensions={0}, use_global_device_ids=true | all-gather | bytes 8448 | tf_op jit(solution)/shard_map/all_gather | solution.py:114
  161.6 47.6 %all-gather.13.cloned.1.call-done = bf16[1024,1024]{1,0:T(8,128)(2,1)} async-done(((bf16[32,1024]{1,0:T(8,128)(2,1)}), bf16[1024,1024]{1,0:T(8,128)(2,1)}) %all-gather.13.cloned.1.call-update) | async-done | bytes 2097168 | tf_op jit(solution)/shard_map/all_gather | solution.py:103
  218.9 12.8 multiply_reduce_fusion.1
  242.0 12.0 fusion.56
  254.1 13.8 all-gather.15.cloned.1.call-done
  275.4 72.1 %all-gather.17.cloned.1.call-done = bf16[1024,4096]{1,0:T(8,128)(2,1)} async-done(((bf16[32,4096]{1,0:T(8,128)(2,1)}), bf16[1024,4096]{1,0:T(8,128)(2,1)}) %all-gather.17.cloned.1.call-update) | async-done | bytes 8388624 | tf_op jit(solution)/shard_map/all_gather | solution.py:113
  347.5 21.3 %fusion.33 = (u8[320,4096]{1,0:T(8,128)(4,1)S(1)}, u8[320,4096]{1,0:T(8,128)(4,1)S(1)}, f32[3,320,4096]{2,1,0:T(8,128)}) fusion(f32[4096]{0:T(1024)S(1)} %bitcast.150, bf16[1024,4096]{1,0:T(8,128)(2,1)} %all-gather.17.cloned.1.call-done, f32[3,320,1024]{2,1,0:T(8,128)} %copy-done.6, f32[1024]{0:T(1024)S(1)} %convert_element_type.134, ...), kind=kOutput, calls=%fused_computation.78 | convolution fusion | flops 8110407680 | bytes 30703104 | tf_op jit(solution)/shard_map/rsd,de->rse/dot_general | solution.py:36
  368.8 38.6 %multiply_convert_fusion.1 = (bf16[3,320,4096]{2,1,0:T(8,128)(2,1)}, f32[3,320,4096]{2,1,0:T(8,128)}) fusion(f32[3,320,4096]{2,1,0:T(8,128)} %get-tuple-element.109, f32[4096]{0:T(1024)S(1)} %bitcast.151, u8[320,4096]{1,0:T(8,128)(4,1)S(1)} %get-tuple-element.69, u8[320,4096]{1,0:T(8,128)(4,1)S(1)} %get-tuple-element.68), kind=kLoop, calls=%fused_computation.18 | loop fusion | flops 279183360 | bytes 41959424 | tf_op jit(solution)/shard_map/convert_element_type | solution.py:149
  407.3 19.3 %all-gather.19.cloned.1.call-done = bf16[4096,1024]{1,0:T(8,128)(2,1)} async-done(((bf16[128,1024]{1,0:T(8,128)(2,1)}), bf16[4096,1024]{1,0:T(8,128)(2,1)}) %all-gather.19.cloned.1.call-update) | async-done | bytes 8388624 | tf_op jit(solution)/shard_map/all_gather | solution.py:115
  426.6 14.2 fusion.87
  452.7 26.6 %convert_reduce_fusion = (f32[4096]{0:T(1024)}, bf16[3,320,4096]{2,1,0:T(8,128)(2,1)}) fusion(f32[3,320,4096]{2,1,0:T(8,128)} %get-tuple-element.102, bf16[3,320,1024]{2,1,0:T(8,128)(2,1)} %get-tuple-element.96, bf16[4096,1024]{1,0:T(8,128)(2,1)} %all-gather.19.cloned.1.call-done, f32[3,320,4096]{2,1,0:T(8,128)} %get-tuple-element.109, f32[4096]{0:T(1024)S(1)} %bitcast.152), kind=kOutput, calls=%fused_computation.16 | convolution fusion | flops 8119906304 | bytes 49709056 | tf_op jit(solution)/shard_map/rse,de->rsd/dot_general | solution.py:40
  479.3 16.3 multiply_reduce_fusion.2
  532.8 21.2 %multiply_reduce_fusion = (f32[3,16,320]{2,1,0:T(8,128)S(1)}, f32[3,16,320,320]{2,3,1,0:T(8,128)}) fusion(f32[3,16,320,320]{2,3,1,0:T(8,128)} %get-tuple-element.106, f32[3,16,320]{2,1,0:T(8,128)S(1)} %log_add_fusion, bf16[3,320,16,64]{1,3,2,0:T(8,128)(2,1)S(1)} %bitcast.139, bf16[3,320,16,64]{1,3,2,0:T(8,128)(2,1)} %bitcast.142), kind=kOutput, calls=%fused_computation.2 | convolution fusion | flops 648791040 | bytes 43376640 | tf_op jit(solution)/shard_map/rqhd,rkhd->rhqk/dot_general | solution.py:221
  554.0 15.9 multiply_convert_fusion
  609.0 16.3 convolution_bitcast_fusion.1
  626.8 14.5 convolution_bitcast_fusion
  642.4 42.4 %all-reduce.17 = (f32[1024]{0:T(1024)S(1)}, f32[1024]{0:T(1024)S(1)}, f32[1024]{0:T(1024)S(1)}, f32[1024]{0:T(1024)S(1)}, f32[1024]{0:T(1024)S(1)}, /*index=5*/f...) all-reduce(f32[1024]{0:T(1024)S(1)} %reduce_sum.186, ...), channel_id=7, replica_groups=mesh['dp'=4,'fsdp'=8] {'dp','fsdp'}, use_global_device_ids=true, to_apply=%region_17.18.clone | all-reduce | flops 12288 | bytes 98304
  715.2 72.9 %reduce-scatter.26.cloned.1.call-done = f32[32,1024]{1,0:T(8,128)} async-done(((f32[1024,1024]{1,0:T(8,128)}), f32[32,1024]{1,0:T(8,128)}) %reduce-scatter.26.cloned.1.call-update) | async-done | bytes 131088
  788.2 145.0 %reduce-scatter.22.cloned.1.call-done = f32[32,1024]{1,0:T(8,128)} async-done(((f32[1024,1024]{1,0:T(8,128)}), f32[32,1024]{1,0:T(8,128)}) %reduce-scatter.22.cloned.1.call-update) | async-done | bytes 131088
  933.1 142.7 %reduce-scatter.24.cloned.1.call-done = f32[32,1024]{1,0:T(8,128)} async-done(((f32[1024,1024]{1,0:T(8,128)}), f32[32,1024]{1,0:T(8,128)}) %reduce-scatter.24.cloned.1.call-update) | async-done | bytes 131088
  1075.8 359.5 %reduce-scatter.18.cloned.1.call-done = f32[32,4096]{1,0:T(8,128)} async-done(((f32[1024,4096]{1,0:T(8,128)}), f32[32,4096]{1,0:T(8,128)}) %reduce-scatter.18.cloned.1.call-update) | async-done | bytes 524304 | tf_op jit(solution)/shard_map/reduce_scatter | solution.py:260
  1435.3 360.2 %reduce-scatter.20.cloned.1.call-done = f32[128,1024]{1,0:T(8,128)} async-done(((f32[4096,1024]{1,0:T(8,128)}), f32[128,1024]{1,0:T(8,128)}) %reduce-scatter.20.cloned.1.call-update) | async-done | bytes 524304 | tf_op jit(solution)/shard_map/reduce_scatter | solution.py:262
  (191 shorter events, 180.9 us)
Async XLA Ops:
  8.0 134.8 %all-gather.11.cloned.1.call-start = ((), (), s32[]{:S(2)}) async-start(), calls=%async_computation.8 | async-start | bytes 2162688 | tf_op jit(solution)/shard_map/all_gather | solution.py:102
  8.8 142.3 %all-gather.9.cloned.1.call-start = ((), (), s32[]{:S(2)}) async-start(), calls=%async_computation.7 | async-start | bytes 2162688 | tf_op jit(solution)/shard_map/all_gather | solution.py:104
  9.5 199.7 %all-gather.13.cloned.1.call-start = ((), (), s32[]{:S(2)}) async-start(), calls=%async_computation.9 | async-start | bytes 2162688 | tf_op jit(solution)/shard_map/all_gather | solution.py:103
  10.2 257.7 %all-gather.15.cloned.1.call-start = ((), (), s32[]{:S(2)}) async-start(), calls=%async_computation.10 | async-start | bytes 2162688 | tf_op jit(solution)/shard_map/all_gather | solution.py:105
  10.8 336.6 %all-gather.17.cloned.1.call-start = ((), (), s32[]{:S(2)}) async-start(), calls=%async_computation.11 | async-start | bytes 8650752 | tf_op jit(solution)/shard_map/all_gather | solution.py:113
  11.4 415.2 %all-gather.19.cloned.1.call-start = ((), (), s32[]{:S(2)}) async-start(), calls=%async_computation.12 | async-start | bytes 8650752 | tf_op jit(solution)/shard_map/all_gather | solution.py:115
  12.0 431.4 %reduce-scatter.14.cloned.1.call-start = ((), (), s32[]{:S(2)}) async-start(), calls=%async_computation.14 | async-start | bytes 9830400 | tf_op jit(solution)/shard_map/reduce_scatter | solution.py:80
  31.9 45.3 %copy-start.24 = (bf16[128]{0:T(256)(128)(2,1)S(1)}, bf16[128]{0:T(256)(128)(2,1)}, u32[]{:S(2)}) copy-start(bf16[128]{0:T(256)(128)(2,1)} %param.33) | copy-start | bytes 772
  31.9 110.9 %copy-start.27 = (bf16[3,320,1024]{2,1,0:T(8,128)(2,1)S(1)}, bf16[3,320,1024]{2,1,0:T(8,128)(2,1)}, u32[]{:S(2)}) copy-start(bf16[3,320,1024]{2,1,0:T(8,128)(2,1)} %param.19) | copy-start | bytes 5898244
  31.9 672.7 %all-gather.21.cloned.1.call-start = ((), (), s32[]{:S(2)}) async-start(), calls=%async_computation.13 | async-start | bytes 9830400 | tf_op jit(solution)/shard_map/all_gather | solution.py:154
  151.0 67.9 %copy-start.3 = (bf16[3,320,1024]{1,2,0:T(8,128)(2,1)}, bf16[3,320,1024]{1,2,0:T(8,128)(2,1)S(1)}, u32[]{:S(2)}) copy-start(bf16[3,320,1024]{1,2,0:T(8,128)(2,1)S(1)} %copy.83) | copy-start | bytes 5898244
  231.7 10.3 copy-start.9
  242.0 25.9 %copy-start.28 = (bf16[3,320,1024]{2,1,0:T(8,128)(2,1)S(1)}, bf16[3,320,1024]{2,1,0:T(8,128)(2,1)}, u32[]{:S(2)}) copy-start(bf16[3,320,1024]{2,1,0:T(8,128)(2,1)} %param.19) | copy-start | bytes 5898244
  452.7 262.6 %reduce-scatter.16.cloned.1.call-start = ((), (), s32[]{:S(2)}) async-start(), calls=%async_computation.15 | async-start | bytes 4325376 | tf_op jit(solution)/shard_map/reduce_scatter | solution.py:254
  479.3 16.3 copy-start.7
  503.0 285.2 %reduce-scatter.26.cloned.1.call-start = ((), (), s32[]{:S(2)}) async-start(), calls=%async_computation.20 | async-start | bytes 4325376
  511.4 11.7 copy-start.29
  532.8 400.3 %reduce-scatter.22.cloned.1.call-start = ((), (), s32[]{:S(2)}) async-start(), calls=%async_computation.18 | async-start | bytes 4325376
  554.0 16.0 copy-start.5
  570.0 6.0 copy-start.30
  585.8 490.0 %reduce-scatter.24.cloned.1.call-start = ((), (), s32[]{:S(2)}) async-start(), calls=%async_computation.19 | async-start | bytes 4325376
  608.9 826.3 %reduce-scatter.18.cloned.1.call-start = ((), (), s32[]{:S(2)}) async-start(), calls=%async_computation.16 | async-start | bytes 17301504 | tf_op jit(solution)/shard_map/reduce_scatter | solution.py:260
  625.3 1170.1 %reduce-scatter.20.cloned.1.call-start = ((), (), s32[]{:S(2)}) async-start(), calls=%async_computation.17 | async-start | bytes 17301504 | tf_op jit(solution)/shard_map/reduce_scatter | solution.py:262
  641.4 48.6 %copy-start.17 = (bf16[3,16,64,320]{3,2,1,0:T(8,128)(2,1)S(1)}, bf16[3,16,64,320]{3,2,1,0:T(8,128)(2,1)}, u32[]{:S(2)}) copy-start(bf16[3,16,64,320]{3,2,1,0:T(8,128)(2,1)} %copy-done.16) | copy-start | bytes 5898244
  (30 other events, 70.7 us)
Sparse Core Ops, SparseCore 0:
  12.3 59.4 all-gather.10
  75.2 75.1 all-gather.8
  153.8 55.3 all-gather.12
  212.5 55.3 all-gather.14
  271.2 76.2 all-gather.16
  350.7 75.8 all-gather.18
  503.1 142.0 reduce-scatter.15
  648.1 139.9 reduce-scatter.25
  791.1 141.9 reduce-scatter.21
  935.9 139.8 reduce-scatter.23
  1078.8 356.4 reduce-scatter.17
  1438.1 357.2 reduce-scatter.19
Sparse Core Ops, SparseCore 1:
  32.0 75.4 reduce-scatter.13
  452.7 53.8 all-gather.20
where the time goes:
time: 1810 us; the launch traced here: 1800 us
  waiting for transfers between devices  1240 us (69%)
  matrix products  245 us (14%)
  blocking collectives  151 us (8%)
  other arithmetic  81.2 us (4%)
  local copies, waits for them, and re-layouts  70.8 us (4%)
    unnamed x17, waiting for transfers between devices  364 us
    reduce_scatter x1, waiting for transfers between devices, on_device(): lax.psum_scatter(down_grad, ('dp', 'fsdp'), scatter_dimension=0, tiled=True)  360 us
    reduce_scatter x1, waiting for transfers between devices, on_device(): lax.psum_scatter(up_grad, ('dp', 'fsdp'), scatter_dimension=0, tiled=True)  359 us
    unnamed x2, blocking collectives  85.2 us
    all_gather x1, waiting for transfers between devices, on_device(): lax.all_gather(expand_weight, ('dp', 'fsdp'), axis=0, tiled=True)  72.1 us
    all_gather x1, blocking collectives, on_device(): lax.all_gather(up_bias, ('dp', 'fsdp'), axis=0, tiled=True)  65.5 us
    dot_general x6, matrix products, apply_back(): jnp.einsum('rse,de->rsd', grads, weight, preferred_element_type=jnp.float32)  60.6 us
    dot_general x6, matrix products, apply_weight(): jnp.einsum('rsd,de->rse', acts, weight, preferred_element_type=jnp.float32)  57.8 us
  transfers between devices with their start and end apart: 14, of which 9 were waited for; matrix products, arithmetic and copies ran while one was open for 21% of the time, Pallas kernels for 0%

commit v1 on v0

--- a/solution.py
+++ b/solution.py
@@ -88,34 +88,24 @@
         scatter_dimension=0,
         tiled=True,
     ).astype(jnp.float32)
+    smalls = (query_bias, value_bias, output_bias, attn_gain, attn_shift, down_bias, ffn_gain, ffn_shift)
+    small_rows = query_bias.shape[0]
+    packed = jnp.concatenate([v.reshape(-1, small_rows) for v in (*smalls, up_bias)], axis=0)
+    packed_full = lax.all_gather(packed, ("dp", "fsdp"), axis=0)
     (
-        query_full,
-        key_full,
-        value_full,
-        output_full,
         qbias_full,
         vbias_full,
         obias_full,
         gain1_full,
         shift1_full,
-    ) = (
-        lax.all_gather(query_weight, ("dp", "fsdp"), axis=0, tiled=True),
-        lax.all_gather(key_weight, ("dp", "fsdp"), axis=0, tiled=True),
-        lax.all_gather(value_weight, ("dp", "fsdp"), axis=0, tiled=True),
-        lax.all_gather(output_weight, ("dp", "fsdp"), axis=0, tiled=True),
-        lax.all_gather(query_bias, ("dp", "fsdp"), axis=0, tiled=True),
-        lax.all_gather(value_bias, ("dp", "fsdp"), axis=0, tiled=True),
-        lax.all_gather(output_bias, ("dp", "fsdp"), axis=0, tiled=True),
-        lax.all_gather(attn_gain, ("dp", "fsdp"), axis=0, tiled=True),
-        lax.all_gather(attn_shift, ("dp", "fsdp"), axis=0, tiled=True),
-    )
-    up_full, upbias_full, down_full, downbias_full, gain2_full, shift2_full = (
-        lax.all_gather(expand_weight, ("dp", "fsdp"), axis=0, tiled=True),
-        lax.all_gather(up_bias, ("dp", "fsdp"), axis=0, tiled=True),
-        lax.all_gather(down_weight, ("dp", "fsdp"), axis=0, tiled=True),
-        lax.all_gather(down_bias, ("dp", "fsdp"), axis=0, tiled=True),
-        lax.all_gather(ffn_gain, ("dp", "fsdp"), axis=0, tiled=True),
-        lax.all_gather(ffn_shift, ("dp", "fsdp"), axis=0, tiled=True),
+        downbias_full,
+        gain2_full,
+        shift2_full,
+    ) = (packed_full[:, i].reshape(-1) for i in range(8))
+    upbias_full = packed_full[:, 8:].reshape(-1)
+    query_full, key_full, value_full, output_full, up_full, down_full = (
+        lax.all_gather(weight, ("dp", "fsdp"), axis=0, tiled=True)
+        for weight in (query_weight, key_weight, value_weight, output_weight, expand_weight, down_weight)
     )
     inputs = rows_in.astype(jnp.float32)
     query = (apply_weight(rows_in, query_full) + qbias_full.astype(jnp.float32)).astype(
@@ -157,39 +147,6 @@
     picked = jnp.take(shard_rows, jnp.clip(slot_row, 0, span_rows - 1), axis=0)
     slot_acts = jnp.where(
         inside[:, None, None], picked, jnp.zeros(slot_activation_gradient.shape, jnp.bfloat16)
-    )
-    (
-        query_full,
-        key_full,
-        value_full,
-        output_full,
-        qbias_full,
-        vbias_full,
-        obias_full,
-        gain1_full,
-        shift1_full,
-        up_full,
-        upbias_full,
-        down_full,
-        downbias_full,
-        gain2_full,
-        shift2_full,
-    ) = (
-        lax.all_gather(query_weight, ("dp", "fsdp"), axis=0, tiled=True),
-        lax.all_gather(key_weight, ("dp", "fsdp"), axis=0, tiled=True),
-        lax.all_gather(value_weight, ("dp", "fsdp"), axis=0, tiled=True),
-        lax.all_gather(output_weight, ("dp", "fsdp"), axis=0, tiled=True),
-        lax.all_gather(query_bias, ("dp", "fsdp"), axis=0, tiled=True),
-        lax.all_gather(value_bias, ("dp", "fsdp"), axis=0, tiled=True),
-        lax.all_gather(output_bias, ("dp", "fsdp"), axis=0, tiled=True),
-        lax.all_gather(attn_gain, ("dp", "fsdp"), axis=0, tiled=True),
-        lax.all_gather(attn_shift, ("dp", "fsdp"), axis=0, tiled=True),
-        lax.all_gather(expand_weight, ("dp", "fsdp"), axis=0, tiled=True),
-        lax.all_gather(up_bias, ("dp", "fsdp"), axis=0, tiled=True),
-        lax.all_gather(down_weight, ("dp", "fsdp"), axis=0, tiled=True),
-        lax.all_gather(down_bias, ("dp", "fsdp"), axis=0, tiled=True),
-        lax.all_gather(ffn_gain, ("dp", "fsdp"), axis=0, tiled=True),
-        lax.all_gather(ffn_shift, ("dp", "fsdp"), axis=0, tiled=True),
     )
     gain1 = gain1_full.astype(jnp.float32)
     gain2 = gain2_full.astype(jnp.float32)
@@ -247,41 +204,49 @@
     )
     live_rows = lax.broadcasted_iota(jnp.int32, (row_count,), 0) < live_count[0]
     input_grad = jnp.where(live_rows[:, None, None], input_full, 0.0)
-    summed = (
-        lax.psum_scatter(query_wgrad, ("dp", "fsdp"), scatter_dimension=0, tiled=True),
-        lax.psum_scatter(key_wgrad, ("dp", "fsdp"), scatter_dimension=0, tiled=True),
-        lax.psum_scatter(value_wgrad, ("dp", "fsdp"), scatter_dimension=0, tiled=True),
-        lax.psum_scatter(output_grad, ("dp", "fsdp"), scatter_dimension=0, tiled=True),
-        lax.psum_scatter(query_bias_grad, ("dp", "fsdp"), scatter_dimension=0, tiled=True),
-        lax.psum_scatter(value_bias_grad, ("dp", "fsdp"), scatter_dimension=0, tiled=True),
-        lax.psum_scatter(output_bias_grad, ("dp", "fsdp"), scatter_dimension=0, tiled=True),
-        lax.psum_scatter(gain1_grad, ("dp", "fsdp"), scatter_dimension=0, tiled=True),
-        lax.psum_scatter(shift1_grad, ("dp", "fsdp"), scatter_dimension=0, tiled=True),
-        lax.psum_scatter(up_grad, ("dp", "fsdp"), scatter_dimension=0, tiled=True),
-        lax.psum_scatter(up_bias_grad, ("dp", "fsdp"), scatter_dimension=0, tiled=True),
-        lax.psum_scatter(down_grad, ("dp", "fsdp"), scatter_dimension=0, tiled=True),
-        lax.psum_scatter(down_bias_grad, ("dp", "fsdp"), scatter_dimension=0, tiled=True),
-        lax.psum_scatter(gain2_grad, ("dp", "fsdp"), scatter_dimension=0, tiled=True),
-        lax.psum_scatter(shift2_grad, ("dp", "fsdp"), scatter_dimension=0, tiled=True),
+    devices = packed_full.shape[0]
+    small_terms = jnp.concatenate(
+        [
+            v.reshape(devices, -1, small_rows)
+            for v in (
+                query_bias_grad,
+                value_bias_grad,
+                output_bias_grad,
+                gain1_grad,
+                shift1_grad,
+                down_bias_grad,
+                gain2_grad,
+                shift2_grad,
+                up_bias_grad,
+            )
+        ],
+        axis=1,
+    )
+    small_sum = lax.psum_scatter(small_terms, ("dp", "fsdp"), scatter_dimension=0, tiled=True)[0]
+    down_sum, up_sum, output_sum, value_sum, query_sum, key_sum = (
+        lax.psum_scatter(
+            term.astype(jnp.bfloat16), ("dp", "fsdp"), scatter_dimension=0, tiled=True
+        ).astype(jnp.float32)
+        for term in (down_grad, up_grad, output_grad, value_wgrad, query_wgrad, key_wgrad)
     )
     return (
         slot_acts,
         input_grad,
-        summed[0],
-        summed[1],
-        summed[2],
-        summed[3],
-        summed[4],
-        summed[5],
-        summed[6],
-        summed[7],
-        summed[8],
-        summed[9],
-        summed[10],
-        summed[11],
-        summed[12],
-        summed[13],
-        summed[14],
+        query_sum,
+        key_sum,
+        value_sum,
+        output_sum,
+        small_sum[0],
+        small_sum[1],
+        small_sum[2],
+        small_sum[3],
+        small_sum[4],
+        up_sum,
+        small_sum[8:].reshape(-1),
+        down_sum,
+        small_sum[5],
+        small_sum[6],
+        small_sum[7],
     )
 
 

time: 1810 us -> 1620 us (0.90)
  waiting for transfers between devices: 1240 us -> 1130 us
  blocking collectives: 151 us -> 71.8 us
    reduce_scatter x3 -> x4, waiting for transfers between devices: 720 us -> 534 us  [the longest x3 491 us: on_device(): lax.psum_scatter(term.astype(jnp.bfloat16), ('dp', 'fsdp'), scatter_dimen...]
    unnamed x2 -> x0, blocking collectives: 85.2 us -> none
    unnamed x17 -> x18, waiting for transfers between devices: 364 us -> 407 us
    all_gather x6, waiting for transfers between devices: 153 us -> 192 us  [on_device(): lax.all_gather(weight, ('dp', 'fsdp'), axis=0, tiled=True)]
    unnamed x108 -> x81, local copies, waits for them, and re-layouts: 38.6 us -> 28.1 us
  transfers between devices with their start and end apart: 14 -> 15, of which waited for: 9 -> 12; matrix products, arithmetic and copies ran while one was open for 21% -> 17% of each run, Pallas kernels for 0% -> 0%
where the time goes in v1:
time: 1620 us
  waiting for transfers between devices  1130 us (70%)
  matrix products  243 us (15%)
  other arithmetic  85.3 us (5%)
  blocking collectives  71.8 us (4%)
  local copies, waits for them, and re-layouts  64.2 us (4%)
  between operations  17.1 us (1%)
    reduce_scatter x3, waiting for transfers between devices, on_device(): lax.psum_scatter(term.astype(jnp.bfloat16), ('dp', 'fsdp'), scatter_dimen...  491 us
    unnamed x18, waiting for transfers between devices  407 us
    all_gather x6, waiting for transfers between devices, on_device(): lax.all_gather(weight, ('dp', 'fsdp'), axis=0, tiled=True)  192 us
    all_gather x1, blocking collectives, on_device(): packed_full = lax.all_gather(packed, ('dp', 'fsdp'), axis=0)  71.8 us
    dot_general x6, matrix products, apply_back(): jnp.einsum('rse,de->rsd', grads, weight, preferred_element_type=jnp.float32)  57.3 us
    dot_general x6, matrix products, apply_weight(): jnp.einsum('rsd,de->rse', acts, weight, preferred_element_type=jnp.float32)  56.4 us
    dot_general x6, matrix products, weight_term(): jnp.einsum('rsd,rse->de', acts, grads, preferred_element_type=jnp.float32)  50.6 us
    reduce_scatter x1, waiting for transfers between devices, on_device(): lax.psum_scatter(small_terms, ('dp', 'fsdp'), scatter_dimension=0, tiled=...  42.7 us
  transfers between devices with their start and end apart: 15, of which 12 were waited for; matrix products, arithmetic and copies ran while one was open for 17% of the time, Pallas kernels for 0%

profile of v1, /device:TPU:0, one launch (start us, length us, event | category | flops | bytes accessed | tf_op | source)
XLA Modules:
  0.0 1615.1 jit_solution(8123495696669099)
XLA Ops:
  32.8 71.8 %all-gather.1 = bf16[32,12,32]{2,1,0:T(8,128)(2,1)S(1)} all-gather(bf16[1,12,32]{2,1,0:T(8,128)(2,1)S(1)} %bitcast.179), channel_id=2, replica_groups=mesh['dp'=4,'fsdp'=8] {'dp','fsdp'}, dimensions={0}, use_global_device_ids=true | all-gather | bytes 25344 | tf_op jit(solution)/shard_map/all_gather | solution.py:94
  112.9 37.0 %all-gather.12.cloned.1.call-done = bf16[1024,1024]{1,0:T(8,128)(2,1)} async-done(((bf16[32,1024]{1,0:T(8,128)(2,1)}), bf16[1024,1024]{1,0:T(8,128)(2,1)}) %all-gather.12.cloned.1.call-update) | async-done | bytes 2097168 | tf_op jit(solution)/shard_map/all_gather | solution.py:107
  158.4 50.3 %all-gather.14.cloned.1.call-done = bf16[1024,1024]{1,0:T(8,128)(2,1)} async-done(((bf16[32,1024]{1,0:T(8,128)(2,1)}), bf16[1024,1024]{1,0:T(8,128)(2,1)}) %all-gather.14.cloned.1.call-update) | async-done | bytes 2097168 | tf_op jit(solution)/shard_map/all_gather | solution.py:107
  218.4 12.8 multiply_reduce_fusion.1
  241.6 12.0 fusion.56
  253.6 13.8 all-gather.16.cloned.1.call-done
  275.0 72.0 %all-gather.18.cloned.1.call-done = bf16[1024,4096]{1,0:T(8,128)(2,1)} async-done(((bf16[32,4096]{1,0:T(8,128)(2,1)}), bf16[1024,4096]{1,0:T(8,128)(2,1)}) %all-gather.18.cloned.1.call-update) | async-done | bytes 8388624 | tf_op jit(solution)/shard_map/all_gather | solution.py:107
  347.0 21.3 %fusion.33 = (u8[320,4096]{1,0:T(8,128)(4,1)S(1)}, u8[320,4096]{1,0:T(8,128)(4,1)S(1)}, f32[3,320,4096]{2,1,0:T(8,128)}) fusion(f32[4096]{0:T(1024)S(1)} %reshape.293, bf16[1024,4096]{1,0:T(8,128)(2,1)} %all-gather.18.cloned.1.call-done, f32[3,320,1024]{2,1,0:T(8,128)} %copy-done.6, f32[1024]{0:T(1024)S(1)} %reshape.292, f32[1024]{0:T(1024)S(1)} %reshape.291, ...), kind=kOutput, calls=%fused_computation.82 | convolution fusion | flops 8110407680 | bytes 30703104 | tf_op jit(solution)/shard_map/rsd,de->rse/dot_general | solution.py:36
  368.3 38.6 %multiply_convert_fusion.1 = (bf16[3,320,4096]{2,1,0:T(8,128)(2,1)}, f32[3,320,4096]{2,1,0:T(8,128)}) fusion(f32[3,320,4096]{2,1,0:T(8,128)} %get-tuple-element.108, f32[4096]{0:T(1024)S(1)} %reshape.293, u8[320,4096]{1,0:T(8,128)(4,1)S(1)} %get-tuple-element.69, u8[320,4096]{1,0:T(8,128)(4,1)S(1)} %get-tuple-element.68), kind=kLoop, calls=%fused_computation.20 | loop fusion | flops 279183360 | bytes 41959424 | tf_op jit(solution)/shard_map/convert_element_type | solution.py:139
  406.8 19.4 %all-gather.20.cloned.1.call-done = bf16[4096,1024]{1,0:T(8,128)(2,1)} async-done(((bf16[128,1024]{1,0:T(8,128)(2,1)}), bf16[4096,1024]{1,0:T(8,128)(2,1)}) %all-gather.20.cloned.1.call-update) | async-done | bytes 8388624 | tf_op jit(solution)/shard_map/all_gather | solution.py:107
  426.2 14.3 fusion.98
  450.9 24.2 %convert_reduce_fusion = (f32[4096]{0:T(1024)S(1)}, bf16[3,320,4096]{2,1,0:T(8,128)(2,1)}) fusion(f32[3,320,4096]{2,1,0:T(8,128)} %get-tuple-element.93, bf16[3,320,1024]{2,1,0:T(8,128)(2,1)} %get-tuple-element.87, bf16[4096,1024]{1,0:T(8,128)(2,1)} %all-gather.20.cloned.1.call-done, f32[3,320,4096]{2,1,0:T(8,128)} %get-tuple-element.108, ...), kind=kOutput, calls=%fused_computation.18 | convolution fusion | flops 8119906304 | bytes 49709056 | tf_op jit(solution)/shard_map/rse,de->rsd/dot_general | solution.py:40
  475.2 16.7 %multiply_reduce_fusion.2 = (f32[1024]{0:T(1024)S(1)}, f32[3,320]{1,0:T(4,128)S(1)}, f32[3,320]{1,0:T(4,128)S(1)}, f32[1024]{0:T(1024)S(1)}, f32[3,320,1024]{2,1,0:T(8,128)S(1)}) fusion(f32[3,320,1024]{2,1,0:T(8,128)} %copy-done.6, f32[3,320]{1,0:T(4,128)S(1)} %add_rsqrt_fusion.1, f32[3,320]{1,0:T(4,128)S(1)} %broadcast_multiply_fusion.5, ...), kind=kOutput, calls=%fused_computation.67 | convolution fusion | flops 8070754304 | bytes 30062592 | tf_op jit(solution)/shard_map/rse,de->rsd/dot_general | solution.py:40
  512.8 20.9 %multiply_reduce_fusion = (f32[3,16,320]{2,1,0:T(8,128)S(1)}, f32[3,16,320,320]{2,3,1,0:T(8,128)}) fusion(f32[3,16,320,320]{2,3,1,0:T(8,128)} %get-tuple-element.105, f32[3,16,320]{2,1,0:T(8,128)S(1)} %log_add_fusion, bf16[3,320,16,64]{1,3,2,0:T(8,128)(2,1)S(1)} %bitcast.168, bf16[3,320,16,64]{1,3,2,0:T(8,128)(2,1)} %bitcast.171), kind=kOutput, calls=%fused_computation.2 | convolution fusion | flops 648791040 | bytes 43376640 | tf_op jit(solution)/shard_map/rqhd,rkhd->rhqk/dot_general | solution.py:178
  534.4 15.9 multiply_convert_fusion
  600.6 14.5 bitcast_convert_fusion
  615.8 15.2 bitcast_convert_fusion.1
  647.4 42.7 %reduce-scatter.19.cloned.1.call-done = f32[1,12,32]{2,1,0:T(8,128)} async-done(((f32[32,12,32]{2,1,0:T(8,128)}), f32[1,12,32]{2,1,0:T(8,128)}) %reduce-scatter.19.cloned.1.call-update) | async-done | bytes 1552 | tf_op jit(solution)/shard_map/reduce_scatter | solution.py:225
  692.9 132.9 %reduce-scatter.29.cloned.1.call-done = bf16[32,1024]{1,0:T(8,128)(2,1)} async-done(((bf16[1024,1024]{1,0:T(8,128)(2,1)}), bf16[32,1024]{1,0:T(8,128)(2,1)}) %reduce-scatter.29.cloned.1.call-update) | async-done | bytes 65552
  827.6 135.1 %reduce-scatter.25.cloned.1.call-done = bf16[32,1024]{1,0:T(8,128)(2,1)} async-done(((bf16[1024,1024]{1,0:T(8,128)(2,1)}), bf16[32,1024]{1,0:T(8,128)(2,1)}) %reduce-scatter.25.cloned.1.call-update) | async-done | bytes 65552
  964.5 134.4 %reduce-scatter.27.cloned.1.call-done = bf16[32,1024]{1,0:T(8,128)(2,1)} async-done(((bf16[1024,1024]{1,0:T(8,128)(2,1)}), bf16[32,1024]{1,0:T(8,128)(2,1)}) %reduce-scatter.27.cloned.1.call-update) | async-done | bytes 65552
  1100.7 135.6 %reduce-scatter.17.cloned.1.call-done = bf16[32,1024]{1,0:T(8,128)(2,1)} async-done(((bf16[1024,1024]{1,0:T(8,128)(2,1)}), bf16[32,1024]{1,0:T(8,128)(2,1)}) %reduce-scatter.17.cloned.1.call-update) | async-done | bytes 65552 | tf_op jit(solution)/shard_map/reduce_scatter | solution.py:227
  1248.4 171.4 %reduce-scatter.23.cloned.1.call-done = bf16[128,1024]{1,0:T(8,128)(2,1)} async-done(((bf16[4096,1024]{1,0:T(8,128)(2,1)}), bf16[128,1024]{1,0:T(8,128)(2,1)}) %reduce-scatter.23.cloned.1.call-update) | async-done | bytes 262160 | tf_op jit(solution)/shard_map/reduce_scatter | solution.py:227
  1421.5 184.3 %reduce-scatter.21.cloned.1.call-done = bf16[32,4096]{1,0:T(8,128)(2,1)} async-done(((bf16[1024,4096]{1,0:T(8,128)(2,1)}), bf16[32,4096]{1,0:T(8,128)(2,1)}) %reduce-scatter.21.cloned.1.call-update) | async-done | bytes 262160 | tf_op jit(solution)/shard_map/reduce_scatter | solution.py:227
  (183 shorter events, 191.1 us)
Async XLA Ops:
  8.0 97.6 %all-gather.10.cloned.1.call-start = ((), (), s32[]{:S(2)}) async-start(), calls=%async_computation.8 | async-start | bytes 2162688 | tf_op jit(solution)/shard_map/all_gather | solution.py:107
  8.8 141.1 %all-gather.12.cloned.1.call-start = ((), (), s32[]{:S(2)}) async-start(), calls=%async_computation.9 | async-start | bytes 2162688 | tf_op jit(solution)/shard_map/all_gather | solution.py:107
  9.5 199.2 %all-gather.14.cloned.1.call-start = ((), (), s32[]{:S(2)}) async-start(), calls=%async_computation.10 | async-start | bytes 2162688 | tf_op jit(solution)/shard_map/all_gather | solution.py:107
  10.2 257.2 %all-gather.16.cloned.1.call-start = ((), (), s32[]{:S(2)}) async-start(), calls=%async_computation.11 | async-start | bytes 2162688 | tf_op jit(solution)/shard_map/all_gather | solution.py:107
  10.8 336.2 %all-gather.18.cloned.1.call-start = ((), (), s32[]{:S(2)}) async-start(), calls=%async_computation.12 | async-start | bytes 8650752 | tf_op jit(solution)/shard_map/all_gather | solution.py:107
  11.4 414.8 %all-gather.20.cloned.1.call-start = ((), (), s32[]{:S(2)}) async-start(), calls=%async_computation.13 | async-start | bytes 8650752 | tf_op jit(solution)/shard_map/all_gather | solution.py:107
  12.0 431.0 %reduce-scatter.15.cloned.1.call-start = ((), (), s32[]{:S(2)}) async-start(), calls=%async_computation.15 | async-start | bytes 9830400 | tf_op jit(solution)/shard_map/reduce_scatter | solution.py:80
  32.0 658.1 %reduce-scatter.19.cloned.1.call-start = ((), (), s32[]{:S(2)}) async-start(), calls=%async_computation.17 | async-start | bytes 270336 | tf_op jit(solution)/shard_map/reduce_scatter | solution.py:225
  105.3 320.9 %copy-start.20 = (f32[1024]{0:T(1024)}, f32[1024]{0:T(1024)S(1)}, u32[]{:S(2)}) copy-start(f32[1024]{0:T(1024)S(1)} %reshape.292) | copy-start | bytes 12292
  158.4 60.0 %copy-start.3 = (bf16[3,320,1024]{1,2,0:T(8,128)(2,1)}, bf16[3,320,1024]{1,2,0:T(8,128)(2,1)S(1)}, u32[]{:S(2)}) copy-start(bf16[3,320,1024]{1,2,0:T(8,128)(2,1)S(1)} %copy.83) | copy-start | bytes 5898244
  231.2 10.3 copy-start.9
  241.6 25.9 %copy-start.34 = (bf16[3,320,1024]{2,1,0:T(8,128)(2,1)S(1)}, bf16[3,320,1024]{2,1,0:T(8,128)(2,1)}, u32[]{:S(2)}) copy-start(bf16[3,320,1024]{2,1,0:T(8,128)(2,1)} %param.19) | copy-start | bytes 5898244
  442.9 4.8 copy-start.2
  475.2 16.7 %copy-start.7 = (f32[3,320,1024]{2,1,0:T(8,128)S(1)}, f32[3,320,1024]{2,1,0:T(8,128)}, u32[]{:S(2)}) copy-start(f32[3,320,1024]{2,1,0:T(8,128)} %copy-done.6) | copy-start | bytes 11796484
  534.4 16.0 copy-start.5
  550.4 5.5 copy-start
  550.4 7.1 copy-start.14
  557.5 268.3 %reduce-scatter.29.cloned.1.call-start = ((), (), s32[]{:S(2)}) async-start(), calls=%async_computation.22 | async-start | bytes 2162688
  566.9 395.8 %reduce-scatter.25.cloned.1.call-start = ((), (), s32[]{:S(2)}) async-start(), calls=%async_computation.20 | async-start | bytes 2162688
  576.3 522.6 %reduce-scatter.27.cloned.1.call-start = ((), (), s32[]{:S(2)}) async-start(), calls=%async_computation.21 | async-start | bytes 2162688
  593.1 643.2 %reduce-scatter.17.cloned.1.call-start = ((), (), s32[]{:S(2)}) async-start(), calls=%async_computation.16 | async-start | bytes 2162688 | tf_op jit(solution)/shard_map/reduce_scatter | solution.py:227
  599.0 638.7 %all-gather.22.cloned.1.call-start = ((), (), s32[]{:S(2)}) async-start(), calls=%async_computation.14 | async-start | bytes 9830400 | tf_op jit(solution)/shard_map/all_gather | solution.py:144
  599.6 820.1 %reduce-scatter.23.cloned.1.call-start = ((), (), s32[]{:S(2)}) async-start(), calls=%async_computation.19 | async-start | bytes 8650752 | tf_op jit(solution)/shard_map/reduce_scatter | solution.py:227
  615.1 990.7 %reduce-scatter.21.cloned.1.call-start = ((), (), s32[]{:S(2)}) async-start(), calls=%async_computation.18 | async-start | bytes 8650752 | tf_op jit(solution)/shard_map/reduce_scatter | solution.py:227
  (27 other events, 58.9 us)
Sparse Core Ops, SparseCore 0:
  12.3 59.4 all-gather.9
  75.2 74.6 all-gather.11
  153.3 55.3 all-gather.13
  212.0 55.3 all-gather.15
  270.7 76.2 all-gather.17
  350.2 75.8 all-gather.19
  557.6 132.3 reduce-scatter.18
  692.3 133.4 reduce-scatter.28
  828.2 134.5 reduce-scatter.24
  964.8 134.0 reduce-scatter.26
  1101.3 134.9 reduce-scatter.16
  1238.4 181.3 reduce-scatter.22
  1422.0 183.7 reduce-scatter.20
Sparse Core Ops, SparseCore 1:
  32.1 74.9 reduce-scatter.14
  601.2 54.2 all-gather.21

commit v2 on v1

--- a/solution.py
+++ b/solution.py
@@ -3,12 +3,298 @@
 import jax
 import jax.numpy as jnp
 from jax import lax
+from jax.experimental import pallas as pl
+from jax.experimental.pallas import tpu as pltpu
 from jax.sharding import PartitionSpec as P
 
 HEADS = 16
 
 
 EPSILON = 1e-05
+
+
+MESH = pl.DeviceIdType.MESH
+LANES = 128
+
+
+def place(nz, nx):
+    dp, fs = lax.axis_index("dp"), lax.axis_index("fsdp")
+    y, core = dp // 2, lax.rem(dp, 2)
+    z, x = fs // nx, lax.rem(fs, nx)
+    return y, core, z, x
+
+
+def device(y, core, z, x, nx):
+    return (y * 2 + core, z * nx + x)
+
+
+class Partners:
+    def __init__(self, nz, nx):
+        self.nz, self.nx = nz, nx
+        self.y, self.core, self.z, self.x = place(nz, nx)
+        y, core, z, x = self.y, self.core, self.z, self.x
+        self.sibling = device(y, 1 - core, z, x, nx)
+        self.across_x = device(y, core, z, 1 - x, nx)
+        self.across_y = device(1 - y, core, z, x, nx)
+        self.along_z = [device(y, core, lax.rem(z + k, nz), x, nx) for k in range(1, nz)]
+        self.all = [self.sibling, self.across_x, self.across_y, *self.along_z]
+
+    def meet(self):
+        barrier = pltpu.get_barrier_semaphore()
+        for other in self.all:
+            pl.semaphore_signal(barrier, inc=1, device_id=other, device_id_type=MESH)
+        pl.semaphore_wait(barrier, len(self.all))
+
+
+def remote(src, dst, send, recv, to):
+    return pltpu.make_async_remote_copy(
+        src_ref=src, dst_ref=dst, send_sem=send, recv_sem=recv, device_id=to, device_id_type=MESH
+    )
+
+
+def added(*blocks):
+    total = blocks[0].astype(jnp.float32)
+    for block in blocks[1:]:
+        total = total + block.astype(jnp.float32)
+    return total
+
+
+class Scatter:
+    def __init__(self, at, wide, rc, r3a, r3b, r2, rz, send, recv):
+        self.at, self.wide = at, wide
+        self.rc, self.r3a, self.r3b, self.r2, self.rz = rc, r3a, r3b, r2, rz
+        self.send, self.recv = send, recv
+
+    def to_sibling(self, m, theirs):
+        return remote(theirs, self.rc.at[m], self.send.at[m, 0], self.recv.at[m, 0], self.at.sibling)
+
+    def first_a(self, m):
+        at, wide = self.at, self.wide
+        src = self.rc.at[m, :, :, 1 - at.x, :, pl.ds(0, wide)]
+        return remote(src, self.r3a.at[m], self.send.at[m, 1], self.recv.at[m, 1], at.across_x)
+
+    def first_b(self, m):
+        at, wide = self.at, self.wide
+        src = self.rc.at[m, 1 - at.y, :, :, :, pl.ds(wide, self.rc.shape[-1] - wide)]
+        return remote(src, self.r3b.at[m], self.send.at[m, 2], self.recv.at[m, 2], at.across_y)
+
+    def second_a(self, m):
+        at, wide = self.at, self.wide
+        src, dst = self.r3a.at[m, 1 - at.y], self.r2.at[m, :, :, pl.ds(0, wide)]
+        return remote(src, dst, self.send.at[m, 3], self.recv.at[m, 3], at.across_y)
+
+    def second_b(self, m):
+        at, wide = self.at, self.wide
+        src = self.r3b.at[m, :, 1 - at.x]
+        dst = self.r2.at[m, :, :, pl.ds(wide, self.r2.shape[-1] - wide)]
+        return remote(src, dst, self.send.at[m, 4], self.recv.at[m, 4], at.across_x)
+
+    def last(self, m, k):
+        at = self.at
+        src = self.r2.at[m, lax.rem(at.z + k, at.nz)]
+        return remote(src, self.rz.at[m, k - 1], self.send.at[m, 4 + k], self.recv.at[m, 4 + k], at.along_z[k - 1])
+
+    def start(self, m, theirs):
+        self.to_sibling(m, theirs).start()
+
+    def step1(self, m, own):
+        at, rc = self.at, self.rc
+        self.to_sibling(m, rc.at[m]).wait_recv()
+        nz = at.nz
+
+        def add(i, carry):
+            y, z = i // nz, lax.rem(i, nz)
+            rc[m, y, z] = added(rc[m, y, z], own(y, z)).astype(rc.dtype)
+            return carry
+
+        lax.fori_loop(0, rc.shape[1] * nz, add, 0)
+        self.first_a(m).start()
+        self.first_b(m).start()
+
+    def step2(self, m):
+        at, rc, wide, r3a, r3b = self.at, self.rc, self.wide, self.r3a, self.r3b
+        columns = rc.shape[-1]
+        self.first_a(m).wait_recv()
+        self.first_b(m).wait_recv()
+
+        def add(z, carry):
+            for y in range(rc.shape[1]):
+                r3a[m, y, z] = added(r3a[m, y, z], rc[m, y, z, at.x, :, pl.ds(0, wide)]).astype(rc.dtype)
+            r3b[m, z] = added(r3b[m, z], rc[m, at.y, z, :, :, pl.ds(wide, columns - wide)]).astype(rc.dtype)
+            return carry
+
+        lax.fori_loop(0, at.nz, add, 0)
+        self.second_a(m).start()
+        self.second_b(m).start()
+
+    def step3(self, m):
+        at, r3a, r3b, r2, wide = self.at, self.r3a, self.r3b, self.r2, self.wide
+        columns = r2.shape[-1]
+        self.second_a(m).wait_recv()
+        self.second_b(m).wait_recv()
+
+        def add(z, carry):
+            left, right = pl.ds(0, wide), pl.ds(wide, columns - wide)
+            r2[m, z, :, left] = added(r2[m, z, :, left], r3a[m, at.y, z]).astype(r2.dtype)
+            r2[m, z, :, right] = added(r2[m, z, :, right], r3b[m, z, at.x]).astype(r2.dtype)
+            return carry
+
+        lax.fori_loop(0, at.nz, add, 0)
+        for k in range(1, at.nz):
+            self.last(m, k).start()
+
+    def step4(self, m, out):
+        at = self.at
+        for k in range(1, at.nz):
+            self.last(m, k).wait_recv()
+        out[m] = added(self.r2[m, at.z], *[self.rz[m, k] for k in range(at.nz - 1)])
+
+    def drain(self, m):
+        self.to_sibling(m, self.rc.at[m]).wait_send()
+        self.first_a(m).wait_send()
+        self.first_b(m).wait_send()
+        self.second_a(m).wait_send()
+        self.second_b(m).wait_send()
+        for k in range(1, self.at.nz):
+            self.last(m, k).wait_send()
+
+
+class SmallSum:
+    def __init__(self, at, total, landing, send, recv):
+        self.at, self.total, self.landing, self.send, self.recv = at, total, landing, send, recv
+
+    def hop(self, i, to):
+        return remote(self.total.at[i], self.landing.at[i], self.send.at[i], self.recv.at[i], to)
+
+    def along(self, k):
+        i = 2 + k
+        return remote(self.total.at[3], self.landing.at[i], self.send.at[i], self.recv.at[i], self.at.along_z[k - 1])
+
+    def start(self):
+        self.hop(0, self.at.sibling).start()
+
+    def step(self, i):
+        at = self.at
+        to = (at.sibling, at.across_x, at.across_y)
+        self.hop(i, to[i]).wait_recv()
+        self.total[i + 1] = self.total[i] + self.landing[i]
+        if i < 2:
+            self.hop(i + 1, to[i + 1]).start()
+        else:
+            for k in range(1, at.nz):
+                self.along(k).start()
+
+    def finish(self, out):
+        at = self.at
+        for k in range(1, at.nz):
+            self.along(k).wait_recv()
+        total = self.total[3]
+        for k in range(1, at.nz):
+            total = total + self.landing[2 + k]
+        out[...] = total
+        to = (at.sibling, at.across_x, at.across_y)
+        for i in range(3):
+            self.hop(i, to[i]).wait_send()
+        for k in range(1, at.nz):
+            self.along(k).wait_send()
+
+
+def scatter_kernel(nz, nx, wide, count, terms, small, out, small_out, own, rc, r3a, r3b, r2, rz, send, recv, total, landing, ssend, srecv, osem):
+    at = Partners(nz, nx)
+    at.meet()
+    scatter = Scatter(at, wide, rc, r3a, r3b, r2, rz, send, recv)
+    sums = SmallSum(at, total, landing, ssend, srecv)
+    total[0] = small[...]
+    sums.start()
+
+    def fetch(m):
+        slot = lax.rem(m, 2)
+        return pltpu.make_async_copy(terms.at[m, :, at.core], own.at[slot], osem.at[slot])
+
+    def tick(i, carry):
+        @pl.when(i < count)
+        def _():
+            fetch(i).start()
+            scatter.start(i, terms.at[i, :, 1 - at.core])
+
+        @pl.when((i >= 1) & (i < count + 1))
+        def _():
+            m = i - 1
+            fetch(m).wait()
+            slot = lax.rem(m, 2)
+            scatter.step1(m, lambda y, z: own[slot, y, z])
+
+        @pl.when((i >= 2) & (i < count + 2))
+        def _():
+            scatter.step2(i - 2)
+
+        @pl.when((i >= 3) & (i < count + 3))
+        def _():
+            scatter.step3(i - 3)
+
+        @pl.when(i >= 4)
+        def _():
+            scatter.step4(i - 4, out)
+
+        return carry
+
+    lax.fori_loop(0, 4, tick, 0)
+    for i in range(3):
+        sums.step(i)
+    lax.fori_loop(4, count + 4, tick, 0)
+    sums.finish(small_out)
+
+    def drain(m, carry):
+        scatter.drain(m)
+        return carry
+
+    lax.fori_loop(0, count, drain, 0)
+
+
+def scatter_scratch(count, nz, nx, rows, columns, wide):
+    bf16 = jnp.bfloat16
+    return [
+        pltpu.VMEM((count, 2, nz, nx, rows, columns), bf16),
+        pltpu.VMEM((count, 2, nz, rows, wide), bf16),
+        pltpu.VMEM((count, nz, nx, rows, columns - wide), bf16),
+        pltpu.VMEM((count, nz, rows, columns), bf16),
+        pltpu.VMEM((count, nz - 1, rows, columns), bf16),
+        pltpu.SemaphoreType.DMA((count, 4 + nz)),
+        pltpu.SemaphoreType.DMA((count, 4 + nz)),
+    ]
+
+
+def small_scratch(nz, shape):
+    return [
+        pltpu.VMEM((4, *shape), jnp.float32),
+        pltpu.VMEM((2 + nz, *shape), jnp.float32),
+        pltpu.SemaphoreType.DMA((2 + nz,)),
+        pltpu.SemaphoreType.DMA((2 + nz,)),
+    ]
+
+
+def scatter_terms(terms, small, nz, nx):
+    count, _, _, _, _, rows, columns = terms.shape
+    wide = columns * 3 // 4
+    vmem = pl.BlockSpec(memory_space=pltpu.VMEM)
+    return pl.pallas_call(
+        partial(scatter_kernel, nz, nx, wide, count),
+        out_shape=[
+            jax.ShapeDtypeStruct((count, rows, columns), jnp.float32),
+            jax.ShapeDtypeStruct(small.shape, jnp.float32),
+        ],
+        in_specs=[pl.BlockSpec(memory_space=pl.ANY), vmem],
+        out_specs=[vmem, vmem],
+        scratch_shapes=[
+            pltpu.VMEM((2, 2, nz, nx, rows, columns), jnp.bfloat16),
+            *scatter_scratch(count, nz, nx, rows, columns, wide),
+            *small_scratch(nz, small.shape),
+            pltpu.SemaphoreType.DMA((2,)),
+        ],
+        compiler_params=pltpu.CompilerParams(
+            collective_id=2, has_side_effects=True, vmem_limit_bytes=56 * 2**20
+        ),
+    )(terms, small)
 
 
 def norm_forward(hidden, gain, shift):
@@ -205,10 +491,22 @@
     live_rows = lax.broadcasted_iota(jnp.int32, (row_count,), 0) < live_count[0]
     input_grad = jnp.where(live_rows[:, None, None], input_full, 0.0)
     devices = packed_full.shape[0]
-    small_terms = jnp.concatenate(
-        [
-            v.reshape(devices, -1, small_rows)
-            for v in (
+    if small_rows % 16 == 0 and lax.axis_size("dp") == 4:
+        nx = 2
+        nz = lax.axis_size("fsdp") // nx
+        terms = [
+            query_wgrad,
+            key_wgrad,
+            value_wgrad,
+            output_grad,
+            *(up_grad[:, j * feature_count : (j + 1) * feature_count] for j in range(4)),
+            *(down_grad.reshape(devices, 4, -1, feature_count)[:, j] for j in range(4)),
+        ]
+        terms = jnp.stack(
+            [t.astype(jnp.bfloat16).reshape(2, 2, nz, nx, small_rows, feature_count) for t in terms]
+        )
+        small = jnp.stack(
+            [
                 query_bias_grad,
                 value_bias_grad,
                 output_bias_grad,
@@ -217,18 +515,42 @@
                 down_bias_grad,
                 gain2_grad,
                 shift2_grad,
-                up_bias_grad,
-            )
-        ],
-        axis=1,
-    )
-    small_sum = lax.psum_scatter(small_terms, ("dp", "fsdp"), scatter_dimension=0, tiled=True)[0]
-    down_sum, up_sum, output_sum, value_sum, query_sum, key_sum = (
-        lax.psum_scatter(
-            term.astype(jnp.bfloat16), ("dp", "fsdp"), scatter_dimension=0, tiled=True
-        ).astype(jnp.float32)
-        for term in (down_grad, up_grad, output_grad, value_wgrad, query_wgrad, key_wgrad)
-    )
+                *up_bias_grad.reshape(devices, 4, small_rows).transpose(1, 0, 2).reshape(4, -1),
+                *([jnp.zeros_like(gain1_grad)] * 4),
+            ]
+        )
+        wsum, small_sum = scatter_terms(terms, small, nz, nx)
+        me = lax.axis_index(("dp", "fsdp"))
+        small_sum = lax.dynamic_slice(small_sum, (0, me * small_rows), (16, small_rows))
+        query_sum, key_sum, value_sum, output_sum = (wsum[i] for i in range(4))
+        up_sum = wsum[4:8].transpose(1, 0, 2).reshape(small_rows, -1)
+        down_sum = wsum[8:12].reshape(-1, feature_count)
+        small_sum = small_sum[:12]
+    else:
+        small_terms = jnp.concatenate(
+            [
+                v.reshape(devices, -1, small_rows)
+                for v in (
+                    query_bias_grad,
+                    value_bias_grad,
+                    output_bias_grad,
+                    gain1_grad,
+                    shift1_grad,
+                    down_bias_grad,
+                    gain2_grad,
+                    shift2_grad,
+                    up_bias_grad,
+                )
+            ],
+            axis=1,
+        )
+        small_sum = lax.psum_scatter(small_terms, ("dp", "fsdp"), scatter_dimension=0, tiled=True)[0]
+        down_sum, up_sum, output_sum, value_sum, query_sum, key_sum = (
+            lax.psum_scatter(
+                term.astype(jnp.bfloat16), ("dp", "fsdp"), scatter_dimension=0, tiled=True
+            ).astype(jnp.float32)
+            for term in (down_grad, up_grad, output_grad, value_wgrad, query_wgrad, key_wgrad)
+        )
     return (
         slot_acts,
         input_grad,

time: 1620 us -> 834 us (0.51)
  waiting for transfers between devices: 1130 us -> 194 us
  Pallas kernels: 0 us -> 145 us
    reduce_scatter x4 -> x0, waiting for transfers between devices: 534 us -> none  [the longest x3 491 us: on_device(): lax.psum_scatter(term.astype(jnp.bfloat16), ('dp', 'fsdp'), scatter_dimen...]
    unnamed x18 -> x8, waiting for transfers between devices: 407 us -> 3.67 us
    pallas_call x0 -> x1, Pallas kernels: none -> 145 us  [scatter_terms(): pl.pallas_call(partial(scatter_kernel, nz, nx, wide, count), out_shape=[j...]
  transfers between devices with their start and end apart: 15 -> 8, of which waited for: 12 -> 5; matrix products, arithmetic and copies ran while one was open for 17% -> 30% of each run, Pallas kernels for 0% -> 18%
where the time goes in v2:
time: 834 us; the launch traced here: 826 us
  matrix products  237 us (28%)
  waiting for transfers between devices  194 us (23%)
  Pallas kernels  145 us (17%)
  other arithmetic  86.5 us (10%)
  local copies, waits for them, and re-layouts  74 us (9%)
  blocking collectives  71.7 us (9%)
  between operations  17.3 us (2%)
    all_gather x6, waiting for transfers between devices, on_device(): lax.all_gather(weight, ('dp', 'fsdp'), axis=0, tiled=True)  190 us
    pallas_call x1, Pallas kernels, scatter_terms(): pl.pallas_call(partial(scatter_kernel, nz, nx, wide, count), out_shape=[j...  145 us
    all_gather x1, blocking collectives, on_device(): packed_full = lax.all_gather(packed, ('dp', 'fsdp'), axis=0)  71.7 us
    dot_general x6, matrix products, apply_back(): jnp.einsum('rse,de->rsd', grads, weight, preferred_element_type=jnp.float32)  60.8 us
    dot_general x6, matrix products, apply_weight(): jnp.einsum('rsd,de->rse', acts, weight, preferred_element_type=jnp.float32)  56.3 us
    convert_element_type x1, other arithmetic, on_device(): act_low = jax.nn.gelu(pre_act, approximate=False).astype(jnp.bfloat16)  38.6 us
    dot_general x6, matrix products, weight_term(): jnp.einsum('rsd,rse->de', acts, grads, preferred_element_type=jnp.float32)  37.2 us
    unnamed x109, local copies, waits for them, and re-layouts  28.8 us
  transfers between devices with their start and end apart: 8, of which 5 were waited for; matrix products, arithmetic and copies ran while one was open for 30% of the time, Pallas kernels for 18%

profile of v2, /device:TPU:0, one launch (start us, length us, event | category | flops | bytes accessed | tf_op | source)
XLA Modules:
  0.0 826.3 jit_solution(4100655951788669072)
XLA Ops:
  12.0 8.3 %fusion.26 = bf16[12,320,1024]{2,0,1:T(8,128)(2,1)} fusion(bf16[6,320,1024]{2,1,0:T(8,128)(2,1)} %param.22, s32[6]{0:T(128)} %param.20), kind=kOutput, calls=%fused_computation.52 | convolution fusion | flops 47185992 | bytes 11796504 | tf_op jit(solution)/shard_map/az,zfy->afy/dot_general | solution.py:367
  20.3 11.6 %copy.128 = bf16[12,320,1024]{2,1,0:T(8,128)(2,1)} copy(bf16[12,320,1024]{2,0,1:T(8,128)(2,1)} %fusion.26) | data formatting | bytes 15728640 | tf_op jit(solution)/shard_map/az,zfy->afy/dot_general | solution.py:367
  33.3 71.7 %all-gather.1 = bf16[32,12,32]{2,1,0:T(8,128)(2,1)S(1)} all-gather(bf16[1,12,32]{2,1,0:T(8,128)(2,1)S(1)} %bitcast.233), channel_id=2, replica_groups=mesh['dp'=4,'fsdp'=8] {'dp','fsdp'}, dimensions={0}, use_global_device_ids=true | all-gather | bytes 25344 | tf_op jit(solution)/shard_map/all_gather | solution.py:380
  115.2 34.8 %all-gather.12.cloned.1.call-done = bf16[1024,1024]{1,0:T(8,128)(2,1)} async-done(((bf16[32,1024]{1,0:T(8,128)(2,1)}), bf16[1024,1024]{1,0:T(8,128)(2,1)}) %all-gather.12.cloned.1.call-update) | async-done | bytes 2097168 | tf_op jit(solution)/shard_map/all_gather | solution.py:393
  158.5 50.3 %all-gather.14.cloned.1.call-done = bf16[1024,1024]{1,0:T(8,128)(2,1)} async-done(((bf16[32,1024]{1,0:T(8,128)(2,1)}), bf16[1024,1024]{1,0:T(8,128)(2,1)}) %all-gather.14.cloned.1.call-update) | async-done | bytes 2097168 | tf_op jit(solution)/shard_map/all_gather | solution.py:393
  218.6 12.8 %multiply_reduce_fusion.1 = (f32[3,16,320]{2,1,0:T(8,128)S(1)}, f32[3,16,320,320]{2,3,1,0:T(8,128)}) fusion(bf16[3,320,16,64]{1,3,2,0:T(8,128)(2,1)S(1)} %bitcast.197, bf16[3,320,16,64]{1,3,2,0:T(8,128)(2,1)} %bitcast.201), kind=kOutput, calls=%fused_computation.8 | convolution fusion | flops 638960640 | bytes 23654400 | tf_op jit(solution)/shard_map/rqhd,rkhd->rhqk/dot_general | solution.py:408
  231.3 10.3 %fusion = f32[3,16,320]{2,1,0:T(8,128)S(1)} fusion(f32[3,16,320,320]{2,3,1,0:T(8,128)} %get-tuple-element.76, f32[3,16,320]{2,1,0:T(8,128)S(1)} %get-tuple-element.75), kind=kLoop, calls=%fused_computation.7 | loop fusion | flops 14730240 | bytes 19783680 | tf_op jit(solution)/shard_map/reduce_sum | solution.py:413
  241.7 11.8 %fusion.56 = bf16[3,16,64,320]{3,2,1,0:T(8,128)(2,1)} fusion(bf16[3,320,16,64]{1,3,2,0:T(8,128)(2,1)S(1)} %bitcast.204, f32[3,16,320,320]{2,3,1,0:T(8,128)} %get-tuple-element.76, f32[3,16,320]{2,1,0:T(8,128)S(1)} %fusion, f32[3,16,320]{2,1,0:T(8,128)S(1)} %get-tuple-element.75), kind=kOutput, calls=%fused_computation.104 | convolution fusion | flops 649789440 | bytes 23715840 | tf_op jit(solution)/shard_map/rhqk,rkhd->rqhd/dot_general | solution.py:416
  253.5 14.0 %all-gather.16.cloned.1.call-done = bf16[1024,1024]{1,0:T(8,128)(2,1)} async-done(((bf16[32,1024]{1,0:T(8,128)(2,1)}), bf16[1024,1024]{1,0:T(8,128)(2,1)}) %all-gather.16.cloned.1.call-update) | async-done | bytes 2097168 | tf_op jit(solution)/shard_map/all_gather | solution.py:393
  275.1 72.0 %all-gather.18.cloned.1.call-done = bf16[1024,4096]{1,0:T(8,128)(2,1)} async-done(((bf16[32,4096]{1,0:T(8,128)(2,1)}), bf16[1024,4096]{1,0:T(8,128)(2,1)}) %all-gather.18.cloned.1.call-update) | async-done | bytes 8388624 | tf_op jit(solution)/shard_map/all_gather | solution.py:393
  347.1 21.3 %fusion.33 = (u8[320,4096]{1,0:T(8,128)(4,1)S(1)}, u8[320,4096]{1,0:T(8,128)(4,1)S(1)}, f32[3,320,4096]{2,1,0:T(8,128)}) fusion(f32[4096]{0:T(1024)S(1)} %reshape.307, bf16[1024,4096]{1,0:T(8,128)(2,1)} %all-gather.18.cloned.1.call-done, f32[3,320,1024]{2,1,0:T(8,128)} %copy-done.5, f32[1024]{0:T(1024)S(1)} %reshape.306, f32[1024]{0:T(1024)S(1)} %reshape.305, ...), kind=kOutput, calls=%fused_computation.82 | convolution fusion | flops 8110407680 | bytes 30703104 | tf_op jit(solution)/shard_map/rsd,de->rse/dot_general | solution.py:322
  368.3 38.6 %multiply_convert_fusion.1 = (bf16[3,320,4096]{2,1,0:T(8,128)(2,1)}, f32[3,320,4096]{2,1,0:T(8,128)}) fusion(f32[3,320,4096]{2,1,0:T(8,128)} %get-tuple-element.79, f32[4096]{0:T(1024)S(1)} %reshape.307, u8[320,4096]{1,0:T(8,128)(4,1)S(1)} %get-tuple-element.22, u8[320,4096]{1,0:T(8,128)(4,1)S(1)} %get-tuple-element.21), kind=kLoop, calls=%fused_computation.20 | loop fusion | flops 279183360 | bytes 41959424 | tf_op jit(solution)/shard_map/convert_element_type | solution.py:425
  406.9 19.3 %all-gather.20.cloned.1.call-done = bf16[4096,1024]{1,0:T(8,128)(2,1)} async-done(((bf16[128,1024]{1,0:T(8,128)(2,1)}), bf16[4096,1024]{1,0:T(8,128)(2,1)}) %all-gather.20.cloned.1.call-update) | async-done | bytes 8388624 | tf_op jit(solution)/shard_map/all_gather | solution.py:393
  426.2 14.3 %fusion.98 = (f32[3,320]{1,0:T(4,128)S(1)}, f32[3,320,1024]{2,1,0:T(8,128)S(1)}) fusion(f32[1024]{0:T(1024)S(1)} %reshape.308, bf16[3,320,4096]{2,1,0:T(8,128)(2,1)} %get-tuple-element.49, bf16[4096,1024]{1,0:T(8,128)(2,1)} %all-gather.20.cloned.1.call-done, f32[1024]{0:T(1024)S(1)} %reshape.306, f32[1024]{0:T(1024)S(1)} %reshape.305, ...), kind=kOutput, calls=%fused_computation.179 | convolution fusion | flops 8059943936 | bytes 24141056 | tf_op jit(solution)/shard_map/rsd,de->rse/dot_general | solution.py:322
  451.1 24.2 %convert_reduce_fusion = (f32[4096]{0:T(1024)S(1)}, bf16[3,320,4096]{2,1,0:T(8,128)(2,1)}) fusion(f32[3,320,4096]{2,1,0:T(8,128)} %get-tuple-element.50, bf16[3,320,1024]{2,1,0:T(8,128)(2,1)} %get-tuple-element.44, bf16[4096,1024]{1,0:T(8,128)(2,1)} %all-gather.20.cloned.1.call-done, f32[3,320,4096]{2,1,0:T(8,128)} %get-tuple-element.79, f32[4096]{0:T(1024)S(1)} %reshape.307), kind=kOutput, calls=%fused_computation.18 | convolution fusion | flops 8119906304 | bytes 49709056 | tf_op jit(solution)/shard_map/rse,de->rsd/dot_general | solution.py:326
  475.3 16.7 %multiply_reduce_fusion.2 = (f32[1024]{0:T(1024)S(1)}, f32[3,320]{1,0:T(4,128)S(1)}, f32[3,320]{1,0:T(4,128)S(1)}, f32[1024]{0:T(1024)S(1)}, f32[3,320,1024]{2,1,0:T(8,128)S(1)}) fusion(f32[3,320,1024]{2,1,0:T(8,128)} %copy-done.5, f32[3,320]{1,0:T(4,128)S(1)} %add_rsqrt_fusion.1, f32[3,320]{1,0:T(4,128)S(1)} %broadcast_multiply_fusion.5, ...), kind=kOutput, calls=%fused_computation.67 | convolution fusion | flops 8070754304 | bytes 30062592 | tf_op jit(solution)/shard_map/rse,de->rsd/dot_general | solution.py:326
  501.7 11.2 %convert_reduce_fusion.2 = (f32[16,64]{1,0:T(8,128)S(1)}, bf16[3,16,64,320]{3,2,1,0:T(8,128)(2,1)}) fusion(bf16[3,320,16,64]{1,3,2,0:T(8,128)(2,1)S(1)} %bitcast.199, f32[3,16,320,320]{2,3,1,0:T(8,128)} %get-tuple-element.76, f32[3,16,320]{2,1,0:T(8,128)S(1)} %log_add_fusion), kind=kOutput, calls=%fused_computation.54 | convolution fusion | flops 646839296 | bytes 23658496 | tf_op jit(solution)/shard_map/rhqk,rqhd->rkhd/dot_general | solution.py:460
  512.9 20.9 %multiply_reduce_fusion = (f32[3,16,320]{2,1,0:T(8,128)S(1)}, f32[3,16,320,320]{2,3,1,0:T(8,128)}) fusion(f32[3,16,320,320]{2,3,1,0:T(8,128)} %get-tuple-element.76, f32[3,16,320]{2,1,0:T(8,128)S(1)} %log_add_fusion, bf16[3,320,16,64]{1,3,2,0:T(8,128)(2,1)S(1)} %bitcast.200, bf16[3,320,16,64]{1,3,2,0:T(8,128)(2,1)} %bitcast.203), kind=kOutput, calls=%fused_computation.2 | convolution fusion | flops 648791040 | bytes 43376640 | tf_op jit(solution)/shard_map/rqhd,rkhd->rhqk/dot_general | solution.py:464
  533.8 20.6 %multiply_convert_fusion = bf16[3,16,320,320]{2,3,1,0:T(8,128)(2,1)} fusion(f32[3,16,320,320]{2,3,1,0:T(8,128)} %get-tuple-element.84, f32[3,16,320,320]{2,3,1,0:T(8,128)} %get-tuple-element.76, f32[3,16,320]{2,1,0:T(8,128)S(1)} %get-tuple-element.83, f32[3,16,320]{2,1,0:T(8,128)S(1)} %log_add_fusion), kind=kLoop, calls=%fused_computation.1 | loop fusion | flops 24576000 | bytes 49274880 | tf_op jit(solution)/shard_map/convert_element_type | solution.py:467
  554.4 9.7 %multiply_convert_fusion.2 = bf16[3,16,64,320]{3,2,1,0:T(8,128)(2,1)} fusion(bf16[3,320,16,64]{1,3,2,0:T(8,128)(2,1)S(1)} %bitcast.198, bf16[3,16,320,320]{2,3,1,0:T(8,128)(2,1)} %multiply_convert_fusion), kind=kOutput, calls=%fused_computation.56 | convolution fusion | flops 631111680 | bytes 13762560 | tf_op jit(solution)/shard_map/rhqk,rqhd->rkhd/dot_general | solution.py:476
  564.1 8.1 convert_reduce_fusion.3
  601.2 10.8 %bitcast_convert_fusion.1 = bf16[1024,4096]{1,0:T(8,128)(2,1)S(1)} fusion(bf16[3,320,4096]{2,1,0:T(8,128)(2,1)S(1)} %bitcast.247, f32[3,320,1024]{2,1,0:T(8,128)S(1)} %copy-done.7, f32[1024]{0:T(1024)S(1)} %reshape.306, f32[1024]{0:T(1024)S(1)} %reshape.305, f32[3,320]{1,0:T(4,128)S(1)} %add_rsqrt_fusion.1, f32[3,320]{1,0:T(4,128)S(1)} %broadcast_multiply_fusion.5), kind=kOutput, calls=%fused_computation.10 | convolution fusion | flops 8062173184 | bytes 20200960 | tf_op jit(solution)/shard_map/rsd,rse->de/dot_general | solution.py:330
  619.5 9.8 %bitcast_convert_fusion = bf16[4096,1024]{1,0:T(8,128)(2,1)S(1)} fusion(bf16[3,320,4096]{2,1,0:T(8,128)(2,1)S(1)} %bitcast.215, bf16[3,320,1024]{2,1,0:T(8,128)(2,1)S(1)} %copy-done.20), kind=kOutput, calls=%fused_computation.9 | convolution fusion | flops 8057257984 | bytes 18219008 | tf_op jit(solution)/shard_map/rsd,rse->de/dot_general | solution.py:330
  636.8 145.2 %shard_map.314 = (f32[12,32,1024]{2,1,0:T(8,128)}, f32[16,1024]{1,0:T(8,128)}) custom-call(bf16[12,2,2,4,2,32,1024]{6,5,4,3,2,1,0:T(8,128)(2,1)} %constant_dynamic-update-slice_fusion.terms, f32[16,1024]{1,0:T(8,128)} %stack.43.small), custom_call_target="tpu_custom_call" | custom-call | tf_op jit(solution)/shard_map/pallas_call | solution.py:280
  (196 shorter events, 140.8 us)
Async XLA Ops:
  8.0 99.8 %all-gather.10.cloned.1.call-start = ((), (), s32[]{:S(2)}) async-start(), calls=%async_computation.1 | async-start | bytes 2162688 | tf_op jit(solution)/shard_map/all_gather | solution.py:393
  8.8 141.2 %all-gather.12.cloned.1.call-start = ((), (), s32[]{:S(2)}) async-start(), calls=%async_computation.2 | async-start | bytes 2162688 | tf_op jit(solution)/shard_map/all_gather | solution.py:393
  9.5 199.3 %all-gather.14.cloned.1.call-start = ((), (), s32[]{:S(2)}) async-start(), calls=%async_computation.3 | async-start | bytes 2162688 | tf_op jit(solution)/shard_map/all_gather | solution.py:393
  10.2 257.2 %all-gather.16.cloned.1.call-start = ((), (), s32[]{:S(2)}) async-start(), calls=%async_computation.4 | async-start | bytes 2162688 | tf_op jit(solution)/shard_map/all_gather | solution.py:393
  10.8 336.2 %all-gather.18.cloned.1.call-start = ((), (), s32[]{:S(2)}) async-start(), calls=%async_computation.5 | async-start | bytes 8650752 | tf_op jit(solution)/shard_map/all_gather | solution.py:393
  11.4 414.8 %all-gather.20.cloned.1.call-start = ((), (), s32[]{:S(2)}) async-start(), calls=%async_computation.6 | async-start | bytes 8650752 | tf_op jit(solution)/shard_map/all_gather | solution.py:393
  12.0 431.1 %reduce-scatter.2.cloned.1.call-start = ((), (), s32[]{:S(2)}) async-start(), calls=%async_computation.8 | async-start | bytes 9830400 | tf_op jit(solution)/shard_map/reduce_scatter | solution.py:366
  32.0 775.7 %all-gather.22.cloned.1.call-start = ((), (), s32[]{:S(2)}) async-start(), calls=%async_computation.7 | async-start | bytes 9830400 | tf_op jit(solution)/shard_map/all_gather | solution.py:430
  158.5 60.0 %copy-start.2 = (bf16[3,320,1024]{1,2,0:T(8,128)(2,1)}, bf16[3,320,1024]{1,2,0:T(8,128)(2,1)S(1)}, u32[]{:S(2)}) copy-start(bf16[3,320,1024]{1,2,0:T(8,128)(2,1)S(1)} %copy.86) | copy-start | bytes 5898244
  231.3 10.3 %copy-start.9 = (bf16[3,320,1024]{1,2,0:T(8,128)(2,1)S(1)}, bf16[3,320,1024]{1,2,0:T(8,128)(2,1)}, u32[]{:S(2)}) copy-start(bf16[3,320,1024]{1,2,0:T(8,128)(2,1)} %copy.85) | copy-start | bytes 5898244
  241.7 25.8 %copy-start.39 = (bf16[3,320,1024]{2,1,0:T(8,128)(2,1)S(1)}, bf16[3,320,1024]{2,1,0:T(8,128)(2,1)}, u32[]{:S(2)}) copy-start(bf16[3,320,1024]{2,1,0:T(8,128)(2,1)} %param.19) | copy-start | bytes 5898244
  475.3 16.7 %copy-start.6 = (f32[3,320,1024]{2,1,0:T(8,128)S(1)}, f32[3,320,1024]{2,1,0:T(8,128)}, u32[]{:S(2)}) copy-start(f32[3,320,1024]{2,1,0:T(8,128)} %copy-done.5) | copy-start | bytes 11796484
  533.8 20.6 %copy-start.3 = (bf16[3,320,1024]{1,2,0:T(8,128)(2,1)S(1)}, bf16[3,320,1024]{1,2,0:T(8,128)(2,1)}, u32[]{:S(2)}) copy-start(bf16[3,320,1024]{1,2,0:T(8,128)(2,1)} %copy-done.2) | copy-start | bytes 5898244
  554.4 9.7 %copy-start.4 = (bf16[3,320,1024]{1,2,0:T(8,128)(2,1)S(1)}, bf16[3,320,1024]{1,2,0:T(8,128)(2,1)}, u32[]{:S(2)}) copy-start(bf16[3,320,1024]{1,2,0:T(8,128)(2,1)} %copy.87) | copy-start | bytes 5898244
  572.4 6.7 copy-start.11
  572.4 6.7 copy-start.40
  593.5 6.3 slice-start.2
  612.0 7.5 slice-start
  613.0 6.5 slice-start.1
  783.4 6.6 copy-start.16
  794.6 6.0 copy-start.36
  794.6 6.0 copy-start.44
  807.7 6.2 copy-start.26
  807.7 6.2 copy-start.27
  (33 other events, 95.0 us)
Sparse Core Ops, SparseCore 0:
  12.3 59.5 all-gather.9
  75.3 74.6 all-gather.11
  153.4 55.3 all-gather.13
  212.1 55.3 all-gather.15
  270.7 76.2 all-gather.17
  350.3 75.8 all-gather.19
Sparse Core Ops, SparseCore 1:
  32.1 74.9 reduce-scatter.1
  572.3 53.7 all-gather.21

commit v3 on v2

--- a/solution.py
+++ b/solution.py
@@ -1,3 +1,4 @@
+import math
 from functools import partial
 
 import jax
@@ -108,6 +109,7 @@
             return carry
 
         lax.fori_loop(0, rc.shape[1] * nz, add, 0)
+        self.to_sibling(m, rc.at[m]).wait_send()
         self.first_a(m).start()
         self.first_b(m).start()
 
@@ -150,7 +152,6 @@
         out[m] = added(self.r2[m, at.z], *[self.rz[m, k] for k in range(at.nz - 1)])
 
     def drain(self, m):
-        self.to_sibling(m, self.rc.at[m]).wait_send()
         self.first_a(m).wait_send()
         self.first_b(m).wait_send()
         self.second_a(m).wait_send()
@@ -199,58 +200,6 @@
             self.along(k).wait_send()
 
 
-def scatter_kernel(nz, nx, wide, count, terms, small, out, small_out, own, rc, r3a, r3b, r2, rz, send, recv, total, landing, ssend, srecv, osem):
-    at = Partners(nz, nx)
-    at.meet()
-    scatter = Scatter(at, wide, rc, r3a, r3b, r2, rz, send, recv)
-    sums = SmallSum(at, total, landing, ssend, srecv)
-    total[0] = small[...]
-    sums.start()
-
-    def fetch(m):
-        slot = lax.rem(m, 2)
-        return pltpu.make_async_copy(terms.at[m, :, at.core], own.at[slot], osem.at[slot])
-
-    def tick(i, carry):
-        @pl.when(i < count)
-        def _():
-            fetch(i).start()
-            scatter.start(i, terms.at[i, :, 1 - at.core])
-
-        @pl.when((i >= 1) & (i < count + 1))
-        def _():
-            m = i - 1
-            fetch(m).wait()
-            slot = lax.rem(m, 2)
-            scatter.step1(m, lambda y, z: own[slot, y, z])
-
-        @pl.when((i >= 2) & (i < count + 2))
-        def _():
-            scatter.step2(i - 2)
-
-        @pl.when((i >= 3) & (i < count + 3))
-        def _():
-            scatter.step3(i - 3)
-
-        @pl.when(i >= 4)
-        def _():
-            scatter.step4(i - 4, out)
-
-        return carry
-
-    lax.fori_loop(0, 4, tick, 0)
-    for i in range(3):
-        sums.step(i)
-    lax.fori_loop(4, count + 4, tick, 0)
-    sums.finish(small_out)
-
-    def drain(m, carry):
-        scatter.drain(m)
-        return carry
-
-    lax.fori_loop(0, count, drain, 0)
-
-
 def scatter_scratch(count, nz, nx, rows, columns, wide):
     bf16 = jnp.bfloat16
     return [
@@ -273,28 +222,821 @@
     ]
 
 
-def scatter_terms(terms, small, nz, nx):
-    count, _, _, _, _, rows, columns = terms.shape
-    wide = columns * 3 // 4
-    vmem = pl.BlockSpec(memory_space=pltpu.VMEM)
+def exact_gelu(pre):
+    half = 0.5 + 0.5 * lax.erf(pre * (0.5**0.5))
+    bell = jnp.exp(-0.5 * pre * pre) * ((0.5 / math.pi) ** 0.5)
+    return pre * half, half + pre * bell
+
+
+def rms_center(hidden):
+    center = hidden - jnp.mean(hidden, axis=-1, keepdims=True)
+    inverse = lax.rsqrt(jnp.mean(center * center, axis=-1, keepdims=True) + EPSILON)
+    return center * inverse, inverse
+
+
+def half_masks(width):
+    left = (lax.broadcasted_iota(jnp.int32, (1, width), 1) < width // 2).astype(jnp.float32)
+    return left.astype(jnp.bfloat16), (1.0 - left).astype(jnp.bfloat16)
+
+
+def across(left, right):
+    return lax.dot_general(left, right, (((1,), (1,)), ((), ())), preferred_element_type=jnp.float32)
+
+
+def down(left, right):
+    return lax.dot_general(left, right, (((0,), (0,)), ((), ())), preferred_element_type=jnp.float32)
+
+
+def dot(left, right):
+    return jnp.dot(left, right, preferred_element_type=jnp.float32)
+
+
+def span(i, size):
+    return pl.ds(pl.multiple_of(i * size, size), size)
+
+
+class Gather:
+    def __init__(self, at, wide, count, shards, g, send, recv):
+        self.at, self.wide, self.count, self.shards, self.g, self.send, self.recv = at, wide, count, shards, g, send, recv
+        self.right = g.shape[-1] - wide
+
+    def along(self, m, k):
+        at = self.at
+        dst = self.g.at[m, at.y, at.core, at.z, at.x]
+        return remote(self.shards.at[m], dst, self.send.at[m, k - 1], self.recv.at[m, k - 1], at.along_z[k - 1])
+
+    def same(self, part, m, i, to):
+        return remote(part, part, self.send.at[m, i], self.recv.at[m, i], to)
+
+    def first_a(self, m):
+        at, nz = self.at, self.at.nz
+        part = self.g.at[m, at.y, at.core, :, at.x, :, pl.ds(0, self.wide)]
+        return self.same(part, m, nz - 1, at.across_y)
+
+    def first_b(self, m):
+        at, nz = self.at, self.at.nz
+        part = self.g.at[m, at.y, at.core, :, at.x, :, pl.ds(self.wide, self.right)]
+        return self.same(part, m, nz, at.across_x)
+
+    def second_a(self, m):
+        at, nz = self.at, self.at.nz
+        part = self.g.at[m, :, at.core, :, at.x, :, pl.ds(0, self.wide)]
+        return self.same(part, m, nz + 1, at.across_x)
+
+    def second_b(self, m):
+        at, nz = self.at, self.at.nz
+        part = self.g.at[m, at.y, at.core, :, :, :, pl.ds(self.wide, self.right)]
+        return self.same(part, m, nz + 2, at.across_y)
+
+    def to_sibling(self, m):
+        at, nz = self.at, self.at.nz
+        return self.same(self.g.at[m, :, at.core], m, nz + 3, at.sibling)
+
+    def step0(self, m):
+        at = self.at
+        for k in range(1, at.nz):
+            self.along(m, k).start()
+        self.g[m, at.y, at.core, at.z, at.x] = self.shards[m]
+
+    def step1(self, m):
+        for k in range(1, self.at.nz):
+            self.along(m, k).wait_recv()
+        self.first_a(m).start()
+        self.first_b(m).start()
+
+    def step2(self, m):
+        self.first_a(m).wait_recv()
+        self.first_b(m).wait_recv()
+        self.second_a(m).start()
+        self.second_b(m).start()
+
+    def step3(self, m):
+        self.second_a(m).wait_recv()
+        self.second_b(m).wait_recv()
+        self.to_sibling(m).start()
+
+    def arrive(self, m):
+        self.to_sibling(m).wait_recv()
+
+    def tick(self, i):
+        for step, ahead in ((self.step3, 3), (self.step2, 2), (self.step1, 1), (self.step0, -2)):
+            m = i - ahead
+            if isinstance(i, int):
+                if 0 <= m < self.count:
+                    step(m)
+            else:
+                pl.when((m >= 0) & (m < self.count))(partial(step, m))
+
+    def drain(self, m):
+        for k in range(1, self.at.nz):
+            self.along(m, k).wait_send()
+        for copy in (self.first_a, self.first_b, self.second_a, self.second_b, self.to_sibling):
+            copy(m).wait_send()
+
+
+def forward_kernel(
+    nz, nx, wide, tokens, head_pair,
+    x, shards, small, pick, slots,
+    g_out, saved, act_out, slope_out, unit_out, final_out, own_out, across_out, small_full, inverse1, inverse2,
+    g, pool, hidden, landed, total, landing,
+    send, recv, ssend, srecv, usend, urecv, isem, gsem, vsem, asem, dsem, fsem,
+):
+    f32, bf16 = jnp.float32, jnp.bfloat16
+    count = g.shape[0]
+    all_rows, width = x.shape
+    rows = all_rows // tokens
+    at = Partners(nz, nx)
+    at.meet()
+    gather = Gather(at, wide, count, shards, g, send, recv)
+    sums = SmallSum(at, total, landing, ssend, srecv)
+    groups = slots.shape[0] // rows
+    members = pick.shape[0] // rows
+
+    def fetch(i):
+        return pltpu.make_async_copy(slots.at[i], pool.at[i // rows, pl.ds((i % rows) * tokens, tokens)], isem.at[i])
+
+    total[0] = small[...]
+    sums.start()
+    gather.step0(0)
+    gather.step0(1)
+    for i in range(slots.shape[0]):
+        fetch(i).start()
+    gather.tick(0)
+    for i in range(slots.shape[0]):
+        fetch(i).wait()
+    gather.tick(1)
+
+    high, part = 16, width // 2
+
+    def sum_slots(i, carry):
+        cols = span(lax.rem(i, 2), part)
+        base = i // 2 * high
+        held = [
+            pool[s // rows, pl.ds(pl.multiple_of(base + (s % rows) * tokens, high), high), cols].astype(f32)
+            for s in range(slots.shape[0])
+        ]
+        for t in range(pick.shape[0]):
+            picked = pick[t, 0] * held[0]
+            for s in range(1, slots.shape[0]):
+                picked = picked + pick[t, s] * held[s]
+            spot = pl.ds(pl.multiple_of(base + (t % rows) * tokens, high), high)
+            pool[groups + t // rows, spot, cols] = picked.astype(bf16)
+        return carry
+
+    lax.fori_loop(0, tokens // high * 2, sum_slots, 0)
+
+    def up_sibling(y):
+        src = pool.at[groups + y * 2 + 1 - at.core]
+        return remote(src, landed.at[y], usend.at[y], urecv.at[y], at.sibling)
+
+    def up_across():
+        return remote(landed.at[1 - at.y], across_out, usend.at[2], urecv.at[2], at.across_y)
+
+    up_own = pltpu.make_async_copy(landed.at[at.y], own_out, isem.at[slots.shape[0]])
+
+    for y in range(2):
+        up_sibling(y).start()
+    sums.step(0)
+    gather.tick(2)
+    for y in range(2):
+        up_sibling(y).wait_recv()
+
+    def chip_sum(i, carry):
+        y, spot = i // (all_rows // 32), span(lax.rem(i, all_rows // 32), 32)
+        landed[y, spot] = added(landed[y, spot], pool[groups + y * 2 + at.core, spot]).astype(bf16)
+        return carry
+
+    lax.fori_loop(0, 2 * all_rows // 32, chip_sum, 0)
+    up_across().start()
+    up_own.start()
+    sums.step(1)
+    gather.tick(3)
+    for y in range(2):
+        up_sibling(y).wait_send()
+    sums.step(2)
+    sums.finish(small_full)
+
+    def keep(m):
+        return pltpu.make_async_copy(g.at[m], g_out.at[m], gsem.at[m])
+
+    def arrive(m):
+        gather.arrive(m)
+        keep(m).start()
+
+    def tile(m, cols):
+        return g[m, :, :, :, :, :, cols].reshape(width, cols.size)
+
+    def bias(i, cols):
+        return small_full[pl.ds(i, 1), cols]
+
+    def tiles(size, body):
+        def one(i, carry):
+            body(span(i // rows, size), span(lax.rem(i, rows), tokens))
+            return carry
+
+        lax.fori_loop(0, width // size * rows, one, 0)
+
+    def save(i):
+        return pltpu.make_async_copy(pool.at[i], saved.at[i], vsem.at[i])
+
+    def project(m):
+        bias_row = (0, None, 1)[m]
+
+        def body(cols, spot):
+            y = dot(x[spot], tile(m, cols))
+            if bias_row is not None:
+                y = y + bias(bias_row, cols)
+            pool[m, spot, cols] = y.astype(bf16)
+
+        arrive(m)
+        tiles(512, body)
+        save(m).start()
+
+    project(0)
+    gather.tick(4)
+    project(1)
+    gather.tick(5)
+    project(2)
+
+    pairs = width // head_pair
+    masks = half_masks(head_pair)
+    scale = (head_pair // 2) ** (-0.5)
+
+    def attend(i, carry):
+        spot, cols = span(i // pairs, tokens), span(lax.rem(i, pairs), head_pair)
+        query, keys, values = pool[0, spot, cols], pool[1, spot, cols], pool[2, spot, cols]
+        query = query * jnp.asarray(scale, bf16)
+        out = None
+        for mask in masks:
+            scores = across(query, keys * mask)
+            weight = jnp.exp(scores - jnp.max(scores, axis=-1, keepdims=True))
+            weight = weight * (1.0 / jnp.sum(weight, axis=-1, keepdims=True))
+            term = dot(weight.astype(bf16), values * mask)
+            out = term if out is None else out + term
+        pool[3, spot, cols] = out.astype(bf16)
+        turn = rows * pairs // 2
+        pl.when(lax.rem(i, turn) == turn - 2)(lambda: gather.tick(6 + i // turn))
+        return carry
+
+    lax.fori_loop(0, rows * pairs, attend, 0)
+    save(3).start()
+
+    def mix(cols, spot):
+        hidden[spot, cols] = dot(pool[3, spot], tile(3, cols)) + x[spot, cols].astype(f32) + bias(2, cols)
+
+    arrive(3)
+    tiles(512, mix)
+    gather.tick(8)
+
+    def unit(i):
+        return pltpu.make_async_copy(pool.at[6], unit_out.at[i], fsem.at[i])
+
+    def norm1(i, carry):
+        spot = span(i, 32)
+        normed, inverse = rms_center(hidden[spot])
+        result = normed * small_full[3:4, :] + small_full[4:5, :]
+        hidden[spot] = result
+        pool[4, spot] = result.astype(bf16)
+        pool[6, spot] = normed.astype(bf16)
+        inverse1[spot] = inverse
+        return carry
+
+    lax.fori_loop(0, all_rows // 32, norm1, 0)
+    save(4).start()
+    unit(0).start()
+
+    def save_act(j):
+        return pltpu.make_async_copy(pool.at[5], act_out.at[j], asem)
+
+    def save_slope(j):
+        return pltpu.make_async_copy(pool.at[6], slope_out.at[j], dsem)
+
+    unit(0).wait()
+
+    def feed(j, carry):
+        m = 4 + 2 * j
+        pl.when(j >= 1)(lambda: gather.tick(m + 3))
+        arrive(m)
+
+        @pl.when(j >= 1)
+        def _():
+            save_act(j - 1).wait()
+            save_slope(j - 1).wait()
+
+        def up(cols, spot):
+            value, slope = exact_gelu(dot(pool[4, spot], tile(m, cols)) + bias(8 + j, cols))
+            pool[5, spot, cols] = value.astype(bf16)
+            pool[6, spot, cols] = slope.astype(bf16)
+
+        tiles(256, up)
+        save_act(j).start()
+        save_slope(j).start()
+        pl.when(j >= 1)(lambda: gather.tick(m + 4))
+        arrive(m + 1)
+
+        def back(cols, spot):
+            hidden[spot, cols] = hidden[spot, cols] + dot(pool[5, spot], tile(m + 1, cols))
+
+        tiles(512, back)
+        return carry
+
+    blocks = (count - 4) // 2
+    lax.fori_loop(0, blocks, feed, 0)
+    save_act(blocks - 1).wait()
+    save_slope(blocks - 1).wait()
+
+    def norm2(i, carry):
+        spot = span(i, 32)
+        normed, inverse = rms_center(hidden[spot] + small_full[5:6, :])
+        pool[5, spot] = (normed * small_full[6:7, :] + small_full[7:8, :]).astype(bf16)
+        pool[6, spot] = normed.astype(bf16)
+        inverse2[spot] = inverse
+        return carry
+
+    lax.fori_loop(0, all_rows // 32, norm2, 0)
+    finish = pltpu.make_async_copy(pool.at[5], final_out, fsem.at[2])
+    finish.start()
+    unit(1).start()
+
+    def drain(m, carry):
+        gather.drain(m)
+        keep(m).wait()
+        return carry
+
+    lax.fori_loop(0, count, drain, 0)
+    for i in range(5):
+        save(i).wait()
+    up_own.wait()
+    up_across().wait()
+    finish.wait()
+    unit(1).wait()
+
+
+def forward(x, shards, small, pick, slots, nz, nx, tokens):
+    f32, bf16 = jnp.float32, jnp.bfloat16
+    count, shard_rows, width = shards.shape
+    all_rows = x.shape[0]
+    group_members = pick.shape[0] * tokens // all_rows
+    assert group_members == 4 and slots.shape[0] * tokens == 2 * all_rows
+    wide = width * 3 // 4
+    vmem, anywhere = pl.BlockSpec(memory_space=pltpu.VMEM), pl.BlockSpec(memory_space=pl.ANY)
+    acts = (all_rows, width)
+    blocks = (count - 4) // 2
+    dma = pltpu.SemaphoreType.DMA
+    full = (count, 2, 2, nz, nx, shard_rows, width)
+    out = jax.ShapeDtypeStruct
     return pl.pallas_call(
-        partial(scatter_kernel, nz, nx, wide, count),
+        partial(forward_kernel, nz, nx, wide, tokens, 2 * width // HEADS),
         out_shape=[
-            jax.ShapeDtypeStruct((count, rows, columns), jnp.float32),
-            jax.ShapeDtypeStruct(small.shape, jnp.float32),
+            out(full, bf16),
+            out((5, *acts), bf16),
+            out((blocks, *acts), bf16),
+            out((blocks, *acts), bf16),
+            out((2, *acts), bf16),
+            out(acts, bf16),
+            out(acts, bf16),
+            out(acts, bf16),
+            out(small.shape, f32),
+            out((all_rows, 1), f32),
+            out((all_rows, 1), f32),
         ],
-        in_specs=[pl.BlockSpec(memory_space=pl.ANY), vmem],
-        out_specs=[vmem, vmem],
+        in_specs=[vmem, vmem, vmem, pl.BlockSpec(memory_space=pltpu.SMEM), anywhere],
+        out_specs=[anywhere] * 8 + [vmem] * 3,
         scratch_shapes=[
-            pltpu.VMEM((2, 2, nz, nx, rows, columns), jnp.bfloat16),
-            *scatter_scratch(count, nz, nx, rows, columns, wide),
-            *small_scratch(nz, small.shape),
-            pltpu.SemaphoreType.DMA((2,)),
+            pltpu.VMEM(full, bf16),
+            pltpu.VMEM((7, *acts), bf16),
+            pltpu.VMEM(acts, f32),
+            pltpu.VMEM((2, *acts), bf16),
+            *small_scratch(nz, small.shape)[:2],
+            dma((count, nz + 4)),
+            dma((count, nz + 4)),
+            dma((2 + nz,)),
+            dma((2 + nz,)),
+            dma((3,)),
+            dma((3,)),
+            dma((slots.shape[0] + 1,)),
+            dma((count,)),
+            dma((5,)),
+            dma,
+            dma,
+            dma((3,)),
         ],
         compiler_params=pltpu.CompilerParams(
-            collective_id=2, has_side_effects=True, vmem_limit_bytes=56 * 2**20
+            collective_id=1, has_side_effects=True, vmem_limit_bytes=60 * 2**20
         ),
-    )(terms, small)
+    )(x, shards, small, pick, slots)
+
+
+def backward_kernel(
+    nz, nx, wide, tokens, head_pair,
+    x, own_up, across_up, final, unit, inverse1, inverse2, small_full, act, slope, saved, g,
+    out, small_out, input_out, table,
+    rc, r3a, r3b, r2, rz, send, recv, total, landing, ssend, srecv,
+    term, weight, pool, hidden, wsem, psem, hsem, tsend, trecv, tsem,
+):
+    f32, bf16 = jnp.float32, jnp.bfloat16
+    count = out.shape[0]
+    all_rows, width = x.shape
+    rows = all_rows // tokens
+    at = Partners(nz, nx)
+    at.meet()
+    scatter = Scatter(at, wide, rc, r3a, r3b, r2, rz, send, recv)
+    sums = SmallSum(at, total, landing, ssend, srecv)
+
+    here = pltpu.make_async_copy(final, table.at[at.y, at.core], tsem)
+    to_sibling = remote(final, table.at[at.y, at.core], tsend.at[0], trecv.at[0], at.sibling)
+    to_across = remote(final, table.at[at.y, at.core], tsend.at[1], trecv.at[1], at.across_y)
+    passed = table.at[1 - at.y, at.core]
+    pass_on = remote(passed, passed, tsend.at[2], trecv.at[2], at.sibling)
+
+    def load(src, entry, i):
+        return pltpu.make_async_copy(src, pool.at[entry], psem.at[i])
+
+    def fetch(m, slot, i):
+        return pltpu.make_async_copy(g.at[m], weight.at[slot], wsem.at[i])
+
+    blocks = act.shape[0]
+    up_block, down_block = (lambda j: 4 + 2 * j), (lambda j: 5 + 2 * j)
+    unit2, own_load, across_load = load(unit.at[1], 1, 0), load(own_up, 2, 1), load(across_up, 3, 2)
+    act_entry = [5, 2, 3, 5]
+    act_load = [load(act.at[j], act_entry[j], 3 + j) for j in range(blocks)]
+    slope_entry = [4, 2, 3, 4]
+    slope_load = [load(slope.at[j], slope_entry[j], 7 + j) for j in range(blocks)]
+    low_load, unit1, mixed_load = load(saved.at[4], 6, 11), load(unit.at[0], 5, 12), load(saved.at[3], 4, 13)
+    query_load, key_load, value_load = (load(saved.at[i], (2, 3, 6)[i], 14 + i) for i in range(3))
+    x_load = load(x, 4, 17)
+    down_fetch = [fetch(down_block(j), 0, 2 * j) for j in range(blocks)]
+    up_fetch = [fetch(up_block(j), 1, 2 * j + 1) for j in range(blocks)]
+    last = 2 * blocks
+    output_fetch, query_fetch, key_fetch, value_fetch = (
+        fetch(m, slot, last + i) for i, (m, slot) in enumerate(((3, 0), (0, 1), (1, 0), (2, 1)))
+    )
+    for copy in (unit2, own_load, across_load, act_load[0], down_fetch[0], up_fetch[0], slope_load[0], low_load):
+        copy.start()
+    to_across.start()
+    to_sibling.start()
+    here.start()
+    total[0] = jnp.zeros_like(total[0])
+
+    def folded(block):
+        return jnp.sum(block.reshape(-1, 8, block.shape[-1]), axis=0)
+
+    def norm_back(gain_row, shift_row, low_row, inverse, incoming, normed_entry, low_entry):
+        def body(i, carry):
+            spot = span(i, 32)
+            grad, normed = incoming(spot), pool[normed_entry, spot].astype(f32)
+            scaled = grad * small_full[gain_row : gain_row + 1, :]
+            inner = (
+                scaled
+                - jnp.mean(scaled, axis=-1, keepdims=True)
+                - normed * jnp.mean(scaled * normed, axis=-1, keepdims=True)
+            )
+            result = inner * inverse[spot]
+            low = result.astype(bf16)
+            hidden[spot] = result
+            pool[low_entry, spot] = low
+            return tuple(c + folded(b) for c, b in zip(carry, (grad * normed, grad, low.astype(f32))))
+
+        zero = jnp.zeros((8, width), f32)
+        found = lax.fori_loop(0, all_rows // 32, body, (zero, zero, zero))
+        for row, value in zip((gain_row, shift_row, low_row), found):
+            total[0, row : row + 1, :] = jnp.sum(value, axis=0, keepdims=True)
+
+    def tiles(size, body):
+        def one(i, carry):
+            body(i // rows, span(i // rows, size), span(lax.rem(i, rows), tokens))
+            return carry
+
+        lax.fori_loop(0, width // size * rows, one, 0)
+
+    def turned(slot, y):
+        return weight[slot, y].reshape(width // 2, width)
+
+    def own_half(slot):
+        return lambda y, z: term[slot, y, at.core, z]
+
+    def produce(m, left, right, after=True):
+        slot = m % 2
+
+        def half(core):
+            def body(i, carry):
+                y, cols = i // 2, span(lax.rem(i, 2), width // 2)
+                picked = span(y * 2 + core, width // 4)
+                value = down(pool[left, :, picked], pool[right, :, cols]).astype(bf16)
+                term[slot, y, core, :, :, :, cols] = value.reshape(nz, nx, -1, width // 2)
+                return carry
+
+            lax.fori_loop(0, 4, body, 0)
+
+        half(1 - at.core)
+        scatter.start(m, term.at[slot, :, 1 - at.core])
+        if m > 0 and after:
+            scatter.step1(m - 1, own_half(1 - slot))
+        half(at.core)
+
+    def tick(i):
+        for step, ahead in ((scatter.step4, 2), (scatter.step3, 1), (scatter.step2, 0)):
+            m = i - ahead
+            call = partial(step, m) if ahead < 2 else partial(step, m, out)
+            if isinstance(i, int):
+                if 0 <= m < count:
+                    call()
+            else:
+                pl.when((m >= 0) & (m < count))(call)
+
+    for copy in (unit2, own_load, across_load):
+        copy.wait()
+    norm_back(6, 7, 5, inverse2, lambda spot: added(pool[2, spot], pool[3, spot]), 1, 0)
+
+    act_load[1].start()
+    act_load[2].start()
+    for j in range(blocks):
+        act_load[j].wait()
+        produce(j, act_entry[j], 0)
+        if j == 0:
+            act_load[3].start()
+        elif j < 3:
+            slope_load[j].start()
+        else:
+            unit1.start()
+    tick(0)
+
+    low_load.wait()
+    for j in range(blocks):
+        down_fetch[j].wait()
+        slope_load[j].wait()
+
+        def pre_back(n, cols, spot, j=j):
+            value = across(pool[0, spot], turned(0, n)) * pool[slope_entry[j], spot, cols].astype(f32)
+            value = value.astype(bf16)
+            pool[1, spot, cols] = value
+            row = pl.ds(8 + j, 1)
+            total[0, row, cols] = total[0, row, cols] + jnp.sum(value.astype(f32), axis=0, keepdims=True)
+
+        tiles(width // 2, pre_back)
+        if j + 1 < blocks:
+            down_fetch[j + 1].start()
+        else:
+            output_fetch.start()
+        (lambda: slope_load[3].start(), query_load.start, key_load.start, mixed_load.start)[j]()
+        produce(blocks + j, 6, 1)
+        up_fetch[j].wait()
+
+        def hidden_back(n, cols, spot):
+            hidden[spot, cols] = hidden[spot, cols] + across(pool[1, spot], turned(1, n))
+
+        tiles(width // 2, hidden_back)
+        if j + 1 < blocks:
+            up_fetch[j + 1].start()
+        else:
+            query_fetch.start()
+        if j == blocks - 1:
+            value_load.start()
+        tick(1 + j)
+
+    unit1.wait()
+    norm_back(3, 4, 2, inverse1, lambda spot: hidden[spot], 5, 0)
+    mixed_load.wait()
+    produce(2 * blocks, 4, 0)
+    x_load.start()
+    output_fetch.wait()
+
+    def mixed_back(n, cols, spot):
+        pool[1, spot, cols] = across(pool[0, spot], turned(0, n)).astype(bf16)
+
+    tiles(width // 2, mixed_back)
+    key_fetch.start()
+    for copy in (query_load, key_load, value_load):
+        copy.wait()
+    tick(5)
+    scatter.step1(2 * blocks, own_half((2 * blocks) % 2))
+
+    pairs = width // head_pair
+    masks = half_masks(head_pair)
+    scale = (head_pair // 2) ** (-0.5)
+
+    def attend(i, carry):
+        spot, cols = span(i // pairs, tokens), span(lax.rem(i, pairs), head_pair)
+        query, keys, values, mixed_grad = (pool[e, spot, cols] for e in (2, 3, 6, 1))
+        query_grad = key_grad = value_grad = None
+        for mask in masks:
+            own_keys = keys * (mask * jnp.asarray(scale, bf16))
+            scores = across(own_keys, query)
+            probs = jnp.exp(scores - jnp.max(scores, axis=0, keepdims=True))
+            probs = probs * (1.0 / jnp.sum(probs, axis=0, keepdims=True))
+            prob_grad = across(values * mask, mixed_grad)
+            weighed = probs * prob_grad
+            score_grad = (weighed - probs * jnp.sum(weighed, axis=0, keepdims=True)).astype(bf16)
+            terms = (
+                down(score_grad, own_keys),
+                dot(score_grad, query * mask),
+                dot(probs.astype(bf16), mixed_grad * mask),
+            )
+            if query_grad is None:
+                query_grad, key_grad, value_grad = terms
+            else:
+                query_grad, key_grad, value_grad = query_grad + terms[0], key_grad + terms[1], value_grad + terms[2]
+        query_grad, value_grad = query_grad.astype(bf16), value_grad.astype(bf16)
+        pool[2, spot, cols] = query_grad
+        pool[3, spot, cols] = (key_grad * scale).astype(bf16)
+        pool[6, spot, cols] = value_grad
+        for row, value in ((0, query_grad), (1, value_grad)):
+            found = jnp.sum(value.astype(f32), axis=0, keepdims=True)
+            total[0, row : row + 1, cols] = total[0, row : row + 1, cols] + found
+        turn = rows * pairs // 3
+        pl.when(lax.rem(i, turn) == turn - 1)(lambda: tick(6 + i // turn))
+        return carry
+
+    lax.fori_loop(0, rows * pairs, attend, 0)
+    sums.start()
+
+    x_load.wait()
+    for i, entry in enumerate((6, 2, 3)):
+        produce(2 * blocks + 1 + i, 4, entry, i > 0)
+        sums.step(i)
+    scatter.step1(count - 1, own_half((count - 1) % 2))
+    tick(9)
+
+    def input_back(slot, entry, fetched):
+        def body(n, cols, spot):
+            hidden[spot, cols] = hidden[spot, cols] + across(pool[entry, spot], turned(slot, n))
+
+        fetched.wait()
+        tiles(width // 2, body)
+
+    input_back(1, 2, query_fetch)
+    value_fetch.start()
+    tick(10)
+    input_back(0, 3, key_fetch)
+    to_across.wait_recv()
+    pass_on.start()
+    tick(11)
+    input_back(1, 6, value_fetch)
+    done = pltpu.make_async_copy(hidden, input_out, hsem)
+    done.start()
+    tick(12)
+    sums.finish(small_out)
+    tick(13)
+    done.wait()
+
+    def drain(m, carry):
+        scatter.drain(m)
+        return carry
+
+    lax.fori_loop(0, count, drain, 0)
+    here.wait()
+    to_sibling.wait()
+    to_across.wait_send()
+    pass_on.wait()
+
+
+def backward(x, own_up, across_up, final, unit, inverse1, inverse2, small_full, act, slope, saved, g, nz, nx, tokens):
+    f32, bf16 = jnp.float32, jnp.bfloat16
+    count, _, _, _, _, shard_rows, width = g.shape
+    acts = x.shape
+    wide = width * 3 // 4
+    vmem, anywhere = pl.BlockSpec(memory_space=pltpu.VMEM), pl.BlockSpec(memory_space=pl.ANY)
+    dma = pltpu.SemaphoreType.DMA
+    out = jax.ShapeDtypeStruct
+    block = (2, 2, nz, nx, shard_rows, width)
+    return pl.pallas_call(
+        partial(backward_kernel, nz, nx, wide, tokens, 2 * width // HEADS),
+        out_shape=[
+            out((count, shard_rows, width), f32),
+            out(small_full.shape, f32),
+            out(acts, f32),
+            out((2, 2, *acts), bf16),
+        ],
+        in_specs=[anywhere] * 5 + [vmem] * 3 + [anywhere] * 4,
+        out_specs=[vmem, vmem, anywhere, anywhere],
+        scratch_shapes=[
+            *scatter_scratch(count, nz, nx, shard_rows, width, wide),
+            *small_scratch(nz, small_full.shape),
+            pltpu.VMEM((2, *block), bf16),
+            pltpu.VMEM((2, *block), bf16),
+            pltpu.VMEM((7, *acts), bf16),
+            pltpu.VMEM(acts, f32),
+            dma((count,)),
+            dma((18,)),
+            dma,
+            dma((3,)),
+            dma((3,)),
+            dma,
+        ],
+        compiler_params=pltpu.CompilerParams(
+            collective_id=2, has_side_effects=True, vmem_limit_bytes=60 * 2**20
+        ),
+    )(x, own_up, across_up, final, unit, inverse1, inverse2, small_full, act, slope, saved, g)
+
+
+def pick_kernel(slot_row, row, out):
+    out[...] = row[...]
+
+
+def pick_rows(slot_row, table):
+    members, tokens, width = table.shape
+    block = (1, tokens, width)
+    return pl.pallas_call(
+        pick_kernel,
+        out_shape=jax.ShapeDtypeStruct((slot_row.shape[0], tokens, width), table.dtype),
+        grid_spec=pltpu.PrefetchScalarGridSpec(
+            num_scalar_prefetch=1,
+            grid=(slot_row.shape[0],),
+            in_specs=[pl.BlockSpec(block, lambda s, slot_row: (jnp.clip(slot_row[s], 0, members - 1), 0, 0))],
+            out_specs=pl.BlockSpec(block, lambda s, slot_row: (s, 0, 0)),
+        ),
+    )(slot_row, table)
+
+
+def prepare(
+    rows_in, slot_row, weights, small_parameters, up_bias, dp_size
+):
+    row_count, token_count, width = rows_in.shape
+    query_weight, key_weight, value_weight, output_weight, expand_weight, down_weight = weights
+    shard = query_weight.shape[0]
+    blocks = down_weight.shape[0] // shard
+    me = lax.axis_index(("dp", "fsdp"))
+    ups = expand_weight.reshape(shard, -1, blocks, shard).transpose(2, 0, 1, 3).reshape(blocks, shard, width)
+    downs = down_weight.reshape(blocks, shard, width)
+    paired = jnp.stack([ups, downs], axis=1).reshape(2 * blocks, shard, width)
+    shards = jnp.concatenate([jnp.stack([query_weight, key_weight, value_weight, output_weight]), paired])
+    mine = jnp.concatenate([jnp.stack(small_parameters), up_bias.reshape(blocks, shard)]).astype(jnp.float32)
+    small = lax.dynamic_update_slice(
+        jnp.zeros((16, width), jnp.float32), mine, (jnp.int32(0), me * shard)
+    )
+    wanted = lax.broadcasted_iota(jnp.int32, (row_count * dp_size, slot_row.shape[0]), 0)
+    pick = (wanted == slot_row[None, :]).astype(jnp.float32)
+    return rows_in.reshape(-1, width), shards, small, pick
+
+
+def on_device_kernels(
+    rows_in,
+    slot_row,
+    live_count,
+    slot_activation_gradient,
+    query_weight,
+    key_weight,
+    value_weight,
+    output_weight,
+    query_bias,
+    value_bias,
+    output_bias,
+    attn_gain,
+    attn_shift,
+    expand_weight,
+    up_bias,
+    down_weight,
+    down_bias,
+    ffn_gain,
+    ffn_shift,
+):
+    row_count, token_count, width = rows_in.shape
+    shard = query_weight.shape[0]
+    nx = 2
+    nz = lax.axis_size("fsdp") // nx
+    x, shards, small, pick = prepare(
+        rows_in,
+        slot_row,
+        (query_weight, key_weight, value_weight, output_weight, expand_weight, down_weight),
+        (query_bias, value_bias, output_bias, attn_gain, attn_shift, down_bias, ffn_gain, ffn_shift),
+        up_bias,
+        lax.axis_size("dp"),
+    )
+    g, saved, act, slope, unit, final, own_up, across_up, small_full, inverse1, inverse2 = forward(
+        x, shards, small, pick, slot_activation_gradient, nz, nx, token_count
+    )
+    sums, small_sums, input_full, table = backward(
+        x, own_up, across_up, final, unit, inverse1, inverse2, small_full, act, slope, saved, g, nz, nx, token_count
+    )
+    slot_acts = pick_rows(slot_row, table.reshape(-1, token_count, width))
+    live_rows = lax.broadcasted_iota(jnp.int32, (row_count,), 0) < live_count[0]
+    input_grad = jnp.where(live_rows[:, None, None], input_full.reshape(rows_in.shape), 0.0)
+    me = lax.axis_index(("dp", "fsdp"))
+    mine = lax.dynamic_slice(small_sums, (jnp.int32(0), me * shard), (small_sums.shape[0], shard))
+    blocks = (sums.shape[0] - 4) // 2
+    down_sum = sums[:blocks].reshape(-1, width)
+    ups = sums[blocks : 2 * blocks].reshape(blocks, shard, -1, shard)
+    up_sum = ups.transpose(1, 2, 0, 3).reshape(shard, -1)
+    output_sum, value_sum, query_sum, key_sum = (sums[2 * blocks + i] for i in range(4))
+    return (
+        slot_acts,
+        input_grad,
+        query_sum,
+        key_sum,
+        value_sum,
+        output_sum,
+        mine[0],
+        mine[1],
+        mine[2],
+        mine[3],
+        mine[4],
+        up_sum,
+        mine[8 : 8 + blocks].reshape(-1),
+        down_sum,
+        mine[5],
+        mine[6],
+        mine[7],
+    )
 
 
 def norm_forward(hidden, gain, shift):
@@ -334,7 +1076,7 @@
     return jnp.sum(grads, axis=(0, 1), dtype=jnp.float32)
 
 
-def on_device(
+def on_device_plain(
     rows_in,
     slot_row,
     live_count,
@@ -491,22 +1233,10 @@
     live_rows = lax.broadcasted_iota(jnp.int32, (row_count,), 0) < live_count[0]
     input_grad = jnp.where(live_rows[:, None, None], input_full, 0.0)
     devices = packed_full.shape[0]
-    if small_rows % 16 == 0 and lax.axis_size("dp") == 4:
-        nx = 2
-        nz = lax.axis_size("fsdp") // nx
-        terms = [
-            query_wgrad,
-            key_wgrad,
-            value_wgrad,
-            output_grad,
-            *(up_grad[:, j * feature_count : (j + 1) * feature_count] for j in range(4)),
-            *(down_grad.reshape(devices, 4, -1, feature_count)[:, j] for j in range(4)),
-        ]
-        terms = jnp.stack(
-            [t.astype(jnp.bfloat16).reshape(2, 2, nz, nx, small_rows, feature_count) for t in terms]
-        )
-        small = jnp.stack(
-            [
+    small_terms = jnp.concatenate(
+        [
+            v.reshape(devices, -1, small_rows)
+            for v in (
                 query_bias_grad,
                 value_bias_grad,
                 output_bias_grad,
@@ -515,42 +1245,18 @@
                 down_bias_grad,
                 gain2_grad,
                 shift2_grad,
-                *up_bias_grad.reshape(devices, 4, small_rows).transpose(1, 0, 2).reshape(4, -1),
-                *([jnp.zeros_like(gain1_grad)] * 4),
-            ]
-        )
-        wsum, small_sum = scatter_terms(terms, small, nz, nx)
-        me = lax.axis_index(("dp", "fsdp"))
-        small_sum = lax.dynamic_slice(small_sum, (0, me * small_rows), (16, small_rows))
-        query_sum, key_sum, value_sum, output_sum = (wsum[i] for i in range(4))
-        up_sum = wsum[4:8].transpose(1, 0, 2).reshape(small_rows, -1)
-        down_sum = wsum[8:12].reshape(-1, feature_count)
-        small_sum = small_sum[:12]
-    else:
-        small_terms = jnp.concatenate(
-            [
-                v.reshape(devices, -1, small_rows)
-                for v in (
-                    query_bias_grad,
-                    value_bias_grad,
-                    output_bias_grad,
-                    gain1_grad,
-                    shift1_grad,
-                    down_bias_grad,
-                    gain2_grad,
-                    shift2_grad,
-                    up_bias_grad,
-                )
-            ],
-            axis=1,
-        )
-        small_sum = lax.psum_scatter(small_terms, ("dp", "fsdp"), scatter_dimension=0, tiled=True)[0]
-        down_sum, up_sum, output_sum, value_sum, query_sum, key_sum = (
-            lax.psum_scatter(
-                term.astype(jnp.bfloat16), ("dp", "fsdp"), scatter_dimension=0, tiled=True
-            ).astype(jnp.float32)
-            for term in (down_grad, up_grad, output_grad, value_wgrad, query_wgrad, key_wgrad)
-        )
+                up_bias_grad,
+            )
+        ],
+        axis=1,
+    )
+    small_sum = lax.psum_scatter(small_terms, ("dp", "fsdp"), scatter_dimension=0, tiled=True)[0]
+    down_sum, up_sum, output_sum, value_sum, query_sum, key_sum = (
+        lax.psum_scatter(
+            term.astype(jnp.bfloat16), ("dp", "fsdp"), scatter_dimension=0, tiled=True
+        ).astype(jnp.float32)
+        for term in (down_grad, up_grad, output_grad, value_wgrad, query_wgrad, key_wgrad)
+    )
     return (
         slot_acts,
         input_grad,
@@ -594,8 +1300,9 @@
         P(("dp", "fsdp")),
         P(("dp", "fsdp")),
     )
+    kernels = mesh.shape["dp"] == 4 and mesh.shape["fsdp"] == 8
     return jax.shard_map(
-        on_device,
+        on_device_kernels if kernels else on_device_plain,
         mesh=mesh,
         in_specs=placed,
         out_specs=(

time: 834 us -> 450 us (0.54)
  Pallas kernels: 145 us -> 418 us
  matrix products: 237 us -> 0 us
  waiting for transfers between devices: 194 us -> 0 us
  other arithmetic: 86.5 us -> 5.56 us
  blocking collectives: 71.7 us -> 0 us
  local copies, waits for them, and re-layouts: 74 us -> 23.9 us
  between operations: 17.3 us -> 1.45 us
    pallas_call x1 -> x3, Pallas kernels: 145 us -> 418 us  [the longest x1 210 us: forward(): pl.pallas_call(partial(forward_kernel, nz, nx, wide, tokens, 2 * width //...]
    dot_general x25 -> x0, matrix products: 237 us -> none  [the longest x6 60.8 us: apply_back(): jnp.einsum('rse,de->rsd', grads, weight, preferred_element_type=jnp.float32)]
    all_gather x7 -> x0, waiting for transfers between devices: 190 us -> none  [the longest x6 190 us: on_device(): lax.all_gather(weight, ('dp', 'fsdp'), axis=0, tiled=True)]
    all_gather x1 -> x0, blocking collectives: 71.7 us -> none  [on_device(): packed_full = lax.all_gather(packed, ('dp', 'fsdp'), axis=0)]
    convert_element_type x4 -> x2, other arithmetic: 59.5 us -> 0.65 us  [the longest x1 0.64 us: prepare(): pick = (wanted == slot_row[None, :]).astype(jnp.float32)]
    unnamed x109 -> x12, local copies, waits for them, and re-layouts: 28.8 us -> 3.65 us
    reduce_sum x6 -> x0, other arithmetic: 20.8 us -> none  [the longest x1 10.3 us: on_device(): row_sum = jnp.sum(expo, axis=-1, keepdims=True)]
    convert_element_type x13 -> x0, local copies, waits for them, and re-layouts: 13.5 us -> none  [the longest x1 4.11 us: on_device(): keys = apply_weight(rows_in, key_full).astype(jnp.bfloat16)]
  transfers between devices with their start and end apart: 8 -> 0, of which waited for: 5 -> 0; matrix products, arithmetic and copies ran while one was open for 30% -> 0% of each run, Pallas kernels for 18% -> 0%
where the time goes in v3:
time: 450 us; the launch traced here: 449 us
  Pallas kernels  418 us (93%)
  local copies, waits for them, and re-layouts  23.9 us (5%)
  other arithmetic  5.56 us (1%)
    pallas_call x1, Pallas kernels, forward(): pl.pallas_call(partial(forward_kernel, nz, nx, wide, tokens, 2 * width //...  210 us
    pallas_call x1, Pallas kernels, backward(): pl.pallas_call(partial(backward_kernel, nz, nx, wide, tokens, 2 * width /...  201 us

profile of v3, /device:TPU:0, one launch (start us, length us, event | category | flops | bytes accessed | tf_op | source)
XLA Modules:
  0.0 448.6 jit_solution(12397025466032155167)
XLA Ops:
  0.7 0.8 reshape.72
  1.5 0.8 concatenate.7
  2.3 0.6 dynamic_update_slice.3.small
  2.9 0.9 bitcast_dynamic-update-slice_fusion.3
  3.7 0.8 bitcast_dynamic-update-slice_fusion.2
  4.6 0.8 bitcast_dynamic-update-slice_fusion.1
  5.4 0.8 bitcast_dynamic-update-slice_fusion
  6.3 1.7 reshape.70
  8.0 0.2 copy.36
  8.2 1.1 stack_reshape.6
  9.4 0.6 fusion.pick
  10.0 0.2 copy-done
  10.3 210.3 %shard_map.314 = (bf16[12,2,2,4,2,32,1024]{6,5,4,3,2,1,0:T(8,128)(2,1)}, bf16[5,960,1024]{2,1,0:T(8,128)(2,1)}, bf16[4,960,1024]{2,1,0:T(8,128)(2,1)}, bf16[4,96...) custom-call(bf16[960,1024]{1,0:T(8,128)(2,1)} %bitcast.56, ...), custom_call_target="tpu_custom_call" | custom-call | tf_op jit(solution)/shard_map/pallas_call | solution.py:588
  220.6 201.2 %shard_map.315 = (f32[12,32,1024]{2,1,0:T(8,128)}, f32[16,1024]{1,0:T(8,128)}, f32[960,1024]{1,0:T(8,128)}, bf16[2,2,960,1024]{3,2,1,0:T(8,128)(2,1)}) custom-call(bf16[960,1024]{1,0:T(8,128)(2,1)} %bitcast.57, bf16[960,1024]{1,0:T(8,128)(2,1)} %get-tuple-element.32.own_up, bf16[960,1024]{1,0:T(8,128)(2,1)} %get-tuple-element.33.across_up, ...), custom_call_target="tpu_custom_call" | custom-call | tf_op jit(solution)/shard_map/pallas_call | solution.py:902
  421.8 2.1 fusion.1
  423.9 0.7 reshape.75
  424.6 3.1 copy.38
  427.7 4.4 reshape.76
  432.8 4.9 %broadcast_select_fusion = f32[3,320,1024]{2,1,0:T(8,128)} fusion(f32[3,320,1024]{2,1,0:T(8,128)} %bitcast.59, pred[3]{0:T(512)(128)(4,1)S(1)} %iota_compare_fusion.1), kind=kLoop, calls=%fused_computation | loop fusion | flops 983040 | bytes 7864323 | tf_op jit(solution)/shard_map/jit(_where)/select_n | solution.py:1013
  437.6 6.1 %shard_map.316 = bf16[6,320,1024]{2,1,0:T(8,128)(2,1)} custom-call(s32[6]{0:T(128)} %slot_row.1, bf16[12,320,1024]{2,1,0:T(8,128)(2,1)} %bitcast.55), custom_call_target="tpu_custom_call" | custom-call | tf_op jit(solution)/shard_map/pallas_call | solution.py:939
  443.8 1.9 slice_bitcast_fusion
  445.7 1.6 dynamic-slice_bitcast_fusion
  447.3 0.7 dynamic-slice.5
  448.0 0.6 reshape.77
  (12 shorter events, 0.1 us)
Async XLA Ops:
  0.7 8.6 %copy-start.2 = (bf16[128,1024]{1,0:T(8,128)(2,1)S(1)}, bf16[128,1024]{1,0:T(8,128)(2,1)}, u32[]{:S(2)}) copy-start(bf16[128,1024]{1,0:T(8,128)(2,1)} %param.34) | copy-start | bytes 786436
  0.7 8.7 %copy-start.3 = (s32[6]{0:T(128)S(1)}, s32[6]{0:T(128)}, u32[]{:S(2)}) copy-start(s32[6]{0:T(128)} %slot_row.1) | copy-start | bytes 76
  2.9 7.2 %copy-start.1 = (f32[16,1024]{1,0:T(8,128)}, f32[16,1024]{1,0:T(8,128)S(1)}, u32[]{:S(2)}) copy-start(f32[16,1024]{1,0:T(8,128)S(1)} %dynamic_update_slice.3.small) | copy-start | bytes 196612
  9.4 0.9 copy-start

commit v4 on v3

--- a/solution.py
+++ b/solution.py
@@ -318,14 +318,10 @@
     def arrive(self, m):
         self.to_sibling(m).wait_recv()
 
-    def tick(self, i):
-        for step, ahead in ((self.step3, 3), (self.step2, 2), (self.step1, 1), (self.step0, -2)):
-            m = i - ahead
-            if isinstance(i, int):
-                if 0 <= m < self.count:
-                    step(m)
-            else:
-                pl.when((m >= 0) & (m < self.count))(partial(step, m))
+    def turn(self, m):
+        for step, ahead in ((self.step3, 0), (self.step2, 2), (self.step1, 4), (self.step0, 6)):
+            if 0 <= m + ahead < self.count:
+                step(m + ahead)
 
     def drain(self, m):
         for k in range(1, self.at.nz):
@@ -339,7 +335,7 @@
     x, shards, small, pick, slots,
     g_out, saved, act_out, slope_out, unit_out, final_out, own_out, across_out, small_full, inverse1, inverse2,
     g, pool, hidden, landed, total, landing,
-    send, recv, ssend, srecv, usend, urecv, isem, gsem, vsem, asem, dsem, fsem,
+    send, recv, ssend, srecv, usend, urecv, across_send, across_recv, isem, gsem, vsem, asem, dsem, fsem,
 ):
     f32, bf16 = jnp.float32, jnp.bfloat16
     count = g.shape[0]
@@ -357,14 +353,12 @@
 
     total[0] = small[...]
     sums.start()
-    gather.step0(0)
-    gather.step0(1)
+    for m in range(4):
+        gather.step0(m)
     for i in range(slots.shape[0]):
         fetch(i).start()
-    gather.tick(0)
     for i in range(slots.shape[0]):
         fetch(i).wait()
-    gather.tick(1)
 
     high, part = 16, width // 2
 
@@ -383,21 +377,39 @@
             pool[groups + t // rows, spot, cols] = picked.astype(bf16)
         return carry
 
+    gather.step1(0)
+    sums.step(0)
+    gather.step0(4)
     lax.fori_loop(0, tokens // high * 2, sum_slots, 0)
+    gather.step1(1)
+    gather.step2(0)
+    sums.step(1)
 
     def up_sibling(y):
         src = pool.at[groups + y * 2 + 1 - at.core]
         return remote(src, landed.at[y], usend.at[y], urecv.at[y], at.sibling)
 
-    def up_across():
-        return remote(landed.at[1 - at.y], across_out, usend.at[2], urecv.at[2], at.across_y)
+    pieces = across_send.shape[0]
+
+    def up_across(i):
+        piece = pl.ds(i * (all_rows // pieces), all_rows // pieces)
+        return remote(
+            landed.at[1 - at.y, piece], across_out.at[piece], across_send.at[i], across_recv.at[i], at.across_y
+        )
+
+    def turn(m):
+        gather.turn(m)
+        up_across(m).start()
 
     up_own = pltpu.make_async_copy(landed.at[at.y], own_out, isem.at[slots.shape[0]])
 
     for y in range(2):
         up_sibling(y).start()
-    sums.step(0)
-    gather.tick(2)
+    gather.step0(5)
+    gather.step1(2)
+    sums.step(2)
+    gather.step2(1)
+    gather.step1(3)
     for y in range(2):
         up_sibling(y).wait_recv()
 
@@ -407,14 +419,11 @@
         return carry
 
     lax.fori_loop(0, 2 * all_rows // 32, chip_sum, 0)
-    up_across().start()
     up_own.start()
-    sums.step(1)
-    gather.tick(3)
     for y in range(2):
         up_sibling(y).wait_send()
-    sums.step(2)
     sums.finish(small_full)
+    turn(0)
 
     def keep(m):
         return pltpu.make_async_copy(g.at[m], g_out.at[m], gsem.at[m])
@@ -453,9 +462,9 @@
         save(m).start()
 
     project(0)
-    gather.tick(4)
+    turn(1)
     project(1)
-    gather.tick(5)
+    turn(2)
     project(2)
 
     pairs = width // head_pair
@@ -474,8 +483,8 @@
             term = dot(weight.astype(bf16), values * mask)
             out = term if out is None else out + term
         pool[3, spot, cols] = out.astype(bf16)
-        turn = rows * pairs // 2
-        pl.when(lax.rem(i, turn) == turn - 2)(lambda: gather.tick(6 + i // turn))
+        pl.when(i == rows * pairs // 4)(partial(turn, 3))
+        pl.when(i == rows * pairs * 3 // 4)(partial(turn, 4))
         return carry
 
     lax.fori_loop(0, rows * pairs, attend, 0)
@@ -486,13 +495,13 @@
 
     arrive(3)
     tiles(512, mix)
-    gather.tick(8)
+    turn(5)
 
     def unit(i):
         return pltpu.make_async_copy(pool.at[6], unit_out.at[i], fsem.at[i])
 
     def norm1(i, carry):
-        spot = span(i, 32)
+        spot = span(i, 64)
         normed, inverse = rms_center(hidden[spot])
         result = normed * small_full[3:4, :] + small_full[4:5, :]
         hidden[spot] = result
@@ -501,7 +510,7 @@
         inverse1[spot] = inverse
         return carry
 
-    lax.fori_loop(0, all_rows // 32, norm1, 0)
+    lax.fori_loop(0, all_rows // 64, norm1, 0)
     save(4).start()
     unit(0).start()
 
@@ -513,13 +522,12 @@
 
     unit(0).wait()
 
-    def feed(j, carry):
+    def feed(j):
         m = 4 + 2 * j
-        pl.when(j >= 1)(lambda: gather.tick(m + 3))
+        if m > 5:
+            turn(m)
         arrive(m)
-
-        @pl.when(j >= 1)
-        def _():
+        if j >= 1:
             save_act(j - 1).wait()
             save_slope(j - 1).wait()
 
@@ -531,29 +539,30 @@
         tiles(256, up)
         save_act(j).start()
         save_slope(j).start()
-        pl.when(j >= 1)(lambda: gather.tick(m + 4))
+        if m + 1 > 5:
+            turn(m + 1)
         arrive(m + 1)
 
         def back(cols, spot):
             hidden[spot, cols] = hidden[spot, cols] + dot(pool[5, spot], tile(m + 1, cols))
 
         tiles(512, back)
-        return carry
 
     blocks = (count - 4) // 2
-    lax.fori_loop(0, blocks, feed, 0)
+    for j in range(blocks):
+        feed(j)
     save_act(blocks - 1).wait()
     save_slope(blocks - 1).wait()
 
     def norm2(i, carry):
-        spot = span(i, 32)
+        spot = span(i, 64)
         normed, inverse = rms_center(hidden[spot] + small_full[5:6, :])
         pool[5, spot] = (normed * small_full[6:7, :] + small_full[7:8, :]).astype(bf16)
         pool[6, spot] = normed.astype(bf16)
         inverse2[spot] = inverse
         return carry
 
-    lax.fori_loop(0, all_rows // 32, norm2, 0)
+    lax.fori_loop(0, all_rows // 64, norm2, 0)
     finish = pltpu.make_async_copy(pool.at[5], final_out, fsem.at[2])
     finish.start()
     unit(1).start()
@@ -567,7 +576,8 @@
     for i in range(5):
         save(i).wait()
     up_own.wait()
-    up_across().wait()
+    for i in range(pieces):
+        up_across(i).wait()
     finish.wait()
     unit(1).wait()
 
@@ -612,8 +622,10 @@
             dma((count, nz + 4)),
             dma((2 + nz,)),
             dma((2 + nz,)),
-            dma((3,)),
-            dma((3,)),
+            dma((2,)),
+            dma((2,)),
+            dma((count,)),
+            dma((count,)),
             dma((slots.shape[0] + 1,)),
             dma((count,)),
             dma((5,)),
@@ -632,7 +644,7 @@
     x, own_up, across_up, final, unit, inverse1, inverse2, small_full, act, slope, saved, g,
     out, small_out, input_out, table,
     rc, r3a, r3b, r2, rz, send, recv, total, landing, ssend, srecv,
-    term, weight, pool, hidden, wsem, psem, hsem, tsend, trecv, tsem,
+    term, weight, pool, hidden, wsem, psem, hsem, tsend, trecv, across_send, across_recv, tsem,
 ):
     f32, bf16 = jnp.float32, jnp.bfloat16
     count = out.shape[0]
@@ -645,9 +657,15 @@
 
     here = pltpu.make_async_copy(final, table.at[at.y, at.core], tsem)
     to_sibling = remote(final, table.at[at.y, at.core], tsend.at[0], trecv.at[0], at.sibling)
-    to_across = remote(final, table.at[at.y, at.core], tsend.at[1], trecv.at[1], at.across_y)
+    pieces = across_send.shape[0]
+
+    def to_across(i):
+        piece = pl.ds(i * (all_rows // pieces), all_rows // pieces)
+        dst = table.at[at.y, at.core, piece]
+        return remote(final.at[piece], dst, across_send.at[i], across_recv.at[i], at.across_y)
+
     passed = table.at[1 - at.y, at.core]
-    pass_on = remote(passed, passed, tsend.at[2], trecv.at[2], at.sibling)
+    pass_on = remote(passed, passed, tsend.at[1], trecv.at[1], at.sibling)
 
     def load(src, entry, i):
         return pltpu.make_async_copy(src, pool.at[entry], psem.at[i])
@@ -673,7 +691,7 @@
     )
     for copy in (unit2, own_load, across_load, act_load[0], down_fetch[0], up_fetch[0], slope_load[0], low_load):
         copy.start()
-    to_across.start()
+    to_across(0).start()
     to_sibling.start()
     here.start()
     total[0] = jnp.zeros_like(total[0])
@@ -683,7 +701,7 @@
 
     def norm_back(gain_row, shift_row, low_row, inverse, incoming, normed_entry, low_entry):
         def body(i, carry):
-            spot = span(i, 32)
+            spot = span(i, 64)
             grad, normed = incoming(spot), pool[normed_entry, spot].astype(f32)
             scaled = grad * small_full[gain_row : gain_row + 1, :]
             inner = (
@@ -698,7 +716,7 @@
             return tuple(c + folded(b) for c, b in zip(carry, (grad * normed, grad, low.astype(f32))))
 
         zero = jnp.zeros((8, width), f32)
-        found = lax.fori_loop(0, all_rows // 32, body, (zero, zero, zero))
+        found = lax.fori_loop(0, all_rows // 64, body, (zero, zero, zero))
         for row, value in zip((gain_row, shift_row, low_row), found):
             total[0, row : row + 1, :] = jnp.sum(value, axis=0, keepdims=True)
 
@@ -734,15 +752,12 @@
             scatter.step1(m - 1, own_half(1 - slot))
         half(at.core)
 
-    def tick(i):
-        for step, ahead in ((scatter.step4, 2), (scatter.step3, 1), (scatter.step2, 0)):
-            m = i - ahead
-            call = partial(step, m) if ahead < 2 else partial(step, m, out)
-            if isinstance(i, int):
-                if 0 <= m < count:
-                    call()
-            else:
-                pl.when((m >= 0) & (m < count))(call)
+    def turn(m):
+        for step, behind in ((scatter.step4, 4), (scatter.step3, 2), (scatter.step2, 0)):
+            if 0 <= m - behind < count:
+                step(*((m - behind, out) if behind == 4 else (m - behind,)))
+        if 0 < m + 1 < pieces:
+            to_across(m + 1).start()
 
     for copy in (unit2, own_load, across_load):
         copy.wait()
@@ -759,7 +774,7 @@
             slope_load[j].start()
         else:
             unit1.start()
-    tick(0)
+    turn(0)
 
     low_load.wait()
     for j in range(blocks):
@@ -792,7 +807,7 @@
             query_fetch.start()
         if j == blocks - 1:
             value_load.start()
-        tick(1 + j)
+        turn(1 + j)
 
     unit1.wait()
     norm_back(3, 4, 2, inverse1, lambda spot: hidden[spot], 5, 0)
@@ -808,7 +823,7 @@
     key_fetch.start()
     for copy in (query_load, key_load, value_load):
         copy.wait()
-    tick(5)
+    turn(5)
     scatter.step1(2 * blocks, own_half((2 * blocks) % 2))
 
     pairs = width // head_pair
@@ -843,8 +858,8 @@
         for row, value in ((0, query_grad), (1, value_grad)):
             found = jnp.sum(value.astype(f32), axis=0, keepdims=True)
             total[0, row : row + 1, cols] = total[0, row : row + 1, cols] + found
-        turn = rows * pairs // 3
-        pl.when(lax.rem(i, turn) == turn - 1)(lambda: tick(6 + i // turn))
+        for third in range(3):
+            pl.when(i == (2 * third + 1) * rows * pairs // 6)(partial(turn, 6 + third))
         return carry
 
     lax.fori_loop(0, rows * pairs, attend, 0)
@@ -855,7 +870,7 @@
         produce(2 * blocks + 1 + i, 4, entry, i > 0)
         sums.step(i)
     scatter.step1(count - 1, own_half((count - 1) % 2))
-    tick(9)
+    turn(9)
 
     def input_back(slot, entry, fetched):
         def body(n, cols, spot):
@@ -866,17 +881,20 @@
 
     input_back(1, 2, query_fetch)
     value_fetch.start()
-    tick(10)
+    turn(10)
     input_back(0, 3, key_fetch)
-    to_across.wait_recv()
+    for i in range(pieces):
+        to_across(i).wait_recv()
     pass_on.start()
-    tick(11)
+    turn(11)
     input_back(1, 6, value_fetch)
     done = pltpu.make_async_copy(hidden, input_out, hsem)
     done.start()
-    tick(12)
+    turn(12)
+    turn(13)
     sums.finish(small_out)
-    tick(13)
+    turn(14)
+    turn(15)
     done.wait()
 
     def drain(m, carry):
@@ -886,7 +904,8 @@
     lax.fori_loop(0, count, drain, 0)
     here.wait()
     to_sibling.wait()
-    to_across.wait_send()
+    for i in range(pieces):
+        to_across(i).wait_send()
     pass_on.wait()
 
 
@@ -919,8 +938,10 @@
             dma((count,)),
             dma((18,)),
             dma,
-            dma((3,)),
-            dma((3,)),
+            dma((2,)),
+            dma((2,)),
+            dma((count,)),
+            dma((count,)),
             dma,
         ],
         compiler_params=pltpu.CompilerParams(

time: 450 us -> 366 us (0.81)
  Pallas kernels: 418 us -> 334 us
    pallas_call x1, Pallas kernels: 210 us -> 159 us  [forward(): pl.pallas_call(partial(forward_kernel, nz, nx, wide, tokens, 2 * width //...]
    pallas_call x1, Pallas kernels: 201 us -> 170 us  [backward(): pl.pallas_call(partial(backward_kernel, nz, nx, wide, tokens, 2 * width /...]
where the time goes in v4:
time: 366 us; the launch traced here: 365 us
  Pallas kernels  334 us (91%)
  local copies, waits for them, and re-layouts  23.9 us (7%)
  other arithmetic  5.56 us (2%)
    pallas_call x1, Pallas kernels, backward(): pl.pallas_call(partial(backward_kernel, nz, nx, wide, tokens, 2 * width /...  170 us
    pallas_call x1, Pallas kernels, forward(): pl.pallas_call(partial(forward_kernel, nz, nx, wide, tokens, 2 * width //...  159 us

profile of v4, /device:TPU:0, one launch (start us, length us, event | category | flops | bytes accessed | tf_op | source)
XLA Modules:
  0.0 365.1 jit_solution(17655845660031820380)
XLA Ops:
  0.7 0.8 reshape.72
  1.5 0.8 concatenate.7
  2.3 0.6 dynamic_update_slice.3.small
  2.9 0.9 bitcast_dynamic-update-slice_fusion.3
  3.7 0.8 bitcast_dynamic-update-slice_fusion.2
  4.6 0.8 bitcast_dynamic-update-slice_fusion.1
  5.4 0.8 bitcast_dynamic-update-slice_fusion
  6.3 1.7 reshape.70
  8.0 0.2 copy.36
  8.2 1.1 stack_reshape.6
  9.4 0.6 fusion.pick
  10.0 0.2 copy-done
  10.3 158.8 %shard_map.314 = (bf16[12,2,2,4,2,32,1024]{6,5,4,3,2,1,0:T(8,128)(2,1)}, bf16[5,960,1024]{2,1,0:T(8,128)(2,1)}, bf16[4,960,1024]{2,1,0:T(8,128)(2,1)}, bf16[4,96...) custom-call(bf16[960,1024]{1,0:T(8,128)(2,1)} %bitcast.56, ...), custom_call_target="tpu_custom_call" | custom-call | tf_op jit(solution)/shard_map/pallas_call | solution.py:598
  169.0 169.7 %shard_map.315 = (f32[12,32,1024]{2,1,0:T(8,128)}, f32[16,1024]{1,0:T(8,128)}, f32[960,1024]{1,0:T(8,128)}, bf16[2,2,960,1024]{3,2,1,0:T(8,128)(2,1)}) custom-call(bf16[960,1024]{1,0:T(8,128)(2,1)} %bitcast.57, bf16[960,1024]{1,0:T(8,128)(2,1)} %get-tuple-element.32.own_up, bf16[960,1024]{1,0:T(8,128)(2,1)} %get-tuple-element.33.across_up, ...), custom_call_target="tpu_custom_call" | custom-call | tf_op jit(solution)/shard_map/pallas_call | solution.py:921
  338.8 2.1 fusion.1
  340.9 0.7 reshape.75
  341.6 3.1 copy.38
  344.7 4.4 %reshape.76 = f32[32,4096]{1,0:T(8,128)} reshape(f32[32,32,4,32]{3,2,1,0:T(4,128)} %copy.38) | data formatting | bytes 1048576 | tf_op jit(solution)/shard_map/reshape | solution.py:1040
  349.8 4.9 %broadcast_select_fusion = f32[3,320,1024]{2,1,0:T(8,128)} fusion(f32[3,320,1024]{2,1,0:T(8,128)} %bitcast.59, pred[3]{0:T(512)(128)(4,1)S(1)} %iota_compare_fusion.1), kind=kLoop, calls=%fused_computation | loop fusion | flops 983040 | bytes 7864323 | tf_op jit(solution)/shard_map/jit(_where)/select_n | solution.py:1034
  354.6 5.7 %shard_map.316 = bf16[6,320,1024]{2,1,0:T(8,128)(2,1)} custom-call(s32[6]{0:T(128)} %slot_row.1, bf16[12,320,1024]{2,1,0:T(8,128)(2,1)} %bitcast.55), custom_call_target="tpu_custom_call" | custom-call | tf_op jit(solution)/shard_map/pallas_call | solution.py:960
  360.3 1.9 slice_bitcast_fusion
  362.2 1.6 dynamic-slice_bitcast_fusion
  363.8 0.7 dynamic-slice.5
  364.6 0.6 reshape.77
  (12 shorter events, 0.1 us)
Async XLA Ops:
  0.7 8.6 %copy-start.2 = (bf16[128,1024]{1,0:T(8,128)(2,1)S(1)}, bf16[128,1024]{1,0:T(8,128)(2,1)}, u32[]{:S(2)}) copy-start(bf16[128,1024]{1,0:T(8,128)(2,1)} %param.34) | copy-start | bytes 786436
  0.7 8.7 %copy-start.3 = (s32[6]{0:T(128)S(1)}, s32[6]{0:T(128)}, u32[]{:S(2)}) copy-start(s32[6]{0:T(128)} %slot_row.1) | copy-start | bytes 76
  2.9 7.2 %copy-start.1 = (f32[16,1024]{1,0:T(8,128)}, f32[16,1024]{1,0:T(8,128)S(1)}, u32[]{:S(2)}) copy-start(f32[16,1024]{1,0:T(8,128)S(1)} %dynamic_update_slice.3.small) | copy-start | bytes 196612
  9.4 0.9 copy-start

commit v5 on v4

--- a/solution.py
+++ b/solution.py
@@ -61,47 +61,74 @@
 
 
 class Scatter:
-    def __init__(self, at, wide, rc, r3a, r3b, r2, rz, send, recv):
-        self.at, self.wide = at, wide
+    def __init__(self, at, parts, rc, r3a, r3b, r2, rz, rcz, rcx, rcy, send, recv):
+        self.at, self.parts = at, parts
         self.rc, self.r3a, self.r3b, self.r2, self.rz = rc, r3a, r3b, r2, rz
+        self.rcz, self.rcx, self.rcy = rcz, rcx, rcy
         self.send, self.recv = send, recv
 
+    def copy(self, m, i, src, dst, to):
+        return remote(src, dst, self.send.at[m, i], self.recv.at[m, i], to)
+
     def to_sibling(self, m, theirs):
-        return remote(theirs, self.rc.at[m], self.send.at[m, 0], self.recv.at[m, 0], self.at.sibling)
-
-    def first_a(self, m):
-        at, wide = self.at, self.wide
-        src = self.rc.at[m, :, :, 1 - at.x, :, pl.ds(0, wide)]
-        return remote(src, self.r3a.at[m], self.send.at[m, 1], self.recv.at[m, 1], at.across_x)
-
-    def first_b(self, m):
-        at, wide = self.at, self.wide
-        src = self.rc.at[m, 1 - at.y, :, :, :, pl.ds(wide, self.rc.shape[-1] - wide)]
-        return remote(src, self.r3b.at[m], self.send.at[m, 2], self.recv.at[m, 2], at.across_y)
-
-    def second_a(self, m):
-        at, wide = self.at, self.wide
-        src, dst = self.r3a.at[m, 1 - at.y], self.r2.at[m, :, :, pl.ds(0, wide)]
-        return remote(src, dst, self.send.at[m, 3], self.recv.at[m, 3], at.across_y)
-
-    def second_b(self, m):
-        at, wide = self.at, self.wide
-        src = self.r3b.at[m, :, 1 - at.x]
-        dst = self.r2.at[m, :, :, pl.ds(wide, self.r2.shape[-1] - wide)]
-        return remote(src, dst, self.send.at[m, 4], self.recv.at[m, 4], at.across_x)
-
-    def last(self, m, k):
-        at = self.at
-        src = self.r2.at[m, lax.rem(at.z + k, at.nz)]
-        return remote(src, self.rz.at[m, k - 1], self.send.at[m, 4 + k], self.recv.at[m, 4 + k], at.along_z[k - 1])
+        return self.copy(m, 0, theirs, self.rc.at[m], self.at.sibling)
+
+    def landings(self, m):
+        a, b, c, _ = self.parts[m]
+        a, b, c = (pl.ds(0, part.size) for part in (a, b, c))
+        return (
+            self.r3a.at[m, :, :, :, a],
+            self.r3b.at[m, :, :, :, b],
+            self.rcz.at[m, :, :, :, :, c],
+            self.rcx.at[m, :, :, c],
+            self.rcy.at[m, :, c],
+        )
+
+    def firsts(self, m):
+        at, rc, nz = self.at, self.rc, self.at.nz
+        a, b, c, _ = self.parts[m]
+        r3a, r3b, rcz, _, _ = self.landings(m)
+        return [
+            self.copy(m, 1, rc.at[m, :, :, 1 - at.x, :, a], r3a, at.across_x),
+            self.copy(m, 2, rc.at[m, 1 - at.y, :, :, :, b], r3b, at.across_y),
+        ] + [
+            self.copy(
+                m, 2 + k, rc.at[m, :, lax.rem(at.z + k, nz), :, :, c], rcz.at[k - 1], at.along_z[k - 1]
+            )
+            for k in range(1, nz)
+        ]
+
+    def seconds(self, m):
+        at, nz = self.at, self.at.nz
+        a, b, _, _ = self.parts[m]
+        r3a, r3b, rcz, rcx, _ = self.landings(m)
+        return [
+            self.copy(m, nz + 2, r3a.at[1 - at.y], self.r2.at[m, :, :, a], at.across_y),
+            self.copy(m, nz + 3, r3b.at[:, 1 - at.x], self.r2.at[m, :, :, b], at.across_x),
+            self.copy(m, nz + 4, rcz.at[0, :, 1 - at.x], rcx, at.across_x),
+        ]
+
+    def thirds(self, m):
+        at, nz = self.at, self.at.nz
+        ab = self.parts[m][3]
+        rcx, rcy = self.landings(m)[3:]
+        return [
+            self.copy(
+                m,
+                nz + 4 + k,
+                self.r2.at[m, lax.rem(at.z + k, nz), :, ab],
+                self.rz.at[m, k - 1, :, ab],
+                at.along_z[k - 1],
+            )
+            for k in range(1, nz)
+        ] + [self.copy(m, 2 * nz + 4, rcx.at[1 - at.y], rcy, at.across_y)]
 
     def start(self, m, theirs):
         self.to_sibling(m, theirs).start()
 
     def step1(self, m, own):
-        at, rc = self.at, self.rc
+        rc, nz = self.rc, self.at.nz
         self.to_sibling(m, rc.at[m]).wait_recv()
-        nz = at.nz
 
         def add(i, carry):
             y, z = i // nz, lax.rem(i, nz)
@@ -110,54 +137,58 @@
 
         lax.fori_loop(0, rc.shape[1] * nz, add, 0)
         self.to_sibling(m, rc.at[m]).wait_send()
-        self.first_a(m).start()
-        self.first_b(m).start()
+        for copy in self.firsts(m):
+            copy.start()
 
     def step2(self, m):
-        at, rc, wide, r3a, r3b = self.at, self.rc, self.wide, self.r3a, self.r3b
-        columns = rc.shape[-1]
-        self.first_a(m).wait_recv()
-        self.first_b(m).wait_recv()
+        at, rc = self.at, self.rc
+        a, b, c, _ = self.parts[m]
+        r3a, r3b, rcz, _, _ = self.landings(m)
+        for copy in self.firsts(m):
+            copy.wait_recv()
 
         def add(z, carry):
             for y in range(rc.shape[1]):
-                r3a[m, y, z] = added(r3a[m, y, z], rc[m, y, z, at.x, :, pl.ds(0, wide)]).astype(rc.dtype)
-            r3b[m, z] = added(r3b[m, z], rc[m, at.y, z, :, :, pl.ds(wide, columns - wide)]).astype(rc.dtype)
+                r3a[y, z] = added(r3a[y, z], rc[m, y, z, at.x, :, a]).astype(rc.dtype)
+            r3b[z] = added(r3b[z], rc[m, at.y, z, :, :, b]).astype(rc.dtype)
             return carry
 
         lax.fori_loop(0, at.nz, add, 0)
-        self.second_a(m).start()
-        self.second_b(m).start()
+        others = [rcz[k] for k in range(at.nz - 1)]
+        rcz[0] = added(rc[m, :, at.z, :, :, c], *others).astype(rc.dtype)
+        for copy in self.seconds(m):
+            copy.start()
 
     def step3(self, m):
-        at, r3a, r3b, r2, wide = self.at, self.r3a, self.r3b, self.r2, self.wide
-        columns = r2.shape[-1]
-        self.second_a(m).wait_recv()
-        self.second_b(m).wait_recv()
+        at, r2 = self.at, self.r2
+        a, b, _, _ = self.parts[m]
+        r3a, r3b, rcz, rcx, _ = self.landings(m)
+        for copy in self.seconds(m):
+            copy.wait_recv()
 
         def add(z, carry):
-            left, right = pl.ds(0, wide), pl.ds(wide, columns - wide)
-            r2[m, z, :, left] = added(r2[m, z, :, left], r3a[m, at.y, z]).astype(r2.dtype)
-            r2[m, z, :, right] = added(r2[m, z, :, right], r3b[m, z, at.x]).astype(r2.dtype)
+            r2[m, z, :, a] = added(r2[m, z, :, a], r3a[at.y, z]).astype(r2.dtype)
+            r2[m, z, :, b] = added(r2[m, z, :, b], r3b[z, at.x]).astype(r2.dtype)
             return carry
 
         lax.fori_loop(0, at.nz, add, 0)
-        for k in range(1, at.nz):
-            self.last(m, k).start()
+        rcx[...] = added(rcx[...], rcz[0, :, at.x]).astype(r2.dtype)
+        for copy in self.thirds(m):
+            copy.start()
 
     def step4(self, m, out):
         at = self.at
-        for k in range(1, at.nz):
-            self.last(m, k).wait_recv()
-        out[m] = added(self.r2[m, at.z], *[self.rz[m, k] for k in range(at.nz - 1)])
+        _, _, c, ab = self.parts[m]
+        rcx, rcy = self.landings(m)[3:]
+        for copy in self.thirds(m):
+            copy.wait_recv()
+        others = [self.rz[m, k, :, ab] for k in range(at.nz - 1)]
+        out[m, :, ab] = added(self.r2[m, at.z, :, ab], *others)
+        out[m, :, c] = added(rcx[at.y], rcy[...])
 
     def drain(self, m):
-        self.first_a(m).wait_send()
-        self.first_b(m).wait_send()
-        self.second_a(m).wait_send()
-        self.second_b(m).wait_send()
-        for k in range(1, self.at.nz):
-            self.last(m, k).wait_send()
+        for copy in self.firsts(m) + self.seconds(m) + self.thirds(m):
+            copy.wait_send()
 
 
 class SmallSum:
@@ -200,16 +231,20 @@
             self.along(k).wait_send()
 
 
-def scatter_scratch(count, nz, nx, rows, columns, wide):
+def scatter_scratch(count, nz, nx, rows, columns, parts):
     bf16 = jnp.bfloat16
+    a, b, c = (max(part[i].size for part in parts) for i in range(3))
     return [
         pltpu.VMEM((count, 2, nz, nx, rows, columns), bf16),
-        pltpu.VMEM((count, 2, nz, rows, wide), bf16),
-        pltpu.VMEM((count, nz, nx, rows, columns - wide), bf16),
+        pltpu.VMEM((count, 2, nz, rows, a), bf16),
+        pltpu.VMEM((count, nz, nx, rows, b), bf16),
         pltpu.VMEM((count, nz, rows, columns), bf16),
         pltpu.VMEM((count, nz - 1, rows, columns), bf16),
-        pltpu.SemaphoreType.DMA((count, 4 + nz)),
-        pltpu.SemaphoreType.DMA((count, 4 + nz)),
+        pltpu.VMEM((count, nz - 1, 2, nx, rows, c), bf16),
+        pltpu.VMEM((count, 2, rows, c), bf16),
+        pltpu.VMEM((count, rows, c), bf16),
+        pltpu.SemaphoreType.DMA((count, 2 * nz + 5)),
+        pltpu.SemaphoreType.DMA((count, 2 * nz + 5)),
     ]
 
 
@@ -256,67 +291,62 @@
 
 
 class Gather:
-    def __init__(self, at, wide, count, shards, g, send, recv):
-        self.at, self.wide, self.count, self.shards, self.g, self.send, self.recv = at, wide, count, shards, g, send, recv
-        self.right = g.shape[-1] - wide
-
-    def along(self, m, k):
-        at = self.at
-        dst = self.g.at[m, at.y, at.core, at.z, at.x]
-        return remote(self.shards.at[m], dst, self.send.at[m, k - 1], self.recv.at[m, k - 1], at.along_z[k - 1])
-
-    def same(self, part, m, i, to):
-        return remote(part, part, self.send.at[m, i], self.recv.at[m, i], to)
-
-    def first_a(self, m):
-        at, nz = self.at, self.at.nz
-        part = self.g.at[m, at.y, at.core, :, at.x, :, pl.ds(0, self.wide)]
-        return self.same(part, m, nz - 1, at.across_y)
-
-    def first_b(self, m):
-        at, nz = self.at, self.at.nz
-        part = self.g.at[m, at.y, at.core, :, at.x, :, pl.ds(self.wide, self.right)]
-        return self.same(part, m, nz, at.across_x)
-
-    def second_a(self, m):
-        at, nz = self.at, self.at.nz
-        part = self.g.at[m, :, at.core, :, at.x, :, pl.ds(0, self.wide)]
-        return self.same(part, m, nz + 1, at.across_x)
-
-    def second_b(self, m):
-        at, nz = self.at, self.at.nz
-        part = self.g.at[m, at.y, at.core, :, :, :, pl.ds(self.wide, self.right)]
-        return self.same(part, m, nz + 2, at.across_y)
-
-    def to_sibling(self, m):
-        at, nz = self.at, self.at.nz
-        return self.same(self.g.at[m, :, at.core], m, nz + 3, at.sibling)
+    def __init__(self, at, parts, count, shards, g, send, recv):
+        self.at, self.count, self.shards, self.g, self.send, self.recv = at, count, shards, g, send, recv
+        self.parts = parts
+
+    def copy(self, m, i, src, dst, to):
+        return remote(src, dst, self.send.at[m, i], self.recv.at[m, i], to)
+
+    def same(self, m, i, part, to):
+        return self.copy(m, i, part, part, to)
+
+    def stages(self, m):
+        at, g, nz = self.at, self.g, self.at.nz
+        a, b, c, ab = self.parts[m]
+        y, core, z, x = at.y, at.core, at.z, at.x
+        across_x, across_y, along_z = at.across_x, at.across_y, at.along_z
+        first = [
+            self.copy(m, k, self.shards.at[m, :, ab], g.at[m, y, core, z, x, :, ab], along_z[k])
+            for k in range(nz - 1)
+        ]
+        first.append(self.copy(m, nz - 1, self.shards.at[m, :, c], g.at[m, y, core, z, x, :, c], across_y))
+        second = [
+            self.same(m, nz, g.at[m, y, core, :, x, :, a], across_y),
+            self.same(m, nz + 1, g.at[m, y, core, :, x, :, b], across_x),
+            self.same(m, nz + 2, g.at[m, :, core, z, x, :, c], across_x),
+        ]
+        third = [
+            self.same(m, nz + 3, g.at[m, :, core, :, x, :, a], across_x),
+            self.same(m, nz + 4, g.at[m, y, core, :, :, :, b], across_y),
+        ]
+        third += [self.same(m, nz + 5 + k, g.at[m, :, core, z, :, :, c], along_z[k]) for k in range(nz - 1)]
+        return first, second, third, [self.same(m, 2 * nz + 4, g.at[m, :, core], at.sibling)]
 
     def step0(self, m):
         at = self.at
-        for k in range(1, at.nz):
-            self.along(m, k).start()
+        for copy in self.stages(m)[0]:
+            copy.start()
         self.g[m, at.y, at.core, at.z, at.x] = self.shards[m]
 
+    def follow(self, stage, m):
+        stages = self.stages(m)
+        for copy in stages[stage - 1]:
+            copy.wait_recv()
+        for copy in stages[stage]:
+            copy.start()
+
     def step1(self, m):
-        for k in range(1, self.at.nz):
-            self.along(m, k).wait_recv()
-        self.first_a(m).start()
-        self.first_b(m).start()
+        self.follow(1, m)
 
     def step2(self, m):
-        self.first_a(m).wait_recv()
-        self.first_b(m).wait_recv()
-        self.second_a(m).start()
-        self.second_b(m).start()
+        self.follow(2, m)
 
     def step3(self, m):
-        self.second_a(m).wait_recv()
-        self.second_b(m).wait_recv()
-        self.to_sibling(m).start()
+        self.follow(3, m)
 
     def arrive(self, m):
-        self.to_sibling(m).wait_recv()
+        self.stages(m)[3][0].wait_recv()
 
     def turn(self, m):
         for step, ahead in ((self.step3, 0), (self.step2, 2), (self.step1, 4), (self.step0, 6)):
@@ -324,18 +354,27 @@
                 step(m + ahead)
 
     def drain(self, m):
-        for k in range(1, self.at.nz):
-            self.along(m, k).wait_send()
-        for copy in (self.first_a, self.first_b, self.second_a, self.second_b, self.to_sibling):
-            copy(m).wait_send()
+        for stage in self.stages(m):
+            for copy in stage:
+                copy.wait_send()
+
+
+def column_parts(width, shares):
+    lanes = 128
+    a, b = (share * lanes for share in shares)
+    return pl.ds(0, a), pl.ds(a, b), pl.ds(a + b, width - a - b), pl.ds(0, a + b)
+
+
+GATHER_SHARES = [(6, 1)] * 12
+SCATTER_SHARES = [(6, 1)] * 12
 
 
 def forward_kernel(
-    nz, nx, wide, tokens, head_pair,
-    x, shards, small, pick, slots,
-    g_out, saved, act_out, slope_out, unit_out, final_out, own_out, across_out, small_full, inverse1, inverse2,
-    g, pool, hidden, landed, total, landing,
-    send, recv, ssend, srecv, usend, urecv, across_send, across_recv, isem, gsem, vsem, asem, dsem, fsem,
+    nz, nx, parts, tokens, head_pair,
+    x, attention_weights, expand, contract, small, pick, slots,
+    g_out, probs_out, saved, act_out, slope_out, unit_out, final_out, own_out, across_out, small_full, inverse1, inverse2,
+    g, shards, pool, hidden, landed, total, landing,
+    send, recv, ssend, srecv, usend, urecv, across_send, across_recv, isem, gsem, vsem, asem, dsem, fsem, held_probs, ksem,
 ):
     f32, bf16 = jnp.float32, jnp.bfloat16
     count = g.shape[0]
@@ -343,7 +382,7 @@
     rows = all_rows // tokens
     at = Partners(nz, nx)
     at.meet()
-    gather = Gather(at, wide, count, shards, g, send, recv)
+    gather = Gather(at, parts, count, shards, g, send, recv)
     sums = SmallSum(at, total, landing, ssend, srecv)
     groups = slots.shape[0] // rows
     members = pick.shape[0] // rows
@@ -351,9 +390,13 @@
     def fetch(i):
         return pltpu.make_async_copy(slots.at[i], pool.at[i // rows, pl.ds((i % rows) * tokens, tokens)], isem.at[i])
 
-    total[0] = small[...]
+    shard = shards.shape[1]
+    lane = lax.broadcasted_iota(jnp.int32, (1, width), 1)
+    mine = lane // shard == lax.axis_index("dp") * (nz * nx) + lax.axis_index("fsdp")
+    total[0] = jnp.where(mine, jnp.concatenate([small[...]] * (width // shard), axis=1), 0.0)
     sums.start()
     for m in range(4):
+        shards[m] = attention_weights[m][...]
         gather.step0(m)
     for i in range(slots.shape[0]):
         fetch(i).start()
@@ -377,14 +420,6 @@
             pool[groups + t // rows, spot, cols] = picked.astype(bf16)
         return carry
 
-    gather.step1(0)
-    sums.step(0)
-    gather.step0(4)
-    lax.fori_loop(0, tokens // high * 2, sum_slots, 0)
-    gather.step1(1)
-    gather.step2(0)
-    sums.step(1)
-
     def up_sibling(y):
         src = pool.at[groups + y * 2 + 1 - at.core]
         return remote(src, landed.at[y], usend.at[y], urecv.at[y], at.sibling)
@@ -399,15 +434,38 @@
 
     def turn(m):
         gather.turn(m)
-        up_across(m).start()
+        if m < pieces:
+            up_across(m).start()
 
     up_own = pltpu.make_async_copy(landed.at[at.y], own_out, isem.at[slots.shape[0]])
 
+    steps = tokens // high * 2
+    lax.fori_loop(0, steps // 4, sum_slots, 0)
+    gather.step1(0)
+    sums.step(0)
+    blocks = (count - 4) // 2
+    for j in range(blocks):
+        shards[5 + 2 * j] = contract[j * shard : (j + 1) * shard, :]
+    lanes = 128
+    per = lanes // shard
+    for q in range(width // lanes):
+        natural = expand[:, q * lanes * blocks : (q + 1) * lanes * blocks].astype(f32)
+        for j in range(blocks):
+            found = [
+                natural[:, t * blocks * shard + j * shard : t * blocks * shard + (j + 1) * shard] for t in range(per)
+            ]
+            shards[4 + 2 * j, :, q * lanes : (q + 1) * lanes] = jnp.concatenate(found, axis=1).astype(bf16)
+    gather.step0(4)
+    sums.step(1)
+    lax.fori_loop(steps // 4, steps // 2, sum_slots, 0)
+    gather.step1(1)
+    gather.step2(0)
+    lax.fori_loop(steps // 2, steps, sum_slots, 0)
     for y in range(2):
         up_sibling(y).start()
+    sums.step(2)
     gather.step0(5)
     gather.step1(2)
-    sums.step(2)
     gather.step2(1)
     gather.step1(3)
     for y in range(2):
@@ -471,17 +529,24 @@
     masks = half_masks(head_pair)
     scale = (head_pair // 2) ** (-0.5)
 
+    def keep_probs(i):
+        slot = lax.rem(i, 2)
+        return pltpu.make_async_copy(held_probs.at[slot], probs_out.at[i], ksem.at[slot])
+
     def attend(i, carry):
         spot, cols = span(i // pairs, tokens), span(lax.rem(i, pairs), head_pair)
         query, keys, values = pool[0, spot, cols], pool[1, spot, cols], pool[2, spot, cols]
         query = query * jnp.asarray(scale, bf16)
+        pl.when(i >= 2)(lambda: keep_probs(i - 2).wait())
         out = None
-        for mask in masks:
-            scores = across(query, keys * mask)
-            weight = jnp.exp(scores - jnp.max(scores, axis=-1, keepdims=True))
-            weight = weight * (1.0 / jnp.sum(weight, axis=-1, keepdims=True))
-            term = dot(weight.astype(bf16), values * mask)
+        for h, mask in enumerate(masks):
+            scores = across(keys * mask, query)
+            probs = jnp.exp(scores - jnp.max(scores, axis=0, keepdims=True))
+            probs = (probs * (1.0 / jnp.sum(probs, axis=0, keepdims=True))).astype(bf16)
+            held_probs[lax.rem(i, 2), h] = probs
+            term = down(probs, values * mask)
             out = term if out is None else out + term
+        keep_probs(i).start()
         pool[3, spot, cols] = out.astype(bf16)
         pl.when(i == rows * pairs // 4)(partial(turn, 3))
         pl.when(i == rows * pairs * 3 // 4)(partial(turn, 4))
@@ -489,6 +554,8 @@
 
     lax.fori_loop(0, rows * pairs, attend, 0)
     save(3).start()
+    for i in range(2):
+        keep_probs(rows * pairs - 2 + i).wait()
 
     def mix(cols, spot):
         hidden[spot, cols] = dot(pool[3, spot], tile(3, cols)) + x[spot, cols].astype(f32) + bias(2, cols)
@@ -548,7 +615,6 @@
 
         tiles(512, back)
 
-    blocks = (count - 4) // 2
     for j in range(blocks):
         feed(j)
     save_act(blocks - 1).wait()
@@ -567,12 +633,9 @@
     finish.start()
     unit(1).start()
 
-    def drain(m, carry):
+    for m in range(count):
         gather.drain(m)
         keep(m).wait()
-        return carry
-
-    lax.fori_loop(0, count, drain, 0)
     for i in range(5):
         save(i).wait()
     up_own.wait()
@@ -582,23 +645,26 @@
     unit(1).wait()
 
 
-def forward(x, shards, small, pick, slots, nz, nx, tokens):
+def forward(x, attention_weights, expand, contract, small, pick, slots, nz, nx, tokens):
     f32, bf16 = jnp.float32, jnp.bfloat16
-    count, shard_rows, width = shards.shape
+    shard_rows, width = attention_weights[0].shape
+    count = 4 + 2 * contract.shape[0] // shard_rows
+    small_shape = (small.shape[0], width)
     all_rows = x.shape[0]
     group_members = pick.shape[0] * tokens // all_rows
     assert group_members == 4 and slots.shape[0] * tokens == 2 * all_rows
-    wide = width * 3 // 4
     vmem, anywhere = pl.BlockSpec(memory_space=pltpu.VMEM), pl.BlockSpec(memory_space=pl.ANY)
     acts = (all_rows, width)
+    rows = all_rows // tokens
     blocks = (count - 4) // 2
     dma = pltpu.SemaphoreType.DMA
     full = (count, 2, 2, nz, nx, shard_rows, width)
     out = jax.ShapeDtypeStruct
     return pl.pallas_call(
-        partial(forward_kernel, nz, nx, wide, tokens, 2 * width // HEADS),
+        partial(forward_kernel, nz, nx, [column_parts(width, s) for s in GATHER_SHARES], tokens, 2 * width // HEADS),
         out_shape=[
             out(full, bf16),
+            out((rows * HEADS // 2, 2, tokens, tokens), bf16),
             out((5, *acts), bf16),
             out((blocks, *acts), bf16),
             out((blocks, *acts), bf16),
@@ -606,20 +672,21 @@
             out(acts, bf16),
             out(acts, bf16),
             out(acts, bf16),
-            out(small.shape, f32),
+            out(small_shape, f32),
             out((all_rows, 1), f32),
             out((all_rows, 1), f32),
         ],
-        in_specs=[vmem, vmem, vmem, pl.BlockSpec(memory_space=pltpu.SMEM), anywhere],
-        out_specs=[anywhere] * 8 + [vmem] * 3,
+        in_specs=[vmem, [vmem] * 4, vmem, vmem, vmem, pl.BlockSpec(memory_space=pltpu.SMEM), anywhere],
+        out_specs=[anywhere] * 9 + [vmem] * 3,
         scratch_shapes=[
             pltpu.VMEM(full, bf16),
+            pltpu.VMEM((count, shard_rows, width), bf16),
             pltpu.VMEM((7, *acts), bf16),
             pltpu.VMEM(acts, f32),
             pltpu.VMEM((2, *acts), bf16),
-            *small_scratch(nz, small.shape)[:2],
-            dma((count, nz + 4)),
-            dma((count, nz + 4)),
+            *small_scratch(nz, small_shape)[:2],
+            dma((count, 2 * nz + 5)),
+            dma((count, 2 * nz + 5)),
             dma((2 + nz,)),
             dma((2 + nz,)),
             dma((2,)),
@@ -632,19 +699,21 @@
             dma,
             dma,
             dma((3,)),
+            pltpu.VMEM((2, 2, tokens, tokens), bf16),
+            dma((2,)),
         ],
         compiler_params=pltpu.CompilerParams(
             collective_id=1, has_side_effects=True, vmem_limit_bytes=60 * 2**20
         ),
-    )(x, shards, small, pick, slots)
+    )(x, attention_weights, expand, contract, small, pick, slots)
 
 
 def backward_kernel(
-    nz, nx, wide, tokens, head_pair,
-    x, own_up, across_up, final, unit, inverse1, inverse2, small_full, act, slope, saved, g,
+    nz, nx, parts, tokens, head_pair,
+    x, own_up, across_up, final, unit, inverse1, inverse2, small_full, act, slope, saved, g, probs,
     out, small_out, input_out, table,
-    rc, r3a, r3b, r2, rz, send, recv, total, landing, ssend, srecv,
-    term, weight, pool, hidden, wsem, psem, hsem, tsend, trecv, across_send, across_recv, tsem,
+    rc, r3a, r3b, r2, rz, rcz, rcx, rcy, send, recv, total, landing, ssend, srecv,
+    term, weight, pool, hidden, wsem, psem, hsem, tsend, trecv, across_send, across_recv, tsem, held_probs, ksem,
 ):
     f32, bf16 = jnp.float32, jnp.bfloat16
     count = out.shape[0]
@@ -652,7 +721,7 @@
     rows = all_rows // tokens
     at = Partners(nz, nx)
     at.meet()
-    scatter = Scatter(at, wide, rc, r3a, r3b, r2, rz, send, recv)
+    scatter = Scatter(at, parts, rc, r3a, r3b, r2, rz, rcz, rcx, rcy, send, recv)
     sums = SmallSum(at, total, landing, ssend, srecv)
 
     here = pltpu.make_async_copy(final, table.at[at.y, at.core], tsem)
@@ -830,22 +899,29 @@
     masks = half_masks(head_pair)
     scale = (head_pair // 2) ** (-0.5)
 
+    def fetch_probs(i):
+        slot = lax.rem(i, 2)
+        return pltpu.make_async_copy(probs.at[i], held_probs.at[slot], ksem.at[slot])
+
+    fetch_probs(0).start()
+
     def attend(i, carry):
+        pl.when(i + 1 < rows * pairs)(lambda: fetch_probs(i + 1).start())
+        fetch_probs(i).wait()
         spot, cols = span(i // pairs, tokens), span(lax.rem(i, pairs), head_pair)
         query, keys, values, mixed_grad = (pool[e, spot, cols] for e in (2, 3, 6, 1))
         query_grad = key_grad = value_grad = None
-        for mask in masks:
+        for h, mask in enumerate(masks):
             own_keys = keys * (mask * jnp.asarray(scale, bf16))
-            scores = across(own_keys, query)
-            probs = jnp.exp(scores - jnp.max(scores, axis=0, keepdims=True))
-            probs = probs * (1.0 / jnp.sum(probs, axis=0, keepdims=True))
+            low = held_probs[lax.rem(i, 2), h]
+            prob = low.astype(f32)
             prob_grad = across(values * mask, mixed_grad)
-            weighed = probs * prob_grad
-            score_grad = (weighed - probs * jnp.sum(weighed, axis=0, keepdims=True)).astype(bf16)
+            weighed = prob * prob_grad
+            score_grad = (weighed - prob * jnp.sum(weighed, axis=0, keepdims=True)).astype(bf16)
             terms = (
                 down(score_grad, own_keys),
                 dot(score_grad, query * mask),
-                dot(probs.astype(bf16), mixed_grad * mask),
+                dot(low, mixed_grad * mask),
             )
             if query_grad is None:
                 query_grad, key_grad, value_grad = terms
@@ -897,11 +973,8 @@
     turn(15)
     done.wait()
 
-    def drain(m, carry):
+    for m in range(count):
         scatter.drain(m)
-        return carry
-
-    lax.fori_loop(0, count, drain, 0)
     here.wait()
     to_sibling.wait()
     for i in range(pieces):
@@ -909,27 +982,29 @@
     pass_on.wait()
 
 
-def backward(x, own_up, across_up, final, unit, inverse1, inverse2, small_full, act, slope, saved, g, nz, nx, tokens):
+def backward(
+    x, own_up, across_up, final, unit, inverse1, inverse2, small_full, act, slope, saved, g, probs, nz, nx, tokens
+):
     f32, bf16 = jnp.float32, jnp.bfloat16
     count, _, _, _, _, shard_rows, width = g.shape
     acts = x.shape
-    wide = width * 3 // 4
+    parts = [column_parts(width, s) for s in SCATTER_SHARES]
     vmem, anywhere = pl.BlockSpec(memory_space=pltpu.VMEM), pl.BlockSpec(memory_space=pl.ANY)
     dma = pltpu.SemaphoreType.DMA
     out = jax.ShapeDtypeStruct
     block = (2, 2, nz, nx, shard_rows, width)
     return pl.pallas_call(
-        partial(backward_kernel, nz, nx, wide, tokens, 2 * width // HEADS),
+        partial(backward_kernel, nz, nx, parts, tokens, 2 * width // HEADS),
         out_shape=[
             out((count, shard_rows, width), f32),
             out(small_full.shape, f32),
             out(acts, f32),
             out((2, 2, *acts), bf16),
         ],
-        in_specs=[anywhere] * 5 + [vmem] * 3 + [anywhere] * 4,
+        in_specs=[anywhere] * 5 + [vmem] * 3 + [anywhere] * 5,
         out_specs=[vmem, vmem, anywhere, anywhere],
         scratch_shapes=[
-            *scatter_scratch(count, nz, nx, shard_rows, width, wide),
+            *scatter_scratch(count, nz, nx, shard_rows, width, parts),
             *small_scratch(nz, small_full.shape),
             pltpu.VMEM((2, *block), bf16),
             pltpu.VMEM((2, *block), bf16),
@@ -943,51 +1018,95 @@
             dma((count,)),
             dma((count,)),
             dma,
+            pltpu.VMEM((2, 2, tokens, tokens), bf16),
+            dma((2,)),
         ],
         compiler_params=pltpu.CompilerParams(
             collective_id=2, has_side_effects=True, vmem_limit_bytes=60 * 2**20
         ),
-    )(x, own_up, across_up, final, unit, inverse1, inverse2, small_full, act, slope, saved, g)
-
-
-def pick_kernel(slot_row, row, out):
-    out[...] = row[...]
-
-
-def pick_rows(slot_row, table):
+    )(x, own_up, across_up, final, unit, inverse1, inverse2, small_full, act, slope, saved, g, probs)
+
+
+def finish_kernel(
+    slot_row, live_count, me, table, full, sums, small_sums,
+    slot_acts, input_grad, query, keys, values, output, up, contract, *small,
+):
+    s = pl.program_id(0)
+    slot_acts[...] = table[...]
+    input_grad[...] = jnp.where(s // 2 < live_count[0], full[...], 0.0)
+
+    @pl.when(s == 0)
+    def _():
+        blocks = (sums.shape[0] - 4) // 2
+        shard, width = query.shape
+        for j in range(blocks):
+            contract[j * shard : (j + 1) * shard, :] = sums[j]
+        lanes = 128
+        per = lanes // shard
+        for q in range(width // lanes):
+            part = [sums[blocks + j, :, q * lanes : (q + 1) * lanes] for j in range(blocks)]
+            for t in range(per):
+                found = jnp.concatenate([p[:, t * shard : (t + 1) * shard] for p in part], axis=1)
+                at = (q * per + t) * blocks * shard
+                up[:, at : at + blocks * shard] = found
+        for i, ref in enumerate((output, values, query, keys)):
+            ref[...] = sums[2 * blocks + i]
+        own = pltpu.roll(small_sums[...], width - me[0] * shard, 1)
+        for i in range(8):
+            small[i][...] = own[i, :shard]
+        small[8][...] = jnp.concatenate([own[8 + j : 9 + j, :shard] for j in range(blocks)], axis=1)[0]
+
+
+def finish(slot_row, live_count, table, full, sums, small_sums):
+    f32 = jnp.float32
     members, tokens, width = table.shape
-    block = (1, tokens, width)
+    slots, rows = slot_row.shape[0], full.shape[0]
+    assert slots == 2 * rows
+    count, shard, _ = sums.shape
+    blocks = (count - 4) // 2
+    me = lax.axis_index(("dp", "fsdp")).astype(jnp.int32).reshape(1)
+    block, half = (1, tokens, width), (1, tokens // 2, width)
+
+    def fixed(shape):
+        return pl.BlockSpec(shape, lambda s, *_: (0,) * len(shape))
+
+    fixed_outs = [(shard, width)] * 4 + [(shard, blocks * width), (blocks * shard, width)]
+    fixed_outs += [(shard,)] * 8 + [(blocks * shard,)]
+    row_half = pl.BlockSpec(half, lambda s, *_: (s // 2, lax.rem(s, 2), 0))
+    out = jax.ShapeDtypeStruct
     return pl.pallas_call(
-        pick_kernel,
-        out_shape=jax.ShapeDtypeStruct((slot_row.shape[0], tokens, width), table.dtype),
+        finish_kernel,
+        out_shape=[
+            out((slots, tokens, width), table.dtype),
+            out(full.shape, f32),
+            *(out(shape, f32) for shape in fixed_outs),
+        ],
         grid_spec=pltpu.PrefetchScalarGridSpec(
-            num_scalar_prefetch=1,
-            grid=(slot_row.shape[0],),
-            in_specs=[pl.BlockSpec(block, lambda s, slot_row: (jnp.clip(slot_row[s], 0, members - 1), 0, 0))],
-            out_specs=pl.BlockSpec(block, lambda s, slot_row: (s, 0, 0)),
+            num_scalar_prefetch=3,
+            grid=(slots,),
+            in_specs=[
+                pl.BlockSpec(block, lambda s, slot_row, *_: (jnp.clip(slot_row[s], 0, members - 1), 0, 0)),
+                row_half,
+                fixed(sums.shape),
+                fixed(small_sums.shape),
+            ],
+            out_specs=[
+                pl.BlockSpec(block, lambda s, *_: (s, 0, 0)),
+                row_half,
+                *(fixed(shape) for shape in fixed_outs),
+            ],
         ),
-    )(slot_row, table)
-
-
-def prepare(
-    rows_in, slot_row, weights, small_parameters, up_bias, dp_size
-):
-    row_count, token_count, width = rows_in.shape
-    query_weight, key_weight, value_weight, output_weight, expand_weight, down_weight = weights
-    shard = query_weight.shape[0]
-    blocks = down_weight.shape[0] // shard
-    me = lax.axis_index(("dp", "fsdp"))
-    ups = expand_weight.reshape(shard, -1, blocks, shard).transpose(2, 0, 1, 3).reshape(blocks, shard, width)
-    downs = down_weight.reshape(blocks, shard, width)
-    paired = jnp.stack([ups, downs], axis=1).reshape(2 * blocks, shard, width)
-    shards = jnp.concatenate([jnp.stack([query_weight, key_weight, value_weight, output_weight]), paired])
-    mine = jnp.concatenate([jnp.stack(small_parameters), up_bias.reshape(blocks, shard)]).astype(jnp.float32)
-    small = lax.dynamic_update_slice(
-        jnp.zeros((16, width), jnp.float32), mine, (jnp.int32(0), me * shard)
-    )
+        compiler_params=pltpu.CompilerParams(vmem_limit_bytes=60 * 2**20),
+    )(slot_row, live_count, me, table, full, sums, small_sums)
+
+
+def prepare(slot_row, small_parameters, up_bias, row_count, dp_size):
+    shard = small_parameters[0].shape[0]
+    rows = [v.reshape(-1, shard) for v in (*small_parameters, up_bias)]
+    rows = jnp.concatenate(rows, axis=0).astype(jnp.float32)
+    small = jnp.pad(rows, ((0, 16 - rows.shape[0]), (0, 0)))
     wanted = lax.broadcasted_iota(jnp.int32, (row_count * dp_size, slot_row.shape[0]), 0)
-    pick = (wanted == slot_row[None, :]).astype(jnp.float32)
-    return rows_in.reshape(-1, width), shards, small, pick
+    return small, (wanted == slot_row[None, :]).astype(jnp.float32)
 
 
 def on_device_kernels(
@@ -1012,51 +1131,66 @@
     ffn_shift,
 ):
     row_count, token_count, width = rows_in.shape
-    shard = query_weight.shape[0]
     nx = 2
     nz = lax.axis_size("fsdp") // nx
-    x, shards, small, pick = prepare(
-        rows_in,
+    small, pick = prepare(
         slot_row,
-        (query_weight, key_weight, value_weight, output_weight, expand_weight, down_weight),
         (query_bias, value_bias, output_bias, attn_gain, attn_shift, down_bias, ffn_gain, ffn_shift),
         up_bias,
+        row_count,
         lax.axis_size("dp"),
     )
-    g, saved, act, slope, unit, final, own_up, across_up, small_full, inverse1, inverse2 = forward(
-        x, shards, small, pick, slot_activation_gradient, nz, nx, token_count
+    x = rows_in.reshape(-1, width)
+    g, probs, saved, act, slope, unit, final, own_up, across_up, small_full, inverse1, inverse2 = forward(
+        x,
+        [query_weight, key_weight, value_weight, output_weight],
+        expand_weight,
+        down_weight,
+        small,
+        pick,
+        slot_activation_gradient,
+        nz,
+        nx,
+        token_count,
     )
     sums, small_sums, input_full, table = backward(
-        x, own_up, across_up, final, unit, inverse1, inverse2, small_full, act, slope, saved, g, nz, nx, token_count
-    )
-    slot_acts = pick_rows(slot_row, table.reshape(-1, token_count, width))
-    live_rows = lax.broadcasted_iota(jnp.int32, (row_count,), 0) < live_count[0]
-    input_grad = jnp.where(live_rows[:, None, None], input_full.reshape(rows_in.shape), 0.0)
-    me = lax.axis_index(("dp", "fsdp"))
-    mine = lax.dynamic_slice(small_sums, (jnp.int32(0), me * shard), (small_sums.shape[0], shard))
-    blocks = (sums.shape[0] - 4) // 2
-    down_sum = sums[:blocks].reshape(-1, width)
-    ups = sums[blocks : 2 * blocks].reshape(blocks, shard, -1, shard)
-    up_sum = ups.transpose(1, 2, 0, 3).reshape(shard, -1)
-    output_sum, value_sum, query_sum, key_sum = (sums[2 * blocks + i] for i in range(4))
+        x,
+        own_up,
+        across_up,
+        final,
+        unit,
+        inverse1,
+        inverse2,
+        small_full,
+        act,
+        slope,
+        saved,
+        g,
+        probs,
+        nz,
+        nx,
+        token_count,
+    )
+    slot_acts, input_grad, query, keys, values, output, up, contract, *small_grads = finish(
+        slot_row,
+        live_count,
+        table.reshape(-1, token_count, width),
+        input_full.reshape(rows_in.shape),
+        sums,
+        small_sums,
+    )
     return (
         slot_acts,
         input_grad,
-        query_sum,
-        key_sum,
-        value_sum,
-        output_sum,
-        mine[0],
-        mine[1],
-        mine[2],
-        mine[3],
-        mine[4],
-        up_sum,
-        mine[8 : 8 + blocks].reshape(-1),
-        down_sum,
-        mine[5],
-        mine[6],
-        mine[7],
+        query,
+        keys,
+        values,
+        output,
+        *small_grads[:5],
+        up,
+        small_grads[8],
+        contract,
+        *small_grads[5:8],
     )
 
 

time: 366 us -> 337 us (0.921)
  local copies, waits for them, and re-layouts: 23.9 us -> 1.56 us
  other arithmetic: 5.56 us -> 1.86 us
    reshape x5 -> x1, local copies, waits for them, and re-layouts: 8.16 us -> 0.74 us  [prepare(): rows = [v.reshape(-1, shard) for v in (*small_parameters, up_bias)]]
    select_n x1 -> x0, other arithmetic: 4.86 us -> none  [on_device_kernels(): jnp.where(live_rows[:, None, None], input_full.reshape(rows_in.shape), 0.0)]
where the time goes in v5:
time: 337 us; the launch traced here: 336 us
  Pallas kernels  331 us (98%)
    pallas_call x1, Pallas kernels, backward(): pl.pallas_call(partial(backward_kernel, nz, nx, parts, tokens, 2 * width...  168 us
    pallas_call x1, Pallas kernels, forward(): pl.pallas_call(partial(forward_kernel, nz, nx, [column_parts(width, s) fo...  153 us
    pallas_call x1, Pallas kernels, finish(): pl.pallas_call(finish_kernel, out_shape=[out((slots, tokens, width), tabl...  10.1 us

profile of v5, /device:TPU:0, one launch (start us, length us, event | category | flops | bytes accessed | tf_op | source)
XLA Modules:
  0.0 335.8 jit_solution(17320854681435945905)
XLA Ops:
  0.7 0.7 reshape.84
  1.4 0.8 concatenate.3
  2.2 0.6 pad_convert_fusion.small
  2.8 1.3 fusion.pick
  4.1 152.8 %shard_map.314 = (bf16[12,2,2,4,2,32,1024]{6,5,4,3,2,1,0:T(8,128)(2,1)}, bf16[24,2,320,320]{3,2,1,0:T(8,128)(2,1)}, bf16[5,960,1024]{2,1,0:T(8,128)(2,1)}, bf16[...) custom-call(bf16[960,1024]{1,0:T(8,128)(2,1)} %bitcast.13, ...), custom_call_target="tpu_custom_call" | custom-call | tf_op jit(solution)/shard_map/pallas_call | solution.py:663
  156.9 168.0 %shard_map.315 = (f32[12,32,1024]{2,1,0:T(8,128)}, f32[16,1024]{1,0:T(8,128)}, f32[960,1024]{1,0:T(8,128)}, bf16[2,2,960,1024]{3,2,1,0:T(8,128)(2,1)}) custom-call(bf16[960,1024]{1,0:T(8,128)(2,1)} %bitcast.14, bf16[960,1024]{1,0:T(8,128)(2,1)} %get-tuple-element.50.own_up, bf16[960,1024]{1,0:T(8,128)(2,1)} %get-tuple-element.51.across_up, ...), custom_call_target="tpu_custom_call" | custom-call | tf_op jit(solution)/shard_map/pallas_call | solution.py:996
  325.6 10.1 %shard_map.316 = (bf16[6,320,1024]{2,1,0:T(8,128)(2,1)}, f32[3,320,1024]{2,1,0:T(8,128)}, f32[32,1024]{1,0:T(8,128)}, f32[32,1024]{1,0:T(8,128)}, f32[32,1024]{1...) custom-call(s32[6]{0:T(128)} %slot_row.1, ...), custom_call_target="tpu_custom_call" | custom-call | tf_op jit(solution)/shard_map/pallas_call | solution.py:1077
